TPU v7x, 1024 devices: a whole 4x8x16 slice. The times are simulated.
1024 devices in a mesh: ctx: 16 (over z), head: 64 (over x, y, core).
Axes of the slice: x: 4, y: 8, z: 16, core: 2. Of those that a mesh axis runs over, the one named last changes fastest.
Arguments:
- queries: bfloat16 [32768, 64, 128], P('ctx', 'head'), may hold values from -54 to 54
- keys: bfloat16 [32768, 8, 128], P(('ctx', 'head')), may hold values from -12 to 12
- values: bfloat16 [32768, 8, 128], P(('ctx', 'head')), may hold values from -6 to 6
- key_blocks: int32 [256, 4], replicated, may hold values from 0 to 255, as said below
- span_order: int32 [32], replicated, may hold values from 0 to 31, as said below
Outputs:
- attended: bfloat16 [32768, 64, 128], P('ctx', 'head')
Inputs may be any that keep to these rules, and one draw needn't show every extreme that they name: `key_blocks`: row b names block b in slot 0; each used slot j (1 <= j <= b) names a block below b, and a block may stand in two slots of a row; unused slots hold 0. The query blocks of one ctx index list at most 2 distinct blocks held by any one other ctx index. `span_order`: each number once.
All inputs are finite; a program needn't handle non-finite values.
Results may differ from a plain program's by a relative error of at most 0.0045.
Values may be sent and summed in bfloat16 or wider, within the bound.
No kernel may reach another device: no remote copies, remote signals or barrier semaphores. Data moves between devices by JAX's collectives and lax.ppermute only.
A program may use at most 32 MiB of HBM per device.

v0:
```python
import jax
import jax.numpy as jnp
from jax import lax
from jax.sharding import PartitionSpec as P

BLK = 128
CAP = 2


def from_behind(shard, axis, by):
    size = lax.axis_size(axis)
    return lax.ppermute(shard, axis, [(i, (i + by) % size) for i in range(size)])


def positions_of(device_ids, span_order, per_span, block_count):
    local_ids = jnp.arange(block_count, dtype=jnp.int32)
    storage_span = 2 * device_ids + local_ids // per_span
    return jnp.take(span_order, storage_span) * per_span + local_ids % per_span


def pick_slots(wanted):
    block_count = wanted.shape[1]
    slot_rank = jnp.cumsum(wanted.astype(jnp.int32), axis=1) - 1
    matches = wanted[:, :, None] & (
        slot_rank[:, :, None] == jnp.arange(CAP, dtype=jnp.int32)[None, None, :]
    )
    chosen = jnp.sum(
        jnp.where(matches, jnp.arange(block_count, dtype=jnp.int32)[None, :, None], 0), axis=1
    )
    return (slot_rank, chosen)


def body(queries, keys, values, key_blocks, span_order):
    cycle_size = lax.axis_size("ctx")
    head_count = lax.axis_size("head")
    rows_device = queries.shape[0]
    heads_here = queries.shape[1]
    width = queries.shape[2]
    slot_count = key_blocks.shape[1]
    block_count = rows_device // BLK
    per_span = block_count // 2
    group_devices = head_count // keys.shape[1]
    spread = jnp.arange(head_count, dtype=jnp.int32) // group_devices
    key_wide = jnp.take(keys, spread, axis=1)
    value_wide = jnp.take(values, spread, axis=1)
    key_local, value_local = (
        lax.all_to_all(key_wide, "head", split_axis=1, concat_axis=0, tiled=True),
        lax.all_to_all(value_wide, "head", split_axis=1, concat_axis=0, tiled=True),
    )
    key_local = key_local.reshape(rows_device, width)
    value_local = value_local.reshape(rows_device, width)
    key_tiles = key_local.reshape(block_count, BLK, width)
    value_tiles = value_local.reshape(block_count, BLK, width)
    cycle_index = lax.axis_index("ctx")
    device_ids = jnp.arange(cycle_size, dtype=jnp.int32)
    held = positions_of(device_ids[:, None], span_order, per_span, block_count)
    query_pos = positions_of(cycle_index, span_order, per_span, block_count)
    listed = jnp.take(key_blocks, query_pos, axis=0)
    slot_ids = jnp.arange(slot_count, dtype=jnp.int32)
    in_use = slot_ids[None, :] <= query_pos[:, None]
    span_ids = jnp.arange(span_order.shape[0], dtype=jnp.int32)
    inverse = jnp.sum(
        jnp.where(span_order[None, :] == span_ids[:, None], span_ids[None, :], 0), axis=1
    )
    key_span = jnp.take(inverse, listed // per_span)
    key_owner = key_span // 2
    key_block = key_span % 2 * per_span + listed % per_span
    others = device_ids != cycle_index
    wanted = (
        jnp.any(
            (listed[None, None, :, :] == held[:, :, None, None]) & in_use[None, None, :, :],
            axis=(2, 3),
        )
        & others[:, None]
    )
    slot_rank, chosen_blocks = pick_slots(wanted)
    holding = jnp.zeros((cycle_size, CAP, BLK, width), jnp.bfloat16)

    def collect(buffers, key_rows, value_rows, owner_index):
        chosen = jnp.take(chosen_blocks, owner_index, axis=0)
        key_part = jnp.take(key_rows.reshape(block_count, BLK, width), chosen, axis=0)
        value_part = jnp.take(value_rows.reshape(block_count, BLK, width), chosen, axis=0)
        return (
            lax.dynamic_update_slice_in_dim(buffers[0], key_part[None], owner_index, 0),
            lax.dynamic_update_slice_in_dim(buffers[1], value_part[None], owner_index, 0),
        )

    def carry_keys(turn_index, carry):
        key_now, value_now, key_store, value_store = carry
        key_now, value_now = from_behind((key_now, value_now), "ctx", 1)
        owner_index = (cycle_index - turn_index) % cycle_size
        key_store, value_store = collect((key_store, value_store), key_now, value_now, owner_index)
        return (key_now, value_now, key_store, value_store)

    final_carry = lax.fori_loop(
        1, cycle_size, carry_keys, (key_local, value_local, holding, holding)
    )
    buffers = (final_carry[2], final_carry[3])
    key_table = jnp.concatenate(
        [key_tiles, buffers[0].reshape(cycle_size * CAP, BLK, width)], axis=0
    )
    value_table = jnp.concatenate(
        [value_tiles, buffers[1].reshape(cycle_size * CAP, BLK, width)], axis=0
    )
    flat_rank = jnp.take(slot_rank.reshape(-1), key_owner * block_count + key_block)
    source_index = jnp.where(
        key_owner == cycle_index, key_block, block_count + key_owner * CAP + flat_rank
    )
    source_index = jnp.clip(source_index, 0, key_table.shape[0] - 1).reshape(-1)
    pair_keys = jnp.take(key_table, source_index, axis=0).reshape(
        block_count, slot_count, BLK, width
    )
    pair_values = jnp.take(value_table, source_index, axis=0).reshape(
        block_count, slot_count, BLK, width
    )
    query_tiles = queries.reshape(block_count, BLK, heads_here, width)
    score_scale = width ** (-0.5)
    scores = (
        jnp.einsum("bqhd,bjkd->bhqjk", query_tiles, pair_keys, preferred_element_type=jnp.float32)
        * score_scale
    )
    causal = jnp.arange(BLK)[None, :] <= jnp.arange(BLK)[:, None]
    on_diagonal = listed == query_pos[:, None]
    allowed = in_use[:, None, None, :, None] & (
        jnp.logical_not(on_diagonal)[:, None, None, :, None] | causal[None, None, :, None, :]
    )
    scores = jnp.where(allowed, scores, jnp.float32(-1e30))
    row_peak = jnp.max(scores, axis=(3, 4), keepdims=True)
    raised = jnp.exp(scores - row_peak)
    row_total = jnp.sum(raised, axis=(3, 4))
    weights = raised.astype(jnp.bfloat16)
    combined = jnp.einsum(
        "bhqjk,bjkd->bqhd", weights, pair_values, preferred_element_type=jnp.float32
    )
    result = combined / jnp.transpose(row_total, (0, 2, 1))[..., None]
    return result.reshape(rows_device, heads_here, width).astype(jnp.bfloat16)


def solution(mesh):
    in_specs = (
        P("ctx", "head", None),
        P(("ctx", "head"), None, None),
        P(("ctx", "head"), None, None),
        P(),
        P(),
    )
    out_specs = P("ctx", "head", None)
    return jax.shard_map(body, mesh=mesh, in_specs=in_specs, out_specs=out_specs, check_vma=False)
```

profile of v0, /device:TPU:6, one launch (start us, length us, event | category | flops | bytes accessed | tf_op | source)
XLA Modules:
  0.0 477.3 jit_solution(7322881473498925630)
XLA Ops:
  7.5 17.5 %all-to-all-start = ((bf16[32,64,128]{2,0,1:T(8,128)(2,1)}), bf16[32,64,128]{2,0,1:T(8,128)(2,1)S(1)}, u32[]{:S(2)}, u32[]{:S(2)}) async-start(bf16[32,64,128]{2,0,1:T(8,128)(2,1)} %copy.47), calls=%async_computation | async-start | bytes 1048576 | tf_op jit(solution)/shard_map/all_to_all | solution.py:48
  30.9 10.8 %all-to-all-done = bf16[32,64,128]{2,0,1:T(8,128)(2,1)S(1)} async-done(((bf16[32,64,128]{2,0,1:T(8,128)(2,1)}), bf16[32,64,128]{2,0,1:T(8,128)(2,1)S(1)}, u32[]{:S(2)}, u32[]{:S(2)}) %all-to-all-start) | async-done | bytes 524320 | tf_op jit(solution)/shard_map/all_to_all | solution.py:48
  41.7 6.9 %all-to-all-start.1 = ((bf16[32,64,128]{2,0,1:T(8,128)(2,1)}), bf16[32,64,128]{2,0,1:T(8,128)(2,1)S(1)}, u32[]{:S(2)}, u32[]{:S(2)}) async-start(bf16[32,64,128]{2,0,1:T(8,128)(2,1)} %copy.48), calls=%async_computation.1 | async-start | bytes 1048576 | tf_op jit(solution)/shard_map/all_to_all | solution.py:47
  51.7 13.6 %all-to-all-done.1 = bf16[32,64,128]{2,0,1:T(8,128)(2,1)S(1)} async-done(((bf16[32,64,128]{2,0,1:T(8,128)(2,1)}), bf16[32,64,128]{2,0,1:T(8,128)(2,1)S(1)}, u32[]{:S(2)}, u32[]{:S(2)}) %all-to-all-start.1) | async-done | bytes 524320 | tf_op jit(solution)/shard_map/all_to_all | solution.py:47
  68.5 392.5 %while.22 = (s32[]{:T(128)}, bf16[2048,128]{1,0:T(8,128)(2,1)}, bf16[2048,128]{1,0:T(8,128)(2,1)S(1)}, bf16[16,2,128,128]{3,2,1,0:T(8,128)(2,1)}, bf16[16,2,128,...) while((s32[]{:T(128)}, bf16[2048,128]{1,0:T(8,128)(2,1)}, ...), condition=%wide.region_4.7_spmd, body=%wide.region_3.6_spmd.sunk | while | flops 66594 | bytes 6820258 | solution.py:95
  72.5 20.4 %collective-permute-done.1 = bf16[2048,128]{1,0:T(8,128)(2,1)S(1)} collective-permute-done((bf16[2048,128]{1,0:T(8,128)(2,1)S(1)}, bf16[2048,128]{1,0:T(8,128)(2,1)S(1)}, u32[]{:S(2)}, u32[]{:S(2)}) %collective-permute-start.1) | collective-permute-done | bytes 524320 | tf_op jit(solution)/shard_map/while/body/eval_jaxpr/ppermute | solution.py:12
  93.4 10.6 %collective-permute-done = bf16[2048,128]{1,0:T(8,128)(2,1)S(1)} collective-permute-done((bf16[2048,128]{1,0:T(8,128)(2,1)}, bf16[2048,128]{1,0:T(8,128)(2,1)S(1)}, u32[]{:S(2)}, u32[]{:S(2)}) %collective-permute-start) | collective-permute-done | bytes 524320 | tf_op jit(solution)/shard_map/while/body/eval_jaxpr/ppermute | solution.py:12
  110.0 14.0 %collective-permute-done.1 = bf16[2048,128]{1,0:T(8,128)(2,1)S(1)} collective-permute-done((bf16[2048,128]{1,0:T(8,128)(2,1)S(1)}, bf16[2048,128]{1,0:T(8,128)(2,1)S(1)}, u32[]{:S(2)}, u32[]{:S(2)}) %collective-permute-start.1) | collective-permute-done | bytes 524320 | tf_op jit(solution)/shard_map/while/body/eval_jaxpr/ppermute | solution.py:12
  124.6 9.7 %collective-permute-done = bf16[2048,128]{1,0:T(8,128)(2,1)S(1)} collective-permute-done((bf16[2048,128]{1,0:T(8,128)(2,1)}, bf16[2048,128]{1,0:T(8,128)(2,1)S(1)}, u32[]{:S(2)}, u32[]{:S(2)}) %collective-permute-start) | collective-permute-done | bytes 524320 | tf_op jit(solution)/shard_map/while/body/eval_jaxpr/ppermute | solution.py:12
  140.4 14.0 %collective-permute-done.1 = bf16[2048,128]{1,0:T(8,128)(2,1)S(1)} collective-permute-done((bf16[2048,128]{1,0:T(8,128)(2,1)S(1)}, bf16[2048,128]{1,0:T(8,128)(2,1)S(1)}, u32[]{:S(2)}, u32[]{:S(2)}) %collective-permute-start.1) | collective-permute-done | bytes 524320 | tf_op jit(solution)/shard_map/while/body/eval_jaxpr/ppermute | solution.py:12
  155.0 8.8 %collective-permute-done = bf16[2048,128]{1,0:T(8,128)(2,1)S(1)} collective-permute-done((bf16[2048,128]{1,0:T(8,128)(2,1)}, bf16[2048,128]{1,0:T(8,128)(2,1)S(1)}, u32[]{:S(2)}, u32[]{:S(2)}) %collective-permute-start) | collective-permute-done | bytes 524320 | tf_op jit(solution)/shard_map/while/body/eval_jaxpr/ppermute | solution.py:12
  169.9 14.0 %collective-permute-done.1 = bf16[2048,128]{1,0:T(8,128)(2,1)S(1)} collective-permute-done((bf16[2048,128]{1,0:T(8,128)(2,1)S(1)}, bf16[2048,128]{1,0:T(8,128)(2,1)S(1)}, u32[]{:S(2)}, u32[]{:S(2)}) %collective-permute-start.1) | collective-permute-done | bytes 524320 | tf_op jit(solution)/shard_map/while/body/eval_jaxpr/ppermute | solution.py:12
  184.5 7.9 %collective-permute-done = bf16[2048,128]{1,0:T(8,128)(2,1)S(1)} collective-permute-done((bf16[2048,128]{1,0:T(8,128)(2,1)}, bf16[2048,128]{1,0:T(8,128)(2,1)S(1)}, u32[]{:S(2)}, u32[]{:S(2)}) %collective-permute-start) | collective-permute-done | bytes 524320 | tf_op jit(solution)/shard_map/while/body/eval_jaxpr/ppermute | solution.py:12
  198.5 14.0 %collective-permute-done.1 = bf16[2048,128]{1,0:T(8,128)(2,1)S(1)} collective-permute-done((bf16[2048,128]{1,0:T(8,128)(2,1)S(1)}, bf16[2048,128]{1,0:T(8,128)(2,1)S(1)}, u32[]{:S(2)}, u32[]{:S(2)}) %collective-permute-start.1) | collective-permute-done | bytes 524320 | tf_op jit(solution)/shard_map/while/body/eval_jaxpr/ppermute | solution.py:12
  213.1 7.0 %collective-permute-done = bf16[2048,128]{1,0:T(8,128)(2,1)S(1)} collective-permute-done((bf16[2048,128]{1,0:T(8,128)(2,1)}, bf16[2048,128]{1,0:T(8,128)(2,1)S(1)}, u32[]{:S(2)}, u32[]{:S(2)}) %collective-permute-start) | collective-permute-done | bytes 524320 | tf_op jit(solution)/shard_map/while/body/eval_jaxpr/ppermute | solution.py:12
  226.2 14.0 %collective-permute-done.1 = bf16[2048,128]{1,0:T(8,128)(2,1)S(1)} collective-permute-done((bf16[2048,128]{1,0:T(8,128)(2,1)S(1)}, bf16[2048,128]{1,0:T(8,128)(2,1)S(1)}, u32[]{:S(2)}, u32[]{:S(2)}) %collective-permute-start.1) | collective-permute-done | bytes 524320 | tf_op jit(solution)/shard_map/while/body/eval_jaxpr/ppermute | solution.py:12
  240.8 6.1 %collective-permute-done = bf16[2048,128]{1,0:T(8,128)(2,1)S(1)} collective-permute-done((bf16[2048,128]{1,0:T(8,128)(2,1)}, bf16[2048,128]{1,0:T(8,128)(2,1)S(1)}, u32[]{:S(2)}, u32[]{:S(2)}) %collective-permute-start) | collective-permute-done | bytes 524320 | tf_op jit(solution)/shard_map/while/body/eval_jaxpr/ppermute | solution.py:12
  252.9 14.0 %collective-permute-done.1 = bf16[2048,128]{1,0:T(8,128)(2,1)S(1)} collective-permute-done((bf16[2048,128]{1,0:T(8,128)(2,1)S(1)}, bf16[2048,128]{1,0:T(8,128)(2,1)S(1)}, u32[]{:S(2)}, u32[]{:S(2)}) %collective-permute-start.1) | collective-permute-done | bytes 524320 | tf_op jit(solution)/shard_map/while/body/eval_jaxpr/ppermute | solution.py:12
  267.5 5.1 %collective-permute-done = bf16[2048,128]{1,0:T(8,128)(2,1)S(1)} collective-permute-done((bf16[2048,128]{1,0:T(8,128)(2,1)}, bf16[2048,128]{1,0:T(8,128)(2,1)S(1)}, u32[]{:S(2)}, u32[]{:S(2)}) %collective-permute-start) | collective-permute-done | bytes 524320 | tf_op jit(solution)/shard_map/while/body/eval_jaxpr/ppermute | solution.py:12
  278.7 13.2 %collective-permute-done.1 = bf16[2048,128]{1,0:T(8,128)(2,1)S(1)} collective-permute-done((bf16[2048,128]{1,0:T(8,128)(2,1)S(1)}, bf16[2048,128]{1,0:T(8,128)(2,1)S(1)}, u32[]{:S(2)}, u32[]{:S(2)}) %collective-permute-start.1) | collective-permute-done | bytes 524320 | tf_op jit(solution)/shard_map/while/body/eval_jaxpr/ppermute | solution.py:12
  303.6 12.3 %collective-permute-done.1 = bf16[2048,128]{1,0:T(8,128)(2,1)S(1)} collective-permute-done((bf16[2048,128]{1,0:T(8,128)(2,1)S(1)}, bf16[2048,128]{1,0:T(8,128)(2,1)S(1)}, u32[]{:S(2)}, u32[]{:S(2)}) %collective-permute-start.1) | collective-permute-done | bytes 524320 | tf_op jit(solution)/shard_map/while/body/eval_jaxpr/ppermute | solution.py:12
  327.6 11.4 %collective-permute-done.1 = bf16[2048,128]{1,0:T(8,128)(2,1)S(1)} collective-permute-done((bf16[2048,128]{1,0:T(8,128)(2,1)S(1)}, bf16[2048,128]{1,0:T(8,128)(2,1)S(1)}, u32[]{:S(2)}, u32[]{:S(2)}) %collective-permute-start.1) | collective-permute-done | bytes 524320 | tf_op jit(solution)/shard_map/while/body/eval_jaxpr/ppermute | solution.py:12
  339.5 5.3 %collective-permute-done = bf16[2048,128]{1,0:T(8,128)(2,1)S(1)} collective-permute-done((bf16[2048,128]{1,0:T(8,128)(2,1)}, bf16[2048,128]{1,0:T(8,128)(2,1)S(1)}, u32[]{:S(2)}, u32[]{:S(2)}) %collective-permute-start) | collective-permute-done | bytes 524320 | tf_op jit(solution)/shard_map/while/body/eval_jaxpr/ppermute | solution.py:12
  350.9 10.5 %collective-permute-done.1 = bf16[2048,128]{1,0:T(8,128)(2,1)S(1)} collective-permute-done((bf16[2048,128]{1,0:T(8,128)(2,1)S(1)}, bf16[2048,128]{1,0:T(8,128)(2,1)S(1)}, u32[]{:S(2)}, u32[]{:S(2)}) %collective-permute-start.1) | collective-permute-done | bytes 524320 | tf_op jit(solution)/shard_map/while/body/eval_jaxpr/ppermute | solution.py:12
  362.0 6.2 %collective-permute-done = bf16[2048,128]{1,0:T(8,128)(2,1)S(1)} collective-permute-done((bf16[2048,128]{1,0:T(8,128)(2,1)}, bf16[2048,128]{1,0:T(8,128)(2,1)S(1)}, u32[]{:S(2)}, u32[]{:S(2)}) %collective-permute-start) | collective-permute-done | bytes 524320 | tf_op jit(solution)/shard_map/while/body/eval_jaxpr/ppermute | solution.py:12
  374.2 9.7 %collective-permute-done.1 = bf16[2048,128]{1,0:T(8,128)(2,1)S(1)} collective-permute-done((bf16[2048,128]{1,0:T(8,128)(2,1)S(1)}, bf16[2048,128]{1,0:T(8,128)(2,1)S(1)}, u32[]{:S(2)}, u32[]{:S(2)}) %collective-permute-start.1) | collective-permute-done | bytes 524320 | tf_op jit(solution)/shard_map/while/body/eval_jaxpr/ppermute | solution.py:12
  384.5 7.1 %collective-permute-done = bf16[2048,128]{1,0:T(8,128)(2,1)S(1)} collective-permute-done((bf16[2048,128]{1,0:T(8,128)(2,1)}, bf16[2048,128]{1,0:T(8,128)(2,1)S(1)}, u32[]{:S(2)}, u32[]{:S(2)}) %collective-permute-start) | collective-permute-done | bytes 524320 | tf_op jit(solution)/shard_map/while/body/eval_jaxpr/ppermute | solution.py:12
  397.6 8.8 %collective-permute-done.1 = bf16[2048,128]{1,0:T(8,128)(2,1)S(1)} collective-permute-done((bf16[2048,128]{1,0:T(8,128)(2,1)S(1)}, bf16[2048,128]{1,0:T(8,128)(2,1)S(1)}, u32[]{:S(2)}, u32[]{:S(2)}) %collective-permute-start.1) | collective-permute-done | bytes 524320 | tf_op jit(solution)/shard_map/while/body/eval_jaxpr/ppermute | solution.py:12
  406.9 7.9 %collective-permute-done = bf16[2048,128]{1,0:T(8,128)(2,1)S(1)} collective-permute-done((bf16[2048,128]{1,0:T(8,128)(2,1)}, bf16[2048,128]{1,0:T(8,128)(2,1)S(1)}, u32[]{:S(2)}, u32[]{:S(2)}) %collective-permute-start) | collective-permute-done | bytes 524320 | tf_op jit(solution)/shard_map/while/body/eval_jaxpr/ppermute | solution.py:12
  420.9 8.4 %collective-permute-done.1 = bf16[2048,128]{1,0:T(8,128)(2,1)S(1)} collective-permute-done((bf16[2048,128]{1,0:T(8,128)(2,1)S(1)}, bf16[2048,128]{1,0:T(8,128)(2,1)S(1)}, u32[]{:S(2)}, u32[]{:S(2)}) %collective-permute-start.1) | collective-permute-done | bytes 524320 | tf_op jit(solution)/shard_map/while/body/eval_jaxpr/ppermute | solution.py:12
  429.8 9.0 %collective-permute-done = bf16[2048,128]{1,0:T(8,128)(2,1)S(1)} collective-permute-done((bf16[2048,128]{1,0:T(8,128)(2,1)}, bf16[2048,128]{1,0:T(8,128)(2,1)S(1)}, u32[]{:S(2)}, u32[]{:S(2)}) %collective-permute-start) | collective-permute-done | bytes 524320 | tf_op jit(solution)/shard_map/while/body/eval_jaxpr/ppermute | solution.py:12
  444.9 8.4 %collective-permute-done.1 = bf16[2048,128]{1,0:T(8,128)(2,1)S(1)} collective-permute-done((bf16[2048,128]{1,0:T(8,128)(2,1)S(1)}, bf16[2048,128]{1,0:T(8,128)(2,1)S(1)}, u32[]{:S(2)}, u32[]{:S(2)}) %collective-permute-start.1) | collective-permute-done | bytes 524320 | tf_op jit(solution)/shard_map/while/body/eval_jaxpr/ppermute | solution.py:12
  (217 shorter events, 149.4 us)
Async XLA Ops:
  7.5 34.2 %all-to-all-start = ((bf16[32,64,128]{2,0,1:T(8,128)(2,1)}), bf16[32,64,128]{2,0,1:T(8,128)(2,1)S(1)}, u32[]{:S(2)}, u32[]{:S(2)}) async-start(bf16[32,64,128]{2,0,1:T(8,128)(2,1)} %copy.47), calls=%async_computation | async-start | bytes 1048576 | tf_op jit(solution)/shard_map/all_to_all | solution.py:48
  41.7 23.6 %all-to-all-start.1 = ((bf16[32,64,128]{2,0,1:T(8,128)(2,1)}), bf16[32,64,128]{2,0,1:T(8,128)(2,1)S(1)}, u32[]{:S(2)}, u32[]{:S(2)}) async-start(bf16[32,64,128]{2,0,1:T(8,128)(2,1)} %copy.48), calls=%async_computation.1 | async-start | bytes 1048576 | tf_op jit(solution)/shard_map/all_to_all | solution.py:47
  68.5 24.3 %collective-permute-start.1 = (bf16[2048,128]{1,0:T(8,128)(2,1)S(1)}, bf16[2048,128]{1,0:T(8,128)(2,1)S(1)}, u32[]{:S(2)}, u32[]{:S(2)}) collective-permute-start(bf16[2048,128]{1,0:T(8,128)(2,1)S(1)} %get-tuple-element.305), channel_id=1, source_target_pairs={{0,64},{64,128},{128,192},{192,256},{256,320},{320,384},{384,448},... | collective-permute-start | bytes 1572872 | tf_op jit(solution)/shard_map/while/body/eval_jaxpr/ppermute | solution.py:12
  70.5 33.5 %collective-permute-start = (bf16[2048,128]{1,0:T(8,128)(2,1)}, bf16[2048,128]{1,0:T(8,128)(2,1)S(1)}, u32[]{:S(2)}, u32[]{:S(2)}) collective-permute-start(bf16[2048,128]{1,0:T(8,128)(2,1)} %get-tuple-element.304), channel_id=1, source_target_pairs={{0,64},{64,128},{128,192},{192,256},{256,320},{320,384},{384,448},... | collective-permute-start | bytes 1572872 | tf_op jit(solution)/shard_map/while/body/eval_jaxpr/ppermute | solution.py:12
  106.1 17.9 %collective-permute-start.1 = (bf16[2048,128]{1,0:T(8,128)(2,1)S(1)}, bf16[2048,128]{1,0:T(8,128)(2,1)S(1)}, u32[]{:S(2)}, u32[]{:S(2)}) collective-permute-start(bf16[2048,128]{1,0:T(8,128)(2,1)S(1)} %get-tuple-element.305), channel_id=1, source_target_pairs={{0,64},{64,128},{128,192},{192,256},{256,320},{320,384},{384,448},... | collective-permute-start | bytes 1572872 | tf_op jit(solution)/shard_map/while/body/eval_jaxpr/ppermute | solution.py:12
  108.1 26.3 %collective-permute-start = (bf16[2048,128]{1,0:T(8,128)(2,1)}, bf16[2048,128]{1,0:T(8,128)(2,1)S(1)}, u32[]{:S(2)}, u32[]{:S(2)}) collective-permute-start(bf16[2048,128]{1,0:T(8,128)(2,1)} %get-tuple-element.304), channel_id=1, source_target_pairs={{0,64},{64,128},{128,192},{192,256},{256,320},{320,384},{384,448},... | collective-permute-start | bytes 1572872 | tf_op jit(solution)/shard_map/while/body/eval_jaxpr/ppermute | solution.py:12
  136.5 18.0 %collective-permute-start.1 = (bf16[2048,128]{1,0:T(8,128)(2,1)S(1)}, bf16[2048,128]{1,0:T(8,128)(2,1)S(1)}, u32[]{:S(2)}, u32[]{:S(2)}) collective-permute-start(bf16[2048,128]{1,0:T(8,128)(2,1)S(1)} %get-tuple-element.305), channel_id=1, source_target_pairs={{0,64},{64,128},{128,192},{192,256},{256,320},{320,384},{384,448},... | collective-permute-start | bytes 1572872 | tf_op jit(solution)/shard_map/while/body/eval_jaxpr/ppermute | solution.py:12
  138.4 25.4 %collective-permute-start = (bf16[2048,128]{1,0:T(8,128)(2,1)}, bf16[2048,128]{1,0:T(8,128)(2,1)S(1)}, u32[]{:S(2)}, u32[]{:S(2)}) collective-permute-start(bf16[2048,128]{1,0:T(8,128)(2,1)} %get-tuple-element.304), channel_id=1, source_target_pairs={{0,64},{64,128},{128,192},{192,256},{256,320},{320,384},{384,448},... | collective-permute-start | bytes 1572872 | tf_op jit(solution)/shard_map/while/body/eval_jaxpr/ppermute | solution.py:12
  166.0 18.0 %collective-permute-start.1 = (bf16[2048,128]{1,0:T(8,128)(2,1)S(1)}, bf16[2048,128]{1,0:T(8,128)(2,1)S(1)}, u32[]{:S(2)}, u32[]{:S(2)}) collective-permute-start(bf16[2048,128]{1,0:T(8,128)(2,1)S(1)} %get-tuple-element.305), channel_id=1, source_target_pairs={{0,64},{64,128},{128,192},{192,256},{256,320},{320,384},{384,448},... | collective-permute-start | bytes 1572872 | tf_op jit(solution)/shard_map/while/body/eval_jaxpr/ppermute | solution.py:12
  167.9 24.5 %collective-permute-start = (bf16[2048,128]{1,0:T(8,128)(2,1)}, bf16[2048,128]{1,0:T(8,128)(2,1)S(1)}, u32[]{:S(2)}, u32[]{:S(2)}) collective-permute-start(bf16[2048,128]{1,0:T(8,128)(2,1)} %get-tuple-element.304), channel_id=1, source_target_pairs={{0,64},{64,128},{128,192},{192,256},{256,320},{320,384},{384,448},... | collective-permute-start | bytes 1572872 | tf_op jit(solution)/shard_map/while/body/eval_jaxpr/ppermute | solution.py:12
  194.6 18.0 %collective-permute-start.1 = (bf16[2048,128]{1,0:T(8,128)(2,1)S(1)}, bf16[2048,128]{1,0:T(8,128)(2,1)S(1)}, u32[]{:S(2)}, u32[]{:S(2)}) collective-permute-start(bf16[2048,128]{1,0:T(8,128)(2,1)S(1)} %get-tuple-element.305), channel_id=1, source_target_pairs={{0,64},{64,128},{128,192},{192,256},{256,320},{320,384},{384,448},... | collective-permute-start | bytes 1572872 | tf_op jit(solution)/shard_map/while/body/eval_jaxpr/ppermute | solution.py:12
  196.5 23.6 %collective-permute-start = (bf16[2048,128]{1,0:T(8,128)(2,1)}, bf16[2048,128]{1,0:T(8,128)(2,1)S(1)}, u32[]{:S(2)}, u32[]{:S(2)}) collective-permute-start(bf16[2048,128]{1,0:T(8,128)(2,1)} %get-tuple-element.304), channel_id=1, source_target_pairs={{0,64},{64,128},{128,192},{192,256},{256,320},{320,384},{384,448},... | collective-permute-start | bytes 1572872 | tf_op jit(solution)/shard_map/while/body/eval_jaxpr/ppermute | solution.py:12
  222.3 18.0 %collective-permute-start.1 = (bf16[2048,128]{1,0:T(8,128)(2,1)S(1)}, bf16[2048,128]{1,0:T(8,128)(2,1)S(1)}, u32[]{:S(2)}, u32[]{:S(2)}) collective-permute-start(bf16[2048,128]{1,0:T(8,128)(2,1)S(1)} %get-tuple-element.305), channel_id=1, source_target_pairs={{0,64},{64,128},{128,192},{192,256},{256,320},{320,384},{384,448},... | collective-permute-start | bytes 1572872 | tf_op jit(solution)/shard_map/while/body/eval_jaxpr/ppermute | solution.py:12
  224.2 22.7 %collective-permute-start = (bf16[2048,128]{1,0:T(8,128)(2,1)}, bf16[2048,128]{1,0:T(8,128)(2,1)S(1)}, u32[]{:S(2)}, u32[]{:S(2)}) collective-permute-start(bf16[2048,128]{1,0:T(8,128)(2,1)} %get-tuple-element.304), channel_id=1, source_target_pairs={{0,64},{64,128},{128,192},{192,256},{256,320},{320,384},{384,448},... | collective-permute-start | bytes 1572872 | tf_op jit(solution)/shard_map/while/body/eval_jaxpr/ppermute | solution.py:12
  249.0 18.0 %collective-permute-start.1 = (bf16[2048,128]{1,0:T(8,128)(2,1)S(1)}, bf16[2048,128]{1,0:T(8,128)(2,1)S(1)}, u32[]{:S(2)}, u32[]{:S(2)}) collective-permute-start(bf16[2048,128]{1,0:T(8,128)(2,1)S(1)} %get-tuple-element.305), channel_id=1, source_target_pairs={{0,64},{64,128},{128,192},{192,256},{256,320},{320,384},{384,448},... | collective-permute-start | bytes 1572872 | tf_op jit(solution)/shard_map/while/body/eval_jaxpr/ppermute | solution.py:12
  250.9 21.7 %collective-permute-start = (bf16[2048,128]{1,0:T(8,128)(2,1)}, bf16[2048,128]{1,0:T(8,128)(2,1)S(1)}, u32[]{:S(2)}, u32[]{:S(2)}) collective-permute-start(bf16[2048,128]{1,0:T(8,128)(2,1)} %get-tuple-element.304), channel_id=1, source_target_pairs={{0,64},{64,128},{128,192},{192,256},{256,320},{320,384},{384,448},... | collective-permute-start | bytes 1572872 | tf_op jit(solution)/shard_map/while/body/eval_jaxpr/ppermute | solution.py:12
  274.8 17.1 %collective-permute-start.1 = (bf16[2048,128]{1,0:T(8,128)(2,1)S(1)}, bf16[2048,128]{1,0:T(8,128)(2,1)S(1)}, u32[]{:S(2)}, u32[]{:S(2)}) collective-permute-start(bf16[2048,128]{1,0:T(8,128)(2,1)S(1)} %get-tuple-element.305), channel_id=1, source_target_pairs={{0,64},{64,128},{128,192},{192,256},{256,320},{320,384},{384,448},... | collective-permute-start | bytes 1572872 | tf_op jit(solution)/shard_map/while/body/eval_jaxpr/ppermute | solution.py:12
  276.7 20.8 %collective-permute-start = (bf16[2048,128]{1,0:T(8,128)(2,1)}, bf16[2048,128]{1,0:T(8,128)(2,1)S(1)}, u32[]{:S(2)}, u32[]{:S(2)}) collective-permute-start(bf16[2048,128]{1,0:T(8,128)(2,1)} %get-tuple-element.304), channel_id=1, source_target_pairs={{0,64},{64,128},{128,192},{192,256},{256,320},{320,384},{384,448},... | collective-permute-start | bytes 1572872 | tf_op jit(solution)/shard_map/while/body/eval_jaxpr/ppermute | solution.py:12
  299.7 16.2 %collective-permute-start.1 = (bf16[2048,128]{1,0:T(8,128)(2,1)S(1)}, bf16[2048,128]{1,0:T(8,128)(2,1)S(1)}, u32[]{:S(2)}, u32[]{:S(2)}) collective-permute-start(bf16[2048,128]{1,0:T(8,128)(2,1)S(1)} %get-tuple-element.305), channel_id=1, source_target_pairs={{0,64},{64,128},{128,192},{192,256},{256,320},{320,384},{384,448},... | collective-permute-start | bytes 1572872 | tf_op jit(solution)/shard_map/while/body/eval_jaxpr/ppermute | solution.py:12
  301.6 19.9 %collective-permute-start = (bf16[2048,128]{1,0:T(8,128)(2,1)}, bf16[2048,128]{1,0:T(8,128)(2,1)S(1)}, u32[]{:S(2)}, u32[]{:S(2)}) collective-permute-start(bf16[2048,128]{1,0:T(8,128)(2,1)} %get-tuple-element.304), channel_id=1, source_target_pairs={{0,64},{64,128},{128,192},{192,256},{256,320},{320,384},{384,448},... | collective-permute-start | bytes 1572872 | tf_op jit(solution)/shard_map/while/body/eval_jaxpr/ppermute | solution.py:12
  323.7 15.3 %collective-permute-start.1 = (bf16[2048,128]{1,0:T(8,128)(2,1)S(1)}, bf16[2048,128]{1,0:T(8,128)(2,1)S(1)}, u32[]{:S(2)}, u32[]{:S(2)}) collective-permute-start(bf16[2048,128]{1,0:T(8,128)(2,1)S(1)} %get-tuple-element.305), channel_id=1, source_target_pairs={{0,64},{64,128},{128,192},{192,256},{256,320},{320,384},{384,448},... | collective-permute-start | bytes 1572872 | tf_op jit(solution)/shard_map/while/body/eval_jaxpr/ppermute | solution.py:12
  325.6 19.2 %collective-permute-start = (bf16[2048,128]{1,0:T(8,128)(2,1)}, bf16[2048,128]{1,0:T(8,128)(2,1)S(1)}, u32[]{:S(2)}, u32[]{:S(2)}) collective-permute-start(bf16[2048,128]{1,0:T(8,128)(2,1)} %get-tuple-element.304), channel_id=1, source_target_pairs={{0,64},{64,128},{128,192},{192,256},{256,320},{320,384},{384,448},... | collective-permute-start | bytes 1572872 | tf_op jit(solution)/shard_map/while/body/eval_jaxpr/ppermute | solution.py:12
  347.0 14.4 %collective-permute-start.1 = (bf16[2048,128]{1,0:T(8,128)(2,1)S(1)}, bf16[2048,128]{1,0:T(8,128)(2,1)S(1)}, u32[]{:S(2)}, u32[]{:S(2)}) collective-permute-start(bf16[2048,128]{1,0:T(8,128)(2,1)S(1)} %get-tuple-element.305), channel_id=1, source_target_pairs={{0,64},{64,128},{128,192},{192,256},{256,320},{320,384},{384,448},... | collective-permute-start | bytes 1572872 | tf_op jit(solution)/shard_map/while/body/eval_jaxpr/ppermute | solution.py:12
  348.9 19.3 %collective-permute-start = (bf16[2048,128]{1,0:T(8,128)(2,1)}, bf16[2048,128]{1,0:T(8,128)(2,1)S(1)}, u32[]{:S(2)}, u32[]{:S(2)}) collective-permute-start(bf16[2048,128]{1,0:T(8,128)(2,1)} %get-tuple-element.304), channel_id=1, source_target_pairs={{0,64},{64,128},{128,192},{192,256},{256,320},{320,384},{384,448},... | collective-permute-start | bytes 1572872 | tf_op jit(solution)/shard_map/while/body/eval_jaxpr/ppermute | solution.py:12
  370.3 13.6 %collective-permute-start.1 = (bf16[2048,128]{1,0:T(8,128)(2,1)S(1)}, bf16[2048,128]{1,0:T(8,128)(2,1)S(1)}, u32[]{:S(2)}, u32[]{:S(2)}) collective-permute-start(bf16[2048,128]{1,0:T(8,128)(2,1)S(1)} %get-tuple-element.305), channel_id=1, source_target_pairs={{0,64},{64,128},{128,192},{192,256},{256,320},{320,384},{384,448},... | collective-permute-start | bytes 1572872 | tf_op jit(solution)/shard_map/while/body/eval_jaxpr/ppermute | solution.py:12
  372.2 19.3 %collective-permute-start = (bf16[2048,128]{1,0:T(8,128)(2,1)}, bf16[2048,128]{1,0:T(8,128)(2,1)S(1)}, u32[]{:S(2)}, u32[]{:S(2)}) collective-permute-start(bf16[2048,128]{1,0:T(8,128)(2,1)} %get-tuple-element.304), channel_id=1, source_target_pairs={{0,64},{64,128},{128,192},{192,256},{256,320},{320,384},{384,448},... | collective-permute-start | bytes 1572872 | tf_op jit(solution)/shard_map/while/body/eval_jaxpr/ppermute | solution.py:12
  393.6 12.7 %collective-permute-start.1 = (bf16[2048,128]{1,0:T(8,128)(2,1)S(1)}, bf16[2048,128]{1,0:T(8,128)(2,1)S(1)}, u32[]{:S(2)}, u32[]{:S(2)}) collective-permute-start(bf16[2048,128]{1,0:T(8,128)(2,1)S(1)} %get-tuple-element.305), channel_id=1, source_target_pairs={{0,64},{64,128},{128,192},{192,256},{256,320},{320,384},{384,448},... | collective-permute-start | bytes 1572872 | tf_op jit(solution)/shard_map/while/body/eval_jaxpr/ppermute | solution.py:12
  395.6 19.3 %collective-permute-start = (bf16[2048,128]{1,0:T(8,128)(2,1)}, bf16[2048,128]{1,0:T(8,128)(2,1)S(1)}, u32[]{:S(2)}, u32[]{:S(2)}) collective-permute-start(bf16[2048,128]{1,0:T(8,128)(2,1)} %get-tuple-element.304), channel_id=1, source_target_pairs={{0,64},{64,128},{128,192},{192,256},{256,320},{320,384},{384,448},... | collective-permute-start | bytes 1572872 | tf_op jit(solution)/shard_map/while/body/eval_jaxpr/ppermute | solution.py:12
  417.0 12.3 %collective-permute-start.1 = (bf16[2048,128]{1,0:T(8,128)(2,1)S(1)}, bf16[2048,128]{1,0:T(8,128)(2,1)S(1)}, u32[]{:S(2)}, u32[]{:S(2)}) collective-permute-start(bf16[2048,128]{1,0:T(8,128)(2,1)S(1)} %get-tuple-element.305), channel_id=1, source_target_pairs={{0,64},{64,128},{128,192},{192,256},{256,320},{320,384},{384,448},... | collective-permute-start | bytes 1572872 | tf_op jit(solution)/shard_map/while/body/eval_jaxpr/ppermute | solution.py:12
  418.9 19.9 %collective-permute-start = (bf16[2048,128]{1,0:T(8,128)(2,1)}, bf16[2048,128]{1,0:T(8,128)(2,1)S(1)}, u32[]{:S(2)}, u32[]{:S(2)}) collective-permute-start(bf16[2048,128]{1,0:T(8,128)(2,1)} %get-tuple-element.304), channel_id=1, source_target_pairs={{0,64},{64,128},{128,192},{192,256},{256,320},{320,384},{384,448},... | collective-permute-start | bytes 1572872 | tf_op jit(solution)/shard_map/while/body/eval_jaxpr/ppermute | solution.py:12
  440.9 12.3 %collective-permute-start.1 = (bf16[2048,128]{1,0:T(8,128)(2,1)S(1)}, bf16[2048,128]{1,0:T(8,128)(2,1)S(1)}, u32[]{:S(2)}, u32[]{:S(2)}) collective-permute-start(bf16[2048,128]{1,0:T(8,128)(2,1)S(1)} %get-tuple-element.305), channel_id=1, source_target_pairs={{0,64},{64,128},{128,192},{192,256},{256,320},{320,384},{384,448},... | collective-permute-start | bytes 1572872 | tf_op jit(solution)/shard_map/while/body/eval_jaxpr/ppermute | solution.py:12
  442.9 16.0 %collective-permute-start = (bf16[2048,128]{1,0:T(8,128)(2,1)}, bf16[2048,128]{1,0:T(8,128)(2,1)S(1)}, u32[]{:S(2)}, u32[]{:S(2)}) collective-permute-start(bf16[2048,128]{1,0:T(8,128)(2,1)} %get-tuple-element.304), channel_id=1, source_target_pairs={{0,64},{64,128},{128,192},{192,256},{256,320},{320,384},{384,448},... | collective-permute-start | bytes 1572872 | tf_op jit(solution)/shard_map/while/body/eval_jaxpr/ppermute | solution.py:12
  (5 other events, 515.9 us)
where the time goes:
time: 478 us; the launch traced here: 477 us
  waiting for transfers between devices  317 us (66%)
  starting transfers between devices  81.8 us (17%)
  local copies, waits for them, and re-layouts  53 us (11%)
  other arithmetic  20.1 us (4%)
    ppermute x30, waiting for transfers between devices, from_behind(): lax.ppermute(shard, axis, [(i, (i + by) % size) for i in range(size)])  293 us
    ppermute x30, starting transfers between devices, from_behind(): lax.ppermute(shard, axis, [(i, (i + by) % size) for i in range(size)])  57.4 us
    all_to_all x1, starting transfers between devices, body(): lax.all_to_all(value_wide, 'head', split_axis=1, concat_axis=0, tiled=True)  17.5 us
    all_to_all x1, waiting for transfers between devices, body(): lax.all_to_all(key_wide, 'head', split_axis=1, concat_axis=0, tiled=True)  13.6 us
    while x30, local copies, waits for them, and re-layouts  12.5 us
    dynamic_update_slice x15, other arithmetic, collect(): lax.dynamic_update_slice_in_dim(buffers[1], value_part[None], owner_index...  11.4 us
    all_to_all x1, waiting for transfers between devices, body(): lax.all_to_all(value_wide, 'head', split_axis=1, concat_axis=0, tiled=True)  10.8 us
  transfers between devices with their start and end apart: 32, of which 32 were waited for; matrix products, arithmetic and copies ran while one was open for 4% of the time, Pallas kernels for 0%

commit v1 on v0

v1 whole, which is shorter than its diff:
```python
import jax
import jax.numpy as jnp
from jax import lax
from jax.experimental import pallas as pl
from jax.experimental.pallas import tpu as pltpu
from jax.sharding import PartitionSpec as P

BLK = 128
CAP = 2
LOG2E = 1.4426950408889634


def pick_first(index_ref, table_ref, out_ref):
    for i in range(out_ref.shape[0]):
        out_ref[i] = table_ref[index_ref[i]]


def pick_second(index_ref, own_ref, foreign_ref, out_ref):
    own_count = own_ref.shape[0]
    for i in range(out_ref.shape[0]):
        at = index_ref[i]
        mine = own_ref[jnp.minimum(at, own_count - 1)]
        theirs = foreign_ref[jnp.maximum(at - own_count, 0)]
        out_ref[i] = jnp.where(at < own_count, mine, theirs)


def attend(pos_ref, query_ref, pair_ref, out_ref, key_all, value_all):
    pieces, pair_count, _, rows, width = pair_ref.shape
    heads = query_ref.shape[0]
    blocks = query_ref.shape[1] // BLK
    slots = pair_count // blocks
    factor = (width ** -0.5) * LOG2E
    row = lax.broadcasted_iota(jnp.int32, (BLK, BLK), 0)
    col = lax.broadcasted_iota(jnp.int32, (BLK, BLK), 1)
    piece = col // rows
    half = pieces // 2
    key_row = 2 * rows * (piece % half) + rows * (piece // half) + col % rows
    causal = key_row <= row
    for b in range(blocks):
        for j in range(slots):
            i = b * slots + j
            key_all[b, pl.ds(j * BLK, BLK), :] = pair_ref[:, i, 0].reshape(BLK, width)
            value_all[b, pl.ds(j * BLK, BLK), :] = pair_ref[:, i, 1].reshape(BLK, width)
    for b in range(blocks):
        pos = pos_ref[b]

        def one_head(h, carry):
            q = query_ref[h, pl.ds(b * BLK, BLK), :]
            s = lax.dot_general(
                q, key_all[b], (((1,), (1,)), ((), ())), preferred_element_type=jnp.float32
            )
            parts = [jnp.where(causal, s[:, :BLK], -1e30)]
            for j in range(1, slots):
                parts.append(jnp.where(pos >= j, s[:, j * BLK:(j + 1) * BLK], -1e30))
            s = jnp.concatenate(parts, axis=1)
            peak = jnp.max(s, axis=1, keepdims=True)
            raised = jnp.exp2((s - peak) * factor)
            total = jnp.sum(raised, axis=1, keepdims=True)
            mixed = jnp.dot(
                raised.astype(jnp.bfloat16), value_all[b], preferred_element_type=jnp.float32
            )
            out_ref[h, pl.ds(b * BLK, BLK), :] = (mixed / total).astype(jnp.bfloat16)
            return carry

        lax.fori_loop(0, heads, one_head, 0, unroll=2)


def body(queries, keys, values, key_blocks, span_order):
    ctx_count = lax.axis_size("ctx")
    head_count = lax.axis_size("head")
    rows_device, _, width = queries.shape
    shard_rows, kv_heads, _ = keys.shape
    slot_count = key_blocks.shape[1]
    block_count = rows_device // BLK
    per_span = block_count // 2
    group = head_count // kv_heads
    shards_per_block = BLK // shard_rows
    halves = group // shards_per_block
    piece_rows = shard_rows // halves
    me = lax.axis_index("ctx")
    rank = lax.axis_index("head") % group
    i32 = jnp.int32

    spread_groups = [
        [shards_per_block * j + q for j in range(block_count)] for q in range(shards_per_block)
    ]
    kv = jnp.stack([keys, values])
    kv = kv.reshape(2, halves, piece_rows, kv_heads, width).transpose(3, 1, 0, 2, 4)
    kv = kv.reshape(block_count, 2, piece_rows, width)
    own = lax.all_to_all(kv, "head", 0, 0, tiled=True, axis_index_groups=spread_groups)

    span_ids = jnp.arange(2 * ctx_count, dtype=i32)
    by_span = key_blocks.reshape(2 * ctx_count, per_span * slot_count)
    stored = jnp.take(by_span, span_order, axis=0)
    lane = jnp.arange(per_span * slot_count, dtype=i32)[None, :]
    position = span_order[:, None] * per_span + lane // slot_count
    in_use = lane % slot_count <= position
    my_spans = lax.dynamic_slice(span_order, (2 * me,), (2,))
    listed_span = stored // per_span
    second = listed_span == my_spans[1]
    from_me = in_use & (second | (listed_span == my_spans[0]))
    local_block = stored % per_span + jnp.where(second, per_span, 0)
    lowest = jnp.where(from_me, local_block, block_count - 1).reshape(ctx_count, -1).min(axis=1)
    highest = jnp.where(from_me, local_block, 0).reshape(ctx_count, -1).max(axis=1)
    chosen = jnp.stack([lowest, highest], axis=1).reshape(-1)

    mine = lax.dynamic_slice(stored, (2 * me, 0), (2, per_span * slot_count)).reshape(-1)
    mine_used = lax.dynamic_slice(in_use, (2 * me, 0), (2, per_span * slot_count)).reshape(-1)
    stored_at = jnp.sum(
        jnp.where(span_order[None, :] == (mine // per_span)[:, None], span_ids[None, :], 0), axis=1
    )
    owner = stored_at // 2
    held = stored_at % 2 * per_span + mine % per_span
    lower = mine_used[None, :] & (owner[None, :] == owner[:, None]) & (held[None, :] < held[:, None])
    upper = jnp.any(lower, axis=1).astype(i32)
    source = jnp.where(owner == me, held, block_count + owner * CAP + upper)
    local_ids = jnp.arange(block_count, dtype=i32)
    own_pos = my_spans[local_ids // per_span] * per_span + local_ids % per_span
    per_rank = block_count // group
    query_pos = lax.dynamic_slice(own_pos, (rank * per_rank,), (per_rank,))

    smem = pl.BlockSpec(memory_space=pltpu.SMEM)
    vmem = pl.BlockSpec(memory_space=pltpu.VMEM)
    piece = (2, piece_rows, width)

    asked = pl.pallas_call(
        pick_first,
        out_shape=jax.ShapeDtypeStruct((ctx_count * CAP,) + piece, jnp.bfloat16),
        in_specs=[smem, vmem],
        out_specs=vmem,
    )(chosen, own)
    foreign = lax.all_to_all(asked, "ctx", 0, 0, tiled=True)

    kv_groups = [[g * group + i for i in range(group)] for g in range(kv_heads)]
    query_rows = queries.reshape(group, rows_device // group, width)
    query_rows, own_after = lax.optimization_barrier((query_rows, own))
    query_here = lax.all_to_all(
        query_rows, "head", 0, 0, tiled=True, axis_index_groups=kv_groups
    )
    pairs = pl.pallas_call(
        pick_second,
        out_shape=jax.ShapeDtypeStruct((block_count * slot_count,) + piece, jnp.bfloat16),
        in_specs=[smem, vmem, vmem],
        out_specs=vmem,
    )(source, own_after, foreign)
    pairs = lax.all_to_all(pairs, "head", 0, 0, tiled=True, axis_index_groups=kv_groups)
    pairs = pairs.reshape((group, per_rank * slot_count) + piece)

    done = pl.pallas_call(
        attend,
        out_shape=jax.ShapeDtypeStruct(query_here.shape, jnp.bfloat16),
        in_specs=[smem, vmem, vmem],
        out_specs=vmem,
        scratch_shapes=[pltpu.VMEM((per_rank, slot_count * BLK, width), jnp.bfloat16)] * 2,
        compiler_params=pltpu.CompilerParams(vmem_limit_bytes=24 * 2**20),
    )(query_pos, query_here, pairs)

    out = lax.all_to_all(done, "head", 0, 0, tiled=True, axis_index_groups=kv_groups)
    return out.reshape(rows_device, 1, width)


def solution(mesh):
    in_specs = (
        P("ctx", "head", None),
        P(("ctx", "head"), None, None),
        P(("ctx", "head"), None, None),
        P(),
        P(),
    )
    out_specs = P("ctx", "head", None)
    return jax.shard_map(body, mesh=mesh, in_specs=in_specs, out_specs=out_specs, check_vma=False)
```

time: 478 us -> 125 us (0.26)
  the two profiles are of different devices: /device:TPU:6 before, /device:TPU:1 now
where the time goes in v1:
time: 125 us; the launch traced here: 124 us
  starting transfers between devices  43.3 us (35%)
  waiting for transfers between devices  41.6 us (33%)
  blocking collectives  17.6 us (14%)
  Pallas kernels  9.66 us (8%)
  local copies, waits for them, and re-layouts  6.44 us (5%)
  other arithmetic  5.2 us (4%)
    all_to_all x1, starting transfers between devices, body(): foreign = lax.all_to_all(asked, 'ctx', 0, 0, tiled=True)  18.6 us
    all_to_all x1, blocking collectives, body(): lax.all_to_all(done, 'head', 0, 0, tiled=True, axis_index_groups=kv_groups)  17.6 us
    all_to_all x1, waiting for transfers between devices, body(): lax.all_to_all(pairs, 'head', 0, 0, tiled=True, axis_index_groups=kv_groups)  13.2 us
    all_to_all x1, waiting for transfers between devices, body(): foreign = lax.all_to_all(asked, 'ctx', 0, 0, tiled=True)  12.8 us
    all_to_all x1, waiting for transfers between devices, body(): lax.all_to_all(query_rows, 'head', 0, 0, tiled=True, axis_index_groups=kv...  11.3 us
    all_to_all x1, starting transfers between devices, body(): lax.all_to_all(query_rows, 'head', 0, 0, tiled=True, axis_index_groups=kv...  10.3 us
    all_to_all x1, starting transfers between devices, body(): lax.all_to_all(kv, 'head', 0, 0, tiled=True, axis_index_groups=spread_gro...  10.2 us
    pallas_call x1, Pallas kernels, body(): pl.pallas_call(attend, out_shape=jax.ShapeDtypeStruct(query_here.shape, j...  5.94 us
  transfers between devices with their start and end apart: 4, of which 4 were waited for; matrix products, arithmetic and copies ran while one was open for 6% of the time, Pallas kernels for 2%

profile of v1, /device:TPU:1, one launch (start us, length us, event | category | flops | bytes accessed | tf_op | source)
XLA Modules:
  0.0 123.9 jit_solution(6112485166049294311)
XLA Ops:
  0.0 0.9 copy.14
  0.9 0.7 pad_maximum_fusion
  1.6 10.2 %all-to-all-start = ((bf16[16,2,16,128]{3,2,1,0:T(8,128)(2,1)}), bf16[16,2,16,128]{3,2,1,0:T(8,128)(2,1)S(1)}, u32[]{:S(2)}, u32[]{:S(2)}) async-start(bf16[16,2,16,128]{3,2,1,0:T(8,128)(2,1)} %bitcast.7), calls=%async_computation | async-start | bytes 262144 | tf_op jit(solution)/shard_map/all_to_all | solution.py:90
  11.8 0.6 copy-done.4
  12.6 0.6 fusion.8
  13.2 0.1 copy-done.3
  13.3 0.1 copy.16
  13.4 0.1 reshape.314
  13.5 0.6 gather_fusion
  14.1 0.7 fusion
  14.8 1.3 %or_and_fusion = (pred[32,32]{1,0:T(8,128)(4,1)S(1)}, pred[32,32]{1,0:T(8,128)(4,1)S(1)}) fusion(s32[]{:T(128)} %bitcast.1, s32[]{:T(128)} %bitcast, s32[32,32]{1,0:T(8,128)S(1)} %get-tuple-element.12, s32[32]{0:T(128)S(1)} %get-tuple-element.21, s32[32]{0:T(128)S(1)} %get-tuple-element.15, s32[32]{0:T(128)S(1)} %get-tuple-element.22), kind=kLoop, calls=%fused_computation.15 | loop fusion | flops 21504 | bytes 6536 | tf_op jit(solution)/shard_map/and | solution.py:101
  16.1 0.1 select_reduce_fusion.1
  16.4 0.1 reduce_min.18
  16.5 0.1 reduce_max.18
  16.7 0.7 reshape.316.index_ref
  17.4 4.3 %all-to-all-done.table_ref.own_ref = bf16[16,2,16,128]{3,2,1,0:T(8,128)(2,1)S(1)} async-done(((bf16[16,2,16,128]{3,2,1,0:T(8,128)(2,1)}), bf16[16,2,16,128]{3,2,1,0:T(8,128)(2,1)S(1)}, u32[]{:S(2)}, u32[]{:S(2)}) %all-to-all-start) | async-done | bytes 131104 | tf_op jit(solution)/shard_map/all_to_all | solution.py:90
  21.7 0.7 copy-done
  22.3 1.6 %shard_map.55 = bf16[32,2,16,128]{3,2,1,0:T(8,128)(2,1)} custom-call(s32[32]{0:T(128)} %reshape.316.index_ref, bf16[16,2,16,128]{3,2,1,0:T(8,128)(2,1)} %copy-done), custom_call_target="tpu_custom_call" | custom-call | tf_op jit(solution)/shard_map/pallas_call | solution.py:126
  24.0 18.6 %all-to-all-start.2 = ((bf16[32,2,16,128]{3,2,1,0:T(8,128)(2,1)}), bf16[32,2,16,128]{3,2,1,0:T(8,128)(2,1)S(1)}, u32[]{:S(2)}, u32[]{:S(2)}) async-start(bf16[32,2,16,128]{3,2,1,0:T(8,128)(2,1)} %shard_map.55), calls=%async_computation.2 | async-start | bytes 524288 | tf_op jit(solution)/shard_map/all_to_all | solution.py:132
  42.6 12.8 %all-to-all-done.2.foreign_ref = bf16[32,2,16,128]{3,2,1,0:T(8,128)(2,1)S(1)} async-done(((bf16[32,2,16,128]{3,2,1,0:T(8,128)(2,1)}), bf16[32,2,16,128]{3,2,1,0:T(8,128)(2,1)S(1)}, u32[]{:S(2)}, u32[]{:S(2)}) %all-to-all-start.2) | async-done | bytes 262176 | tf_op jit(solution)/shard_map/all_to_all | solution.py:132
  55.4 0.7 copy-done.1
  56.0 10.3 %all-to-all-start.1 = ((bf16[8,256,128]{2,1,0:T(8,128)(2,1)}), bf16[8,256,128]{2,1,0:T(8,128)(2,1)S(1)}, u32[]{:S(2)}, u32[]{:S(2)}) async-start(bf16[8,256,128]{2,1,0:T(8,128)(2,1)} %bitcast.3), calls=%async_computation.1 | async-start | bytes 1048576 | tf_op jit(solution)/shard_map/all_to_all | solution.py:137
  66.6 0.2 and_reduce_fusion
  66.8 0.6 compare_select_fusion.3.index_ref
  67.4 2.1 %shard_map.56 = bf16[64,2,16,128]{3,2,1,0:T(8,128)(2,1)} custom-call(s32[64]{0:T(128)} %compare_select_fusion.3.index_ref, bf16[16,2,16,128]{3,2,1,0:T(8,128)(2,1)} %copy-done, bf16[32,2,16,128]{3,2,1,0:T(8,128)(2,1)} %copy-done.1), custom_call_target="tpu_custom_call" | custom-call | tf_op jit(solution)/shard_map/pallas_call | solution.py:140
  69.5 11.3 %all-to-all-done.1.query_ref = bf16[8,256,128]{2,1,0:T(8,128)(2,1)S(1)} async-done(((bf16[8,256,128]{2,1,0:T(8,128)(2,1)}), bf16[8,256,128]{2,1,0:T(8,128)(2,1)S(1)}, u32[]{:S(2)}, u32[]{:S(2)}) %all-to-all-start.1) | async-done | bytes 524320 | tf_op jit(solution)/shard_map/all_to_all | solution.py:137
  80.8 4.3 %all-to-all-start.3 = ((bf16[64,2,16,128]{3,2,1,0:T(8,128)(2,1)}), bf16[64,2,16,128]{3,2,1,0:T(8,128)(2,1)S(1)}, u32[]{:S(2)}, u32[]{:S(2)}) async-start(bf16[64,2,16,128]{3,2,1,0:T(8,128)(2,1)} %shard_map.56), calls=%async_computation.3 | async-start | bytes 1048576 | tf_op jit(solution)/shard_map/all_to_all | solution.py:146
  85.1 1.3 %fusion.3 = s32[16]{0:T(128)S(1)} fusion(s32[]{:T(128)} %bitcast.1, s32[]{:T(128)} %bitcast), kind=kLoop, calls=%fused_computation.45 | loop fusion | flops 336 | bytes 72 | tf_op jit(solution)/shard_map/add | solution.py:118
  86.4 13.2 %all-to-all-done.3 = bf16[64,2,16,128]{3,2,1,0:T(8,128)(2,1)S(1)} async-done(((bf16[64,2,16,128]{3,2,1,0:T(8,128)(2,1)}), bf16[64,2,16,128]{3,2,1,0:T(8,128)(2,1)S(1)}, u32[]{:S(2)}, u32[]{:S(2)}) %all-to-all-start.3) | async-done | bytes 524320 | tf_op jit(solution)/shard_map/all_to_all | solution.py:146
  99.6 5.9 %shard_map.57 = bf16[8,256,128]{2,1,0:T(8,128)(2,1)S(1)} custom-call(s32[2]{0:T(128)S(1)} %dynamic_slice.13.pos_ref, bf16[8,256,128]{2,1,0:T(8,128)(2,1)S(1)} %all-to-all-done.1.query_ref, bf16[8,8,2,16,128]{4,3,2,1,0:T(8,128)(2,1)S(1)} %bitcast.16), custom_call_target="tpu_custom_call" | custom-call | tf_op jit(solution)/shard_map/pallas_call | solution.py:149
  105.5 17.6 %all_to_all.25 = bf16[8,256,128]{2,1,0:T(8,128)(2,1)S(1)} all-to-all(bf16[8,256,128]{2,1,0:T(8,128)(2,1)S(1)} %shard_map.57), channel_id=1, replica_groups={{0,1,2,3,4,5,6,7},{8,9,10,11,12,13,14,15},{16,17,18,19,20,21,22,23},{24..., dimensions={0} | all-to-all | bytes 1048576 | tf_op jit(solution)/shard_map/all_to_all | solution.py:158
  123.1 0.8 copy.19
  (24 shorter events, 0.8 us)
Async XLA Ops:
  0.0 0.9 copy-start.2
  1.6 20.1 %all-to-all-start = ((bf16[16,2,16,128]{3,2,1,0:T(8,128)(2,1)}), bf16[16,2,16,128]{3,2,1,0:T(8,128)(2,1)S(1)}, u32[]{:S(2)}, u32[]{:S(2)}) async-start(bf16[16,2,16,128]{3,2,1,0:T(8,128)(2,1)} %bitcast.7), calls=%async_computation | async-start | bytes 262144 | tf_op jit(solution)/shard_map/all_to_all | solution.py:90
  11.8 0.7 copy-start.4
  12.6 0.7 copy-start.3
  21.7 0.7 copy-start
  24.0 31.4 %all-to-all-start.2 = ((bf16[32,2,16,128]{3,2,1,0:T(8,128)(2,1)}), bf16[32,2,16,128]{3,2,1,0:T(8,128)(2,1)S(1)}, u32[]{:S(2)}, u32[]{:S(2)}) async-start(bf16[32,2,16,128]{3,2,1,0:T(8,128)(2,1)} %shard_map.55), calls=%async_computation.2 | async-start | bytes 524288 | tf_op jit(solution)/shard_map/all_to_all | solution.py:132
  55.4 0.7 copy-start.1
  56.0 24.8 %all-to-all-start.1 = ((bf16[8,256,128]{2,1,0:T(8,128)(2,1)}), bf16[8,256,128]{2,1,0:T(8,128)(2,1)S(1)}, u32[]{:S(2)}, u32[]{:S(2)}) async-start(bf16[8,256,128]{2,1,0:T(8,128)(2,1)} %bitcast.3), calls=%async_computation.1 | async-start | bytes 1048576 | tf_op jit(solution)/shard_map/all_to_all | solution.py:137
  80.8 18.8 %all-to-all-start.3 = ((bf16[64,2,16,128]{3,2,1,0:T(8,128)(2,1)}), bf16[64,2,16,128]{3,2,1,0:T(8,128)(2,1)S(1)}, u32[]{:S(2)}, u32[]{:S(2)}) async-start(bf16[64,2,16,128]{3,2,1,0:T(8,128)(2,1)} %shard_map.56), calls=%async_computation.3 | async-start | bytes 1048576 | tf_op jit(solution)/shard_map/all_to_all | solution.py:146

commit v2 on v1

v2 whole, which is shorter than its diff:
```python
import functools

import jax
import jax.numpy as jnp
from jax import lax
from jax.experimental import pallas as pl
from jax.experimental.pallas import tpu as pltpu
from jax.sharding import PartitionSpec as P

BLK = 128
CAP = 2
LOG2E = 1.4426950408889634
MASKED = -1e30
SMEM = pl.BlockSpec(memory_space=pltpu.SMEM)
VMEM = pl.BlockSpec(memory_space=pltpu.VMEM)


def small(mib=4):
    return pltpu.CompilerParams(vmem_limit_bytes=mib * 2**20)


def asked_range(per_span, me_ref, span_ref, listed_ref, out_ref):
    listed = listed_ref[...]
    slots, positions = listed.shape
    first = span_ref[2 * me_ref[0]]
    second = span_ref[2 * me_ref[0] + 1]
    slot = lax.broadcasted_iota(jnp.int32, listed.shape, 0)
    position = lax.broadcasted_iota(jnp.int32, listed.shape, 1)
    span = listed // per_span
    mine = (slot <= position) & ((span == first) | (span == second))
    block = listed % per_span + jnp.where(span == second, per_span, 0)
    low = jnp.min(jnp.where(mine, block, 2 * per_span - 1), axis=0, keepdims=True)
    high = jnp.max(jnp.where(mine, block, 0), axis=0, keepdims=True)
    low = jnp.broadcast_to(low, (8, positions))
    high = jnp.broadcast_to(high, (8, positions))
    step = 1
    while step < per_span:
        low = jnp.minimum(low, pltpu.roll(low, positions - step, 1))
        high = jnp.maximum(high, pltpu.roll(high, positions - step, 1))
        step *= 2
    out_ref[0:1, :] = low[0:1]
    out_ref[1:2, :] = high[0:1]


def pick_asked(per_span, span_ref, range_ref, own_ref, out_ref):
    for d in range(out_ref.shape[0] // CAP):
        a = span_ref[2 * d] * per_span
        b = span_ref[2 * d + 1] * per_span
        out_ref[2 * d] = own_ref[jnp.minimum(range_ref[0, a], range_ref[0, b])]
        out_ref[2 * d + 1] = own_ref[jnp.maximum(range_ref[1, a], range_ref[1, b])]


def find_sources(per_span, me_ref, span_ref, listed_ref, out_ref, inverse, lowest, owners, helds):
    me = me_ref[0]
    slots = listed_ref.shape[0]
    span_count = span_ref.shape[0]
    blocks = 2 * per_span

    def invert(s, carry):
        inverse[span_ref[s]] = s
        return carry

    def reset(s, carry):
        lowest[s] = blocks
        return carry

    lax.fori_loop(0, span_count, invert, 0, unroll=4)
    lax.fori_loop(0, span_count // 2, reset, 0, unroll=4)

    def scan(block, carry):
        position = span_ref[2 * me + block // per_span] * per_span + block % per_span
        for j in range(1, slots):
            name = listed_ref[j, position]
            at = inverse[name // per_span]
            owner = at // 2
            held = at % 2 * per_span + name % per_span
            owners[block * slots + j] = owner
            helds[block * slots + j] = held
            lowest[owner] = jnp.minimum(lowest[owner], jnp.where(j <= position, held, blocks))
        return carry

    lax.fori_loop(0, blocks, scan, 0, unroll=2)

    def place(block, carry):
        out_ref[block * slots] = block
        for j in range(1, slots):
            owner = owners[block * slots + j]
            held = helds[block * slots + j]
            foreign = blocks + CAP * owner + jnp.where(held > lowest[owner], 1, 0)
            out_ref[block * slots + j] = jnp.where(owner == me, held, foreign)
        return carry

    lax.fori_loop(0, blocks, place, 0, unroll=2)


def pick_pairs(source_ref, own_ref, foreign_ref, out_ref):
    own_count = own_ref.shape[0]
    for i in range(out_ref.shape[0]):
        at = source_ref[i]
        mine = own_ref[jnp.minimum(at, own_count - 1)]
        theirs = foreign_ref[jnp.maximum(at - own_count, 0)]
        out_ref[i] = jnp.where(at < own_count, mine, theirs)


def bundle(rank_ref, query_ref, sibling_ref, *out_refs):
    chip = rank_ref[0] // 2
    core = rank_ref[0] % 2
    for k, out_ref in enumerate(out_refs):
        to = chip ^ k
        out_ref[0] = query_ref[2 * to + core]
        out_ref[1] = sibling_ref[to]


def attend(per_span, me_ref, rank_ref, span_ref, *refs):
    *query_refs, pair_ref, out_ref, key_all, value_all = refs
    pieces, pair_count, _, rows, width = pair_ref.shape
    blocks = key_all.shape[0]
    slots = pair_count // blocks
    factor = (width ** -0.5) * LOG2E
    chip = rank_ref[0] // 2
    core = rank_ref[0] % 2
    row = lax.broadcasted_iota(jnp.int32, (BLK, BLK), 0)
    col = lax.broadcasted_iota(jnp.int32, (BLK, BLK), 1)
    piece = col // rows
    half = pieces // 2
    causal = 2 * rows * (piece % half) + rows * (piece // half) + col % rows <= row
    causal = jnp.concatenate([causal, causal], axis=0)
    for b in range(blocks):
        for j in range(slots):
            i = b * slots + j
            key_all[b, j * BLK:(j + 1) * BLK, :] = pair_ref[:, i, 0].reshape(BLK, width)
            value_all[b, j * BLK:(j + 1) * BLK, :] = pair_ref[:, i, 1].reshape(BLK, width)
    for b in range(blocks):
        block = rank_ref[0] * blocks + b
        position = span_ref[2 * me_ref[0] + block // per_span] * per_span + block % per_span
        here = slice(b * BLK, (b + 1) * BLK)
        for k, query_ref in enumerate(query_refs):
            q = query_ref[:, here, :].reshape(2 * BLK, width)
            s = lax.dot_general(
                q, key_all[b], (((1,), (1,)), ((), ())), preferred_element_type=jnp.float32
            )
            parts = [jnp.where(causal, s[:, :BLK], MASKED)]
            for j in range(1, slots):
                parts.append(jnp.where(position >= j, s[:, j * BLK:(j + 1) * BLK], MASKED))
            peak = functools.reduce(jnp.maximum, parts)
            peak = jnp.max(peak, axis=1, keepdims=True) * factor
            total = jnp.zeros((2 * BLK, BLK), jnp.float32)
            mixed = jnp.zeros((2 * BLK, width), jnp.float32)
            for j in range(slots):
                raised = jnp.exp2(parts[j] * factor - peak)
                total += raised
                mixed += jnp.dot(
                    raised.astype(jnp.bfloat16),
                    value_all[b, j * BLK:(j + 1) * BLK],
                    preferred_element_type=jnp.float32,
                )
            total = jnp.sum(total, axis=1, keepdims=True)
            result = (mixed * (1.0 / total)).astype(jnp.bfloat16)
            out_ref[2 * (chip ^ k) + core, here, :] = result[:BLK]
            out_ref[2 * (chip ^ k) + 1 - core, here, :] = result[BLK:]


def body(queries, keys, values, key_blocks, span_order):
    ctx_count = lax.axis_size("ctx")
    head_count = lax.axis_size("head")
    rows_device, _, width = queries.shape
    shard_rows, kv_heads, _ = keys.shape
    slot_count = key_blocks.shape[1]
    block_count = rows_device // BLK
    per_span = block_count // 2
    group = head_count // kv_heads
    shards_per_block = BLK // shard_rows
    halves = group // shards_per_block
    piece_rows = shard_rows // halves
    per_rank = block_count // group
    chips = group // 2
    i32 = jnp.int32
    bf16 = jnp.bfloat16
    me = lax.axis_index("ctx").astype(i32)
    rank = lax.rem(lax.axis_index("head").astype(i32), group)
    piece = (2, piece_rows, width)
    listed = key_blocks.T

    spread_groups = [
        [shards_per_block * j + q for j in range(block_count)] for q in range(shards_per_block)
    ]
    kv = jnp.stack([keys, values])
    kv = kv.reshape(2, halves, piece_rows, kv_heads, width).transpose(3, 1, 0, 2, 4)
    kv = kv.reshape((block_count,) + piece)
    own = lax.all_to_all(kv, "head", 0, 0, tiled=True, axis_index_groups=spread_groups)

    ranges = pl.pallas_call(
        functools.partial(asked_range, per_span),
        out_shape=jax.ShapeDtypeStruct((2, key_blocks.shape[0]), i32),
        in_specs=[SMEM, SMEM, VMEM],
        out_specs=VMEM,
        compiler_params=small(),
    )(me[None], span_order, listed)

    asked = pl.pallas_call(
        functools.partial(pick_asked, per_span),
        out_shape=jax.ShapeDtypeStruct((ctx_count * CAP,) + piece, bf16),
        in_specs=[SMEM, SMEM, VMEM],
        out_specs=VMEM,
        compiler_params=small(),
    )(span_order, ranges, own)
    foreign = lax.all_to_all(asked, "ctx", 0, 0, tiled=True)

    core = lax.rem(rank, 2)
    query_parts = queries.reshape(chips, 2, rows_device // group, width)
    query_parts, span_after, _ = lax.optimization_barrier((query_parts, span_order, asked))
    crossing = lax.dynamic_index_in_dim(query_parts, 1 - core, 1, keepdims=False)
    sibling = lax.ppermute(crossing, "head", [(i, i ^ 1) for i in range(head_count)])
    part = jax.ShapeDtypeStruct((2, rows_device // group, width), bf16)
    bundles = pl.pallas_call(
        bundle,
        out_shape=(part,) * chips,
        in_specs=[SMEM, VMEM, VMEM],
        out_specs=(VMEM,) * chips,
        compiler_params=small(8),
    )(rank[None], query_parts.reshape(group, rows_device // group, width), sibling)
    source = pl.pallas_call(
        functools.partial(find_sources, per_span),
        out_shape=jax.ShapeDtypeStruct((block_count * slot_count,), i32),
        in_specs=[SMEM, SMEM, SMEM],
        out_specs=SMEM,
        scratch_shapes=[
            pltpu.SMEM((2 * ctx_count,), i32),
            pltpu.SMEM((ctx_count,), i32),
            pltpu.SMEM((block_count * slot_count,), i32),
            pltpu.SMEM((block_count * slot_count,), i32),
        ],
        compiler_params=small(),
    )(me[None], span_after, listed)
    query_here = [bundles[0]] + [
        lax.ppermute(bundles[k], "head", [(i, i ^ (2 * k)) for i in range(head_count)])
        for k in range(1, chips)
    ]
    source, _ = lax.optimization_barrier((source, bundles))

    kv_groups = [[g * group + i for i in range(group)] for g in range(kv_heads)]
    pairs = pl.pallas_call(
        pick_pairs,
        out_shape=jax.ShapeDtypeStruct((block_count * slot_count,) + piece, bf16),
        in_specs=[SMEM, VMEM, VMEM],
        out_specs=VMEM,
        compiler_params=small(),
    )(source, own, foreign)
    pairs = lax.all_to_all(pairs, "head", 0, 0, tiled=True, axis_index_groups=kv_groups)
    pairs = pairs.reshape((group, per_rank * slot_count) + piece)

    done = pl.pallas_call(
        functools.partial(attend, per_span),
        out_shape=jax.ShapeDtypeStruct((group, per_rank * BLK, width), bf16),
        in_specs=[SMEM, SMEM, SMEM] + [VMEM] * (chips + 1),
        out_specs=VMEM,
        scratch_shapes=[pltpu.VMEM((per_rank, slot_count * BLK, width), bf16)] * 2,
        compiler_params=small(24),
    )(me[None], rank[None], span_order, *query_here, pairs)

    out = lax.all_to_all(done, "head", 0, 0, tiled=True, axis_index_groups=kv_groups)
    return out.reshape(rows_device, 1, width)


def solution(mesh):
    in_specs = (
        P("ctx", "head", None),
        P(("ctx", "head"), None, None),
        P(("ctx", "head"), None, None),
        P(),
        P(),
    )
    out_specs = P("ctx", "head", None)
    return jax.shard_map(body, mesh=mesh, in_specs=in_specs, out_specs=out_specs, check_vma=False)
```

time: 125 us -> 113 us (0.904)
  waiting for transfers between devices: 41.6 us -> 29 us
  starting transfers between devices: 43.3 us -> 52.4 us
  local copies, waits for them, and re-layouts: 6.44 us -> 1.73 us
  other arithmetic: 5.2 us -> 0.67 us
  blocking collectives: 17.6 us -> 19.6 us
    ppermute x0 -> x4, waiting for transfers between devices: none -> 13.7 us  [the longest x3 13.7 us: body(): lax.ppermute(bundles[k], 'head', [(i, i ^ 2 * k) for i in range(head_coun...]
    ppermute x0 -> x4, starting transfers between devices: none -> 13.2 us  [the longest x3 9.26 us: body(): lax.ppermute(bundles[k], 'head', [(i, i ^ 2 * k) for i in range(head_coun...]
    all_to_all x1, waiting for transfers between devices: 13.2 us -> 0.01 us  [body(): lax.all_to_all(pairs, 'head', 0, 0, tiled=True, axis_index_groups=kv_groups)]
    all_to_all x1 -> x0, waiting for transfers between devices: 11.3 us -> none  [body(): lax.all_to_all(query_rows, 'head', 0, 0, tiled=True, axis_index_groups=kv...]
    all_to_all x1 -> x0, starting transfers between devices: 10.3 us -> none  [body(): lax.all_to_all(query_rows, 'head', 0, 0, tiled=True, axis_index_groups=kv...]
    all_to_all x1, waiting for transfers between devices: 12.8 us -> 6.29 us  [body(): foreign = lax.all_to_all(asked, 'ctx', 0, 0, tiled=True)]
    all_to_all x1, starting transfers between devices: 4.27 us -> 10.3 us  [body(): lax.all_to_all(pairs, 'head', 0, 0, tiled=True, axis_index_groups=kv_groups)]
    all_to_all x1, waiting for transfers between devices: 4.29 us -> 9.05 us  [body(): lax.all_to_all(kv, 'head', 0, 0, tiled=True, axis_index_groups=spread_gro...]
  transfers between devices with their start and end apart: 4 -> 7, of which waited for: 4 -> 4; matrix products, arithmetic and copies ran while one was open for 6% -> 0% of each run, Pallas kernels for 2% -> 3%
where the time goes in v2:
time: 113 us; the launch traced here: 112 us
  starting transfers between devices  52.4 us (46%)
  waiting for transfers between devices  29 us (26%)
  blocking collectives  19.6 us (17%)
  Pallas kernels  8.51 us (8%)
  local copies, waits for them, and re-layouts  1.73 us (2%)
    all_to_all x1, blocking collectives, body(): lax.all_to_all(done, 'head', 0, 0, tiled=True, axis_index_groups=kv_groups)  19.6 us
    all_to_all x1, starting transfers between devices, body(): foreign = lax.all_to_all(asked, 'ctx', 0, 0, tiled=True)  18.6 us
    ppermute x3, waiting for transfers between devices, body(): lax.ppermute(bundles[k], 'head', [(i, i ^ 2 * k) for i in range(head_coun...  13.7 us
    all_to_all x1, starting transfers between devices, body(): lax.all_to_all(kv, 'head', 0, 0, tiled=True, axis_index_groups=spread_gro...  10.3 us
    all_to_all x1, starting transfers between devices, body(): lax.all_to_all(pairs, 'head', 0, 0, tiled=True, axis_index_groups=kv_groups)  10.3 us
    ppermute x3, starting transfers between devices, body(): lax.ppermute(bundles[k], 'head', [(i, i ^ 2 * k) for i in range(head_coun...  9.26 us
    all_to_all x1, waiting for transfers between devices, body(): lax.all_to_all(kv, 'head', 0, 0, tiled=True, axis_index_groups=spread_gro...  9.05 us
    all_to_all x1, waiting for transfers between devices, body(): foreign = lax.all_to_all(asked, 'ctx', 0, 0, tiled=True)  6.29 us
  transfers between devices with their start and end apart: 7, of which 4 were waited for; matrix products, arithmetic and copies ran while one was open for 0% of the time, Pallas kernels for 3%

profile of v2, /device:TPU:1, one launch (start us, length us, event | category | flops | bytes accessed | tf_op | source)
XLA Modules:
  0.0 112.1 jit_solution(9665810096341282813)
XLA Ops:
  0.0 0.0 copy-start.3
  0.0 0.9 copy.6
  0.9 0.0 copy-done.3
  0.9 0.7 pad_maximum_fusion
  1.6 0.0 copy-start.1
  1.6 0.0 copy-start.2
  1.6 10.3 %all-to-all-start = ((bf16[16,2,16,128]{3,2,1,0:T(8,128)(2,1)}), bf16[16,2,16,128]{3,2,1,0:T(8,128)(2,1)S(1)}, u32[]{:S(2)}, u32[]{:S(2)}) async-start(bf16[16,2,16,128]{3,2,1,0:T(8,128)(2,1)} %bitcast.7), calls=%async_computation | async-start | bytes 262144 | tf_op jit(solution)/shard_map/all_to_all | solution.py:190
  11.9 0.0 copy-start
  12.0 0.0 copy-done.1
  12.0 0.0 copy-done.2
  12.0 0.8 shard_map.55.range_ref
  12.8 9.1 %all-to-all-done.own_ref = bf16[16,2,16,128]{3,2,1,0:T(8,128)(2,1)S(1)} async-done(((bf16[16,2,16,128]{3,2,1,0:T(8,128)(2,1)}), bf16[16,2,16,128]{3,2,1,0:T(8,128)(2,1)S(1)}, u32[]{:S(2)}, u32[]{:S(2)}) %all-to-all-start) | async-done | bytes 131104 | tf_op jit(solution)/shard_map/all_to_all | solution.py:190
  21.8 1.4 %shard_map.56 = bf16[32,2,16,128]{3,2,1,0:T(8,128)(2,1)} custom-call(s32[32]{0:T(128)S(1)} %copy-done.2, s32[2,256]{1,0:T(2,128)S(1)} %shard_map.55.range_ref, bf16[16,2,16,128]{3,2,1,0:T(8,128)(2,1)S(1)} %all-to-all-done.own_ref), custom_call_target="tpu_custom_call" | custom-call | tf_op jit(solution)/shard_map/pallas_call | solution.py:200
  23.2 18.6 %all-to-all-start.1 = ((bf16[32,2,16,128]{3,2,1,0:T(8,128)(2,1)}), bf16[32,2,16,128]{3,2,1,0:T(8,128)(2,1)S(1)}, u32[]{:S(2)}, u32[]{:S(2)}) async-start(bf16[32,2,16,128]{3,2,1,0:T(8,128)(2,1)} %shard_map.56), calls=%async_computation.1 | async-start | bytes 524288 | tf_op jit(solution)/shard_map/all_to_all | solution.py:207
  41.8 0.0 copy-done
  41.8 3.9 %collective-permute-start = (bf16[4,256,128]{2,1,0:T(8,128)(2,1)S(1)}, bf16[4,256,128]{2,1,0:T(8,128)(2,1)S(1)}, u32[]{:S(2)}, u32[]{:S(2)}) collective-permute-start(bf16[4,256,128]{2,1,0:T(8,128)(2,1)S(1)} %dynamic-slice_bitcast_fusion), channel_id=1, source_target_pairs={{0,1},{1,0},{2,3},{3,2},{4,5},{5,4},{6,7},{7,6},{8,9},{9,8},{10,11... | collective-permute-start | bytes 786440 | tf_op jit(solution)/shard_map/ppermute | solution.py:213
  45.8 2.4 %shard_map.58.source_ref = s32[64]{0:T(128)S(1)} custom-call(s32[1]{0:T(128)} %bitcast.me_ref, s32[32]{0:T(128)S(1)} %copy-done.2, s32[4,256]{1,0:T(4,128)S(1)} %bitcast.18), custom_call_target="tpu_custom_call" | custom-call | tf_op jit(solution)/shard_map/pallas_call | solution.py:222
  48.2 0.0 collective-permute-done.sibling_ref
  48.3 6.3 %all-to-all-done.1.foreign_ref = bf16[32,2,16,128]{3,2,1,0:T(8,128)(2,1)S(1)} async-done(((bf16[32,2,16,128]{3,2,1,0:T(8,128)(2,1)}), bf16[32,2,16,128]{3,2,1,0:T(8,128)(2,1)S(1)}, u32[]{:S(2)}, u32[]{:S(2)}) %all-to-all-start.1) | async-done | bytes 262176 | tf_op jit(solution)/shard_map/all_to_all | solution.py:207
  54.6 1.6 %shard_map.59 = bf16[64,2,16,128]{3,2,1,0:T(8,128)(2,1)} custom-call(s32[64]{0:T(128)S(1)} %shard_map.58.source_ref, bf16[16,2,16,128]{3,2,1,0:T(8,128)(2,1)S(1)} %all-to-all-done.own_ref, bf16[32,2,16,128]{3,2,1,0:T(8,128)(2,1)S(1)} %all-to-all-done.1.foreign_ref), custom_call_target="tpu_custom_call" | custom-call | tf_op jit(solution)/shard_map/pallas_call | solution.py:242
  56.2 10.3 %all-to-all-start.2 = ((bf16[64,2,16,128]{3,2,1,0:T(8,128)(2,1)}), bf16[64,2,16,128]{3,2,1,0:T(8,128)(2,1)S(1)}, u32[]{:S(2)}, u32[]{:S(2)}) async-start(bf16[64,2,16,128]{3,2,1,0:T(8,128)(2,1)} %shard_map.59), calls=%async_computation.2 | async-start | bytes 1048576 | tf_op jit(solution)/shard_map/all_to_all | solution.py:249
  66.4 3.3 %collective-permute-start.1 = (bf16[2,256,128]{2,1,0:T(8,128)(2,1)S(1)}, bf16[2,256,128]{2,1,0:T(8,128)(2,1)S(1)}, u32[]{:S(2)}, u32[]{:S(2)}) collective-permute-start(bf16[2,256,128]{2,1,0:T(8,128)(2,1)S(1)} %get-tuple-element.14), channel_id=1, source_target_pairs={{0,2},{1,3},{2,0},{3,1},{4,6},{5,7},{6,4},{7,5},{8,10},{9,11},{10,... | collective-permute-start | bytes 393224 | tf_op jit(solution)/shard_map/ppermute | solution.py:236
  69.7 4.0 %collective-permute-start.2 = (bf16[2,256,128]{2,1,0:T(8,128)(2,1)S(1)}, bf16[2,256,128]{2,1,0:T(8,128)(2,1)S(1)}, u32[]{:S(2)}, u32[]{:S(2)}) collective-permute-start(bf16[2,256,128]{2,1,0:T(8,128)(2,1)S(1)} %get-tuple-element.15), channel_id=1, source_target_pairs={{0,4},{1,5},{2,6},{3,7},{4,0},{5,1},{6,2},{7,3},{8,12},{9,13},{10,... | collective-permute-start | bytes 393224 | tf_op jit(solution)/shard_map/ppermute | solution.py:236
  73.7 2.0 %collective-permute-start.3 = (bf16[2,256,128]{2,1,0:T(8,128)(2,1)S(1)}, bf16[2,256,128]{2,1,0:T(8,128)(2,1)S(1)}, u32[]{:S(2)}, u32[]{:S(2)}) collective-permute-start(bf16[2,256,128]{2,1,0:T(8,128)(2,1)S(1)} %get-tuple-element.16), channel_id=1, source_target_pairs={{0,6},{1,7},{2,4},{3,5},{4,2},{5,3},{6,0},{7,1},{8,14},{9,15},{10,... | collective-permute-start | bytes 393224 | tf_op jit(solution)/shard_map/ppermute | solution.py:236
  75.7 2.6 %collective-permute-done.1.refs_1_ = bf16[2,256,128]{2,1,0:T(8,128)(2,1)S(1)} collective-permute-done((bf16[2,256,128]{2,1,0:T(8,128)(2,1)S(1)}, bf16[2,256,128]{2,1,0:T(8,128)(2,1)S(1)}, u32[]{:S(2)}, u32[]{:S(2)}) %collective-permute-start.1) | collective-permute-done | bytes 131104 | tf_op jit(solution)/shard_map/ppermute | solution.py:236
  78.3 11.1 %collective-permute-done.2.refs_2_ = bf16[2,256,128]{2,1,0:T(8,128)(2,1)S(1)} collective-permute-done((bf16[2,256,128]{2,1,0:T(8,128)(2,1)S(1)}, bf16[2,256,128]{2,1,0:T(8,128)(2,1)S(1)}, u32[]{:S(2)}, u32[]{:S(2)}) %collective-permute-start.2) | collective-permute-done | bytes 131104 | tf_op jit(solution)/shard_map/ppermute | solution.py:236
  89.4 0.0 collective-permute-done.3.refs_3_
  89.4 0.0 all-to-all-done.2
  89.4 2.3 %shard_map.60 = bf16[8,256,128]{2,1,0:T(8,128)(2,1)S(1)} custom-call(s32[1]{0:T(128)} %bitcast.me_ref, s32[1]{0:T(128)} %bitcast.1.rank_ref, s32[32]{0:T(128)S(1)} %copy-done.2, bf16[2,256,128]{2,1,0:T(8,128)(2,1)S(1)} %get-tuple-element.13.refs_0_, bf16[2,256,128]{2,1,0:T(8,128)(2,1)S(1)} %collective-permute-done.1.refs_1_, ...), custom_call_target="tpu_custom_call" | custom-call | tf_op jit(solution)/shard_map/pallas_call | solution.py:252
  91.7 19.6 %all_to_all.20 = bf16[8,256,128]{2,1,0:T(8,128)(2,1)S(1)} all-to-all(bf16[8,256,128]{2,1,0:T(8,128)(2,1)S(1)} %shard_map.60), channel_id=1, replica_groups={{0,1,2,3,4,5,6,7},{8,9,10,11,12,13,14,15},{16,17,18,19,20,21,22,23},{24..., dimensions={0} | all-to-all | bytes 1048576 | tf_op jit(solution)/shard_map/all_to_all | solution.py:261
  111.3 0.8 copy.12
  (3 shorter events, 0.1 us)
Async XLA Ops:
  0.0 0.9 copy-start.3
  1.6 10.4 %copy-start.1 = (s32[256,4]{0,1:T(4,128)S(1)}, s32[256,4]{0,1:T(4,128)}, u32[]{:S(2)}) copy-start(s32[256,4]{0,1:T(4,128)} %param.8) | copy-start | bytes 12292
  1.6 10.4 %copy-start.2 = (s32[32]{0:T(128)S(1)}, s32[32]{0:T(128)}, u32[]{:S(2)}) copy-start(s32[32]{0:T(128)} %span_ref.6) | copy-start | bytes 388
  1.6 20.2 %all-to-all-start = ((bf16[16,2,16,128]{3,2,1,0:T(8,128)(2,1)}), bf16[16,2,16,128]{3,2,1,0:T(8,128)(2,1)S(1)}, u32[]{:S(2)}, u32[]{:S(2)}) async-start(bf16[16,2,16,128]{3,2,1,0:T(8,128)(2,1)} %bitcast.7), calls=%async_computation | async-start | bytes 262144 | tf_op jit(solution)/shard_map/all_to_all | solution.py:190
  11.9 29.9 %copy-start = (bf16[2048,1,128]{2,0,1:T(8,128)(2,1)S(1)}, bf16[2048,1,128]{2,0,1:T(8,128)(2,1)}, u32[]{:S(2)}) copy-start(bf16[2048,1,128]{2,0,1:T(8,128)(2,1)} %param.5) | copy-start | bytes 1572868
  23.2 31.4 %all-to-all-start.1 = ((bf16[32,2,16,128]{3,2,1,0:T(8,128)(2,1)}), bf16[32,2,16,128]{3,2,1,0:T(8,128)(2,1)S(1)}, u32[]{:S(2)}, u32[]{:S(2)}) async-start(bf16[32,2,16,128]{3,2,1,0:T(8,128)(2,1)} %shard_map.56), calls=%async_computation.1 | async-start | bytes 524288 | tf_op jit(solution)/shard_map/all_to_all | solution.py:207
  41.8 6.4 %collective-permute-start = (bf16[4,256,128]{2,1,0:T(8,128)(2,1)S(1)}, bf16[4,256,128]{2,1,0:T(8,128)(2,1)S(1)}, u32[]{:S(2)}, u32[]{:S(2)}) collective-permute-start(bf16[4,256,128]{2,1,0:T(8,128)(2,1)S(1)} %dynamic-slice_bitcast_fusion), channel_id=1, source_target_pairs={{0,1},{1,0},{2,3},{3,2},{4,5},{5,4},{6,7},{7,6},{8,9},{9,8},{10,11... | collective-permute-start | bytes 786440 | tf_op jit(solution)/shard_map/ppermute | solution.py:213
  56.2 33.2 %all-to-all-start.2 = ((bf16[64,2,16,128]{3,2,1,0:T(8,128)(2,1)}), bf16[64,2,16,128]{3,2,1,0:T(8,128)(2,1)S(1)}, u32[]{:S(2)}, u32[]{:S(2)}) async-start(bf16[64,2,16,128]{3,2,1,0:T(8,128)(2,1)} %shard_map.59), calls=%async_computation.2 | async-start | bytes 1048576 | tf_op jit(solution)/shard_map/all_to_all | solution.py:249
  66.4 11.8 %collective-permute-start.1 = (bf16[2,256,128]{2,1,0:T(8,128)(2,1)S(1)}, bf16[2,256,128]{2,1,0:T(8,128)(2,1)S(1)}, u32[]{:S(2)}, u32[]{:S(2)}) collective-permute-start(bf16[2,256,128]{2,1,0:T(8,128)(2,1)S(1)} %get-tuple-element.14), channel_id=1, source_target_pairs={{0,2},{1,3},{2,0},{3,1},{4,6},{5,7},{6,4},{7,5},{8,10},{9,11},{10,... | collective-permute-start | bytes 393224 | tf_op jit(solution)/shard_map/ppermute | solution.py:236
  69.7 19.6 %collective-permute-start.2 = (bf16[2,256,128]{2,1,0:T(8,128)(2,1)S(1)}, bf16[2,256,128]{2,1,0:T(8,128)(2,1)S(1)}, u32[]{:S(2)}, u32[]{:S(2)}) collective-permute-start(bf16[2,256,128]{2,1,0:T(8,128)(2,1)S(1)} %get-tuple-element.15), channel_id=1, source_target_pairs={{0,4},{1,5},{2,6},{3,7},{4,0},{5,1},{6,2},{7,3},{8,12},{9,13},{10,... | collective-permute-start | bytes 393224 | tf_op jit(solution)/shard_map/ppermute | solution.py:236
  73.7 15.6 %collective-permute-start.3 = (bf16[2,256,128]{2,1,0:T(8,128)(2,1)S(1)}, bf16[2,256,128]{2,1,0:T(8,128)(2,1)S(1)}, u32[]{:S(2)}, u32[]{:S(2)}) collective-permute-start(bf16[2,256,128]{2,1,0:T(8,128)(2,1)S(1)} %get-tuple-element.16), channel_id=1, source_target_pairs={{0,6},{1,7},{2,4},{3,5},{4,2},{5,3},{6,0},{7,1},{8,14},{9,15},{10,... | collective-permute-start | bytes 393224 | tf_op jit(solution)/shard_map/ppermute | solution.py:236

commit v3 on v2

--- a/solution.py
+++ b/solution.py
@@ -181,34 +181,8 @@
     piece = (2, piece_rows, width)
     listed = key_blocks.T
 
-    spread_groups = [
-        [shards_per_block * j + q for j in range(block_count)] for q in range(shards_per_block)
-    ]
-    kv = jnp.stack([keys, values])
-    kv = kv.reshape(2, halves, piece_rows, kv_heads, width).transpose(3, 1, 0, 2, 4)
-    kv = kv.reshape((block_count,) + piece)
-    own = lax.all_to_all(kv, "head", 0, 0, tiled=True, axis_index_groups=spread_groups)
-
-    ranges = pl.pallas_call(
-        functools.partial(asked_range, per_span),
-        out_shape=jax.ShapeDtypeStruct((2, key_blocks.shape[0]), i32),
-        in_specs=[SMEM, SMEM, VMEM],
-        out_specs=VMEM,
-        compiler_params=small(),
-    )(me[None], span_order, listed)
-
-    asked = pl.pallas_call(
-        functools.partial(pick_asked, per_span),
-        out_shape=jax.ShapeDtypeStruct((ctx_count * CAP,) + piece, bf16),
-        in_specs=[SMEM, SMEM, VMEM],
-        out_specs=VMEM,
-        compiler_params=small(),
-    )(span_order, ranges, own)
-    foreign = lax.all_to_all(asked, "ctx", 0, 0, tiled=True)
-
     core = lax.rem(rank, 2)
     query_parts = queries.reshape(chips, 2, rows_device // group, width)
-    query_parts, span_after, _ = lax.optimization_barrier((query_parts, span_order, asked))
     crossing = lax.dynamic_index_in_dim(query_parts, 1 - core, 1, keepdims=False)
     sibling = lax.ppermute(crossing, "head", [(i, i ^ 1) for i in range(head_count)])
     part = jax.ShapeDtypeStruct((2, rows_device // group, width), bf16)
@@ -219,6 +193,38 @@
         out_specs=(VMEM,) * chips,
         compiler_params=small(8),
     )(rank[None], query_parts.reshape(group, rows_device // group, width), sibling)
+
+    spread_groups = [
+        [shards_per_block * j + q for j in range(block_count)] for q in range(shards_per_block)
+    ]
+    kv = jnp.stack([keys, values])
+    kv = kv.reshape(2, halves, piece_rows, kv_heads, width).transpose(3, 1, 0, 2, 4)
+    kv = kv.reshape((block_count,) + piece)
+    kv, bundles = lax.optimization_barrier((kv, bundles))
+    own = lax.all_to_all(kv, "head", 0, 0, tiled=True, axis_index_groups=spread_groups)
+
+    ranges = pl.pallas_call(
+        functools.partial(asked_range, per_span),
+        out_shape=jax.ShapeDtypeStruct((2, key_blocks.shape[0]), i32),
+        in_specs=[SMEM, SMEM, VMEM],
+        out_specs=VMEM,
+        compiler_params=small(),
+    )(me[None], span_order, listed)
+
+    asked = pl.pallas_call(
+        functools.partial(pick_asked, per_span),
+        out_shape=jax.ShapeDtypeStruct((ctx_count * CAP,) + piece, bf16),
+        in_specs=[SMEM, SMEM, VMEM],
+        out_specs=VMEM,
+        compiler_params=small(),
+    )(span_order, ranges, own)
+    foreign = lax.all_to_all(asked, "ctx", 0, 0, tiled=True)
+
+    *bundles, span_after, _ = lax.optimization_barrier((*bundles, span_order, asked))
+    query_here = [bundles[0]] + [
+        lax.ppermute(bundles[k], "head", [(i, i ^ (2 * k)) for i in range(head_count)])
+        for k in range(1, chips)
+    ]
     source = pl.pallas_call(
         functools.partial(find_sources, per_span),
         out_shape=jax.ShapeDtypeStruct((block_count * slot_count,), i32),
@@ -232,13 +238,9 @@
         ],
         compiler_params=small(),
     )(me[None], span_after, listed)
-    query_here = [bundles[0]] + [
-        lax.ppermute(bundles[k], "head", [(i, i ^ (2 * k)) for i in range(head_count)])
-        for k in range(1, chips)
-    ]
-    source, _ = lax.optimization_barrier((source, bundles))
 
     kv_groups = [[g * group + i for i in range(group)] for g in range(kv_heads)]
+    source, foreign, query_here = lax.optimization_barrier((source, foreign, query_here))
     pairs = pl.pallas_call(
         pick_pairs,
         out_shape=jax.ShapeDtypeStruct((block_count * slot_count,) + piece, bf16),

time: 113 us -> 105 us (0.929)
  blocking collectives: 19.6 us -> 38.7 us
  waiting for transfers between devices: 29 us -> 12.5 us
  starting transfers between devices: 52.4 us -> 40.9 us
  local copies, waits for them, and re-layouts: 1.73 us -> 3.35 us
    all_to_all x0 -> x1, blocking collectives: none -> 20.9 us  [body(): lax.all_to_all(pairs, 'head', 0, 0, tiled=True, axis_index_groups=kv_groups)]
    ppermute x1, starting transfers between devices: 3.94 us -> 16.1 us  [body(): lax.ppermute(crossing, 'head', [(i, i ^ 1) for i in range(head_count)])]
    all_to_all x1 -> x0, starting transfers between devices: 10.3 us -> none  [body(): lax.all_to_all(pairs, 'head', 0, 0, tiled=True, axis_index_groups=kv_groups)]
    ppermute x3, waiting for transfers between devices: 13.7 us -> 3.8 us  [body(): lax.ppermute(bundles[k], 'head', [(i, i ^ 2 * k) for i in range(head_coun...]
    all_to_all x1, starting transfers between devices: 10.3 us -> 3.52 us  [body(): lax.all_to_all(kv, 'head', 0, 0, tiled=True, axis_index_groups=spread_gro...]
    all_to_all x1, starting transfers between devices: 18.6 us -> 12.1 us  [body(): foreign = lax.all_to_all(asked, 'ctx', 0, 0, tiled=True)]
    all_to_all x1, waiting for transfers between devices: 6.29 us -> 0.01 us  [body(): foreign = lax.all_to_all(asked, 'ctx', 0, 0, tiled=True)]
    all_to_all x1, blocking collectives: 19.6 us -> 17.8 us  [body(): lax.all_to_all(done, 'head', 0, 0, tiled=True, axis_index_groups=kv_groups)]
  transfers between devices with their start and end apart: 7 -> 6, of which waited for: 4 -> 2; matrix products, arithmetic and copies ran while one was open for 0% -> 1% of each run, Pallas kernels for 3% -> 3%
where the time goes in v3:
time: 105 us; the launch traced here: 104 us
  starting transfers between devices  40.9 us (39%)
  blocking collectives  38.7 us (37%)
  waiting for transfers between devices  12.5 us (12%)
  Pallas kernels  7.72 us (7%)
  local copies, waits for them, and re-layouts  3.35 us (3%)
    all_to_all x1, blocking collectives, body(): lax.all_to_all(pairs, 'head', 0, 0, tiled=True, axis_index_groups=kv_groups)  20.9 us
    all_to_all x1, blocking collectives, body(): lax.all_to_all(done, 'head', 0, 0, tiled=True, axis_index_groups=kv_groups)  17.8 us
    ppermute x1, starting transfers between devices, body(): lax.ppermute(crossing, 'head', [(i, i ^ 1) for i in range(head_count)])  16.1 us
    all_to_all x1, starting transfers between devices, body(): foreign = lax.all_to_all(asked, 'ctx', 0, 0, tiled=True)  12.1 us
    ppermute x3, starting transfers between devices, body(): lax.ppermute(bundles[k], 'head', [(i, i ^ 2 * k) for i in range(head_coun...  9.27 us
    all_to_all x1, waiting for transfers between devices, body(): lax.all_to_all(kv, 'head', 0, 0, tiled=True, axis_index_groups=spread_gro...  8.7 us
    ppermute x3, waiting for transfers between devices, body(): lax.ppermute(bundles[k], 'head', [(i, i ^ 2 * k) for i in range(head_coun...  3.8 us
    all_to_all x1, starting transfers between devices, body(): lax.all_to_all(kv, 'head', 0, 0, tiled=True, axis_index_groups=spread_gro...  3.52 us
  transfers between devices with their start and end apart: 6, of which 2 were waited for; matrix products, arithmetic and copies ran while one was open for 1% of the time, Pallas kernels for 3%

profile of v3, /device:TPU:1, one launch (start us, length us, event | category | flops | bytes accessed | tf_op | source)
XLA Modules:
  0.0 104.0 jit_solution(1466751998290899554)
XLA Ops:
  0.0 0.0 copy-start.3
  0.0 0.0 copy-start
  0.0 1.0 dynamic-slice_bitcast_fusion
  1.0 16.1 %collective-permute-start = (bf16[4,256,128]{2,1,0:T(8,128)(2,1)S(1)}, bf16[4,256,128]{2,1,0:T(8,128)(2,1)S(1)}, u32[]{:S(2)}, u32[]{:S(2)}) collective-permute-start(bf16[4,256,128]{2,1,0:T(8,128)(2,1)S(1)} %dynamic-slice_bitcast_fusion), channel_id=1, source_target_pairs={{0,1},{1,0},{2,3},{3,2},{4,5},{5,4},{6,7},{7,6},{8,9},{9,8},{10,11... | collective-permute-start | bytes 786440 | tf_op jit(solution)/shard_map/ppermute | solution.py:187
  17.1 0.0 copy-done.3
  17.1 0.0 copy-start.4
  17.2 0.8 copy-done.4
  18.0 0.7 pad_maximum_fusion
  18.7 0.0 collective-permute-done.sibling_ref
  18.7 0.0 copy-done
  18.7 3.5 %all-to-all-start = ((bf16[16,2,16,128]{3,2,1,0:T(8,128)(2,1)}), bf16[16,2,16,128]{3,2,1,0:T(8,128)(2,1)S(1)}, u32[]{:S(2)}, u32[]{:S(2)}) async-start(bf16[16,2,16,128]{3,2,1,0:T(8,128)(2,1)} %bitcast.5), calls=%async_computation | async-start | bytes 262144 | tf_op jit(solution)/shard_map/all_to_all | solution.py:204
  22.2 0.0 copy-start.1
  22.3 0.0 copy-start.2
  22.3 0.7 copy-done.1
  22.9 0.0 copy-done.2
  22.9 0.8 shard_map.56.range_ref
  23.7 8.7 %all-to-all-done.own_ref = bf16[16,2,16,128]{3,2,1,0:T(8,128)(2,1)S(1)} async-done(((bf16[16,2,16,128]{3,2,1,0:T(8,128)(2,1)}), bf16[16,2,16,128]{3,2,1,0:T(8,128)(2,1)S(1)}, u32[]{:S(2)}, u32[]{:S(2)}) %all-to-all-start) | async-done | bytes 131104 | tf_op jit(solution)/shard_map/all_to_all | solution.py:204
  32.4 1.4 %shard_map.57 = bf16[32,2,16,128]{3,2,1,0:T(8,128)(2,1)} custom-call(s32[32]{0:T(128)S(1)} %copy-done.2, s32[2,256]{1,0:T(2,128)S(1)} %shard_map.56.range_ref, bf16[16,2,16,128]{3,2,1,0:T(8,128)(2,1)S(1)} %all-to-all-done.own_ref), custom_call_target="tpu_custom_call" | custom-call | tf_op jit(solution)/shard_map/pallas_call | solution.py:214
  33.8 12.1 %all-to-all-start.1 = ((bf16[32,2,16,128]{3,2,1,0:T(8,128)(2,1)}), bf16[32,2,16,128]{3,2,1,0:T(8,128)(2,1)S(1)}, u32[]{:S(2)}, u32[]{:S(2)}) async-start(bf16[32,2,16,128]{3,2,1,0:T(8,128)(2,1)} %shard_map.57), calls=%async_computation.1 | async-start | bytes 524288 | tf_op jit(solution)/shard_map/all_to_all | solution.py:221
  45.9 2.5 %collective-permute-start.1 = (bf16[2,256,128]{2,1,0:T(8,128)(2,1)S(1)}, bf16[2,256,128]{2,1,0:T(8,128)(2,1)S(1)}, u32[]{:S(2)}, u32[]{:S(2)}) collective-permute-start(bf16[2,256,128]{2,1,0:T(8,128)(2,1)S(1)} %get-tuple-element.36), channel_id=1, source_target_pairs={{0,2},{1,3},{2,0},{3,1},{4,6},{5,7},{6,4},{7,5},{8,10},{9,11},{10,... | collective-permute-start | bytes 393224 | tf_op jit(solution)/shard_map/ppermute | solution.py:225
  48.4 2.5 %collective-permute-start.2 = (bf16[2,256,128]{2,1,0:T(8,128)(2,1)S(1)}, bf16[2,256,128]{2,1,0:T(8,128)(2,1)S(1)}, u32[]{:S(2)}, u32[]{:S(2)}) collective-permute-start(bf16[2,256,128]{2,1,0:T(8,128)(2,1)S(1)} %get-tuple-element.37), channel_id=1, source_target_pairs={{0,4},{1,5},{2,6},{3,7},{4,0},{5,1},{6,2},{7,3},{8,12},{9,13},{10,... | collective-permute-start | bytes 393224 | tf_op jit(solution)/shard_map/ppermute | solution.py:225
  50.9 4.3 %collective-permute-start.3 = (bf16[2,256,128]{2,1,0:T(8,128)(2,1)S(1)}, bf16[2,256,128]{2,1,0:T(8,128)(2,1)S(1)}, u32[]{:S(2)}, u32[]{:S(2)}) collective-permute-start(bf16[2,256,128]{2,1,0:T(8,128)(2,1)S(1)} %get-tuple-element.38), channel_id=1, source_target_pairs={{0,6},{1,7},{2,4},{3,5},{4,2},{5,3},{6,0},{7,1},{8,14},{9,15},{10,... | collective-permute-start | bytes 393224 | tf_op jit(solution)/shard_map/ppermute | solution.py:225
  55.2 2.4 %shard_map.58.source_ref = s32[64]{0:T(128)S(1)} custom-call(s32[1]{0:T(128)} %bitcast.me_ref, s32[32]{0:T(128)S(1)} %copy-done.2, s32[4,256]{1,0:T(4,128)S(1)} %bitcast.20), custom_call_target="tpu_custom_call" | custom-call | tf_op jit(solution)/shard_map/pallas_call | solution.py:228
  57.6 0.0 collective-permute-done.1.refs_1_
  57.6 3.8 %collective-permute-done.2.refs_2_ = bf16[2,256,128]{2,1,0:T(8,128)(2,1)S(1)} collective-permute-done((bf16[2,256,128]{2,1,0:T(8,128)(2,1)S(1)}, bf16[2,256,128]{2,1,0:T(8,128)(2,1)S(1)}, u32[]{:S(2)}, u32[]{:S(2)}) %collective-permute-start.2) | collective-permute-done | bytes 131104 | tf_op jit(solution)/shard_map/ppermute | solution.py:225
  61.4 0.0 collective-permute-done.3.refs_3_
  61.4 0.0 all-to-all-done.1.foreign_ref
  61.4 0.8 shard_map.59
  62.2 20.9 %all_to_all.20 = bf16[64,2,16,128]{3,2,1,0:T(8,128)(2,1)S(1)} all-to-all(bf16[64,2,16,128]{3,2,1,0:T(8,128)(2,1)S(1)} %shard_map.59), channel_id=1, replica_groups={{0,1,2,3,4,5,6,7},{8,9,10,11,12,13,14,15},{16,17,18,19,20,21,22,23},{24..., dimensions={0} | all-to-all | bytes 1048576 | tf_op jit(solution)/shard_map/all_to_all | solution.py:251
  83.2 2.3 %shard_map.60 = bf16[8,256,128]{2,1,0:T(8,128)(2,1)S(1)} custom-call(s32[1]{0:T(128)} %bitcast.me_ref, s32[1]{0:T(128)} %bitcast.1.rank_ref, s32[32]{0:T(128)S(1)} %copy-done.2, bf16[2,256,128]{2,1,0:T(8,128)(2,1)S(1)} %get-tuple-element.39.refs_0_, bf16[2,256,128]{2,1,0:T(8,128)(2,1)S(1)} %collective-permute-done.1.refs_1_, ...), custom_call_target="tpu_custom_call" | custom-call | tf_op jit(solution)/shard_map/pallas_call | solution.py:254
  85.5 17.8 %all_to_all.21 = bf16[8,256,128]{2,1,0:T(8,128)(2,1)S(1)} all-to-all(bf16[8,256,128]{2,1,0:T(8,128)(2,1)S(1)} %shard_map.60), channel_id=1, replica_groups={{0,1,2,3,4,5,6,7},{8,9,10,11,12,13,14,15},{16,17,18,19,20,21,22,23},{24..., dimensions={0} | all-to-all | bytes 1048576 | tf_op jit(solution)/shard_map/all_to_all | solution.py:263
  103.2 0.8 copy.11
  (3 shorter events, 0.1 us)
Async XLA Ops:
  0.0 17.1 %copy-start.3 = (bf16[32,8,128]{2,1,0:T(8,128)(2,1)S(1)}, bf16[32,8,128]{2,1,0:T(8,128)(2,1)}, u32[]{:S(2)}) copy-start(bf16[32,8,128]{2,1,0:T(8,128)(2,1)} %param.6) | copy-start | bytes 196612
  0.0 18.7 %copy-start = (bf16[2048,1,128]{2,0,1:T(8,128)(2,1)S(1)}, bf16[2048,1,128]{2,0,1:T(8,128)(2,1)}, u32[]{:S(2)}) copy-start(bf16[2048,1,128]{2,0,1:T(8,128)(2,1)} %param.5) | copy-start | bytes 1572868
  1.0 17.6 %collective-permute-start = (bf16[4,256,128]{2,1,0:T(8,128)(2,1)S(1)}, bf16[4,256,128]{2,1,0:T(8,128)(2,1)S(1)}, u32[]{:S(2)}, u32[]{:S(2)}) collective-permute-start(bf16[4,256,128]{2,1,0:T(8,128)(2,1)S(1)} %dynamic-slice_bitcast_fusion), channel_id=1, source_target_pairs={{0,1},{1,0},{2,3},{3,2},{4,5},{5,4},{6,7},{7,6},{8,9},{9,8},{10,11... | collective-permute-start | bytes 786440 | tf_op jit(solution)/shard_map/ppermute | solution.py:187
  17.1 0.8 copy-start.4
  18.7 13.7 %all-to-all-start = ((bf16[16,2,16,128]{3,2,1,0:T(8,128)(2,1)}), bf16[16,2,16,128]{3,2,1,0:T(8,128)(2,1)S(1)}, u32[]{:S(2)}, u32[]{:S(2)}) async-start(bf16[16,2,16,128]{3,2,1,0:T(8,128)(2,1)} %bitcast.5), calls=%async_computation | async-start | bytes 262144 | tf_op jit(solution)/shard_map/all_to_all | solution.py:204
  22.2 0.7 copy-start.1
  22.3 0.7 copy-start.2
  33.8 27.6 %all-to-all-start.1 = ((bf16[32,2,16,128]{3,2,1,0:T(8,128)(2,1)}), bf16[32,2,16,128]{3,2,1,0:T(8,128)(2,1)S(1)}, u32[]{:S(2)}, u32[]{:S(2)}) async-start(bf16[32,2,16,128]{3,2,1,0:T(8,128)(2,1)} %shard_map.57), calls=%async_computation.1 | async-start | bytes 524288 | tf_op jit(solution)/shard_map/all_to_all | solution.py:221
  45.9 11.7 %collective-permute-start.1 = (bf16[2,256,128]{2,1,0:T(8,128)(2,1)S(1)}, bf16[2,256,128]{2,1,0:T(8,128)(2,1)S(1)}, u32[]{:S(2)}, u32[]{:S(2)}) collective-permute-start(bf16[2,256,128]{2,1,0:T(8,128)(2,1)S(1)} %get-tuple-element.36), channel_id=1, source_target_pairs={{0,2},{1,3},{2,0},{3,1},{4,6},{5,7},{6,4},{7,5},{8,10},{9,11},{10,... | collective-permute-start | bytes 393224 | tf_op jit(solution)/shard_map/ppermute | solution.py:225
  48.4 13.0 %collective-permute-start.2 = (bf16[2,256,128]{2,1,0:T(8,128)(2,1)S(1)}, bf16[2,256,128]{2,1,0:T(8,128)(2,1)S(1)}, u32[]{:S(2)}, u32[]{:S(2)}) collective-permute-start(bf16[2,256,128]{2,1,0:T(8,128)(2,1)S(1)} %get-tuple-element.37), channel_id=1, source_target_pairs={{0,4},{1,5},{2,6},{3,7},{4,0},{5,1},{6,2},{7,3},{8,12},{9,13},{10,... | collective-permute-start | bytes 393224 | tf_op jit(solution)/shard_map/ppermute | solution.py:225
  50.9 10.5 %collective-permute-start.3 = (bf16[2,256,128]{2,1,0:T(8,128)(2,1)S(1)}, bf16[2,256,128]{2,1,0:T(8,128)(2,1)S(1)}, u32[]{:S(2)}, u32[]{:S(2)}) collective-permute-start(bf16[2,256,128]{2,1,0:T(8,128)(2,1)S(1)} %get-tuple-element.38), channel_id=1, source_target_pairs={{0,6},{1,7},{2,4},{3,5},{4,2},{5,3},{6,0},{7,1},{8,14},{9,15},{10,... | collective-permute-start | bytes 393224 | tf_op jit(solution)/shard_map/ppermute | solution.py:225

commit v4 on v2

--- a/solution.py
+++ b/solution.py
@@ -19,17 +19,23 @@
     return pltpu.CompilerParams(vmem_limit_bytes=mib * 2**20)
 
 
-def asked_range(per_span, me_ref, span_ref, listed_ref, out_ref):
+def tables(per_span, me_ref, span_ref, listed_ref, out_ref):
     listed = listed_ref[...]
     slots, positions = listed.shape
-    first = span_ref[2 * me_ref[0]]
-    second = span_ref[2 * me_ref[0] + 1]
+    span_count = span_ref.shape[0]
+    blocks = 2 * per_span
+    me = me_ref[0]
+    first = span_ref[2 * me]
+    second = span_ref[2 * me + 1]
     slot = lax.broadcasted_iota(jnp.int32, listed.shape, 0)
     position = lax.broadcasted_iota(jnp.int32, listed.shape, 1)
+    used = slot <= position
     span = listed // per_span
-    mine = (slot <= position) & ((span == first) | (span == second))
-    block = listed % per_span + jnp.where(span == second, per_span, 0)
-    low = jnp.min(jnp.where(mine, block, 2 * per_span - 1), axis=0, keepdims=True)
+    rest = listed % per_span
+
+    mine = used & ((span == first) | (span == second))
+    block = rest + jnp.where(span == second, per_span, 0)
+    low = jnp.min(jnp.where(mine, block, blocks - 1), axis=0, keepdims=True)
     high = jnp.max(jnp.where(mine, block, 0), axis=0, keepdims=True)
     low = jnp.broadcast_to(low, (8, positions))
     high = jnp.broadcast_to(high, (8, positions))
@@ -41,65 +47,42 @@
     out_ref[0:1, :] = low[0:1]
     out_ref[1:2, :] = high[0:1]
 
-
-def pick_asked(per_span, span_ref, range_ref, own_ref, out_ref):
+    at = jnp.zeros_like(listed)
+    for s in range(span_count):
+        at = jnp.where(span == span_ref[s], s, at)
+    owner = at // 2
+    held = at % 2 * per_span + rest
+    asker = position // per_span
+    asking = used & ((asker == first) | (asker == second))
+    held_float = held.astype(jnp.float32)
+    lowest = jnp.zeros(listed.shape, jnp.float32)
+    for o in range(span_count // 2):
+        here = owner == o
+        least = jnp.where(here & asking, held_float, float(blocks))
+        least = jnp.min(jnp.min(least, axis=0, keepdims=True), axis=1, keepdims=True)
+        lowest = jnp.where(here, least, lowest)
+    foreign = blocks + CAP * owner + jnp.where(held_float > lowest, 1, 0)
+    out_ref[2:2 + slots, :] = jnp.where(owner == me, held, foreign)
+
+
+def pick_asked(per_span, span_ref, table_ref, own_ref, out_ref):
     for d in range(out_ref.shape[0] // CAP):
         a = span_ref[2 * d] * per_span
         b = span_ref[2 * d + 1] * per_span
-        out_ref[2 * d] = own_ref[jnp.minimum(range_ref[0, a], range_ref[0, b])]
-        out_ref[2 * d + 1] = own_ref[jnp.maximum(range_ref[1, a], range_ref[1, b])]
-
-
-def find_sources(per_span, me_ref, span_ref, listed_ref, out_ref, inverse, lowest, owners, helds):
-    me = me_ref[0]
-    slots = listed_ref.shape[0]
-    span_count = span_ref.shape[0]
-    blocks = 2 * per_span
-
-    def invert(s, carry):
-        inverse[span_ref[s]] = s
-        return carry
-
-    def reset(s, carry):
-        lowest[s] = blocks
-        return carry
-
-    lax.fori_loop(0, span_count, invert, 0, unroll=4)
-    lax.fori_loop(0, span_count // 2, reset, 0, unroll=4)
-
-    def scan(block, carry):
-        position = span_ref[2 * me + block // per_span] * per_span + block % per_span
-        for j in range(1, slots):
-            name = listed_ref[j, position]
-            at = inverse[name // per_span]
-            owner = at // 2
-            held = at % 2 * per_span + name % per_span
-            owners[block * slots + j] = owner
-            helds[block * slots + j] = held
-            lowest[owner] = jnp.minimum(lowest[owner], jnp.where(j <= position, held, blocks))
-        return carry
-
-    lax.fori_loop(0, blocks, scan, 0, unroll=2)
-
-    def place(block, carry):
-        out_ref[block * slots] = block
-        for j in range(1, slots):
-            owner = owners[block * slots + j]
-            held = helds[block * slots + j]
-            foreign = blocks + CAP * owner + jnp.where(held > lowest[owner], 1, 0)
-            out_ref[block * slots + j] = jnp.where(owner == me, held, foreign)
-        return carry
-
-    lax.fori_loop(0, blocks, place, 0, unroll=2)
-
-
-def pick_pairs(source_ref, own_ref, foreign_ref, out_ref):
+        out_ref[2 * d] = own_ref[jnp.minimum(table_ref[0, a], table_ref[0, b])]
+        out_ref[2 * d + 1] = own_ref[jnp.maximum(table_ref[1, a], table_ref[1, b])]
+
+
+def pick_pairs(per_span, me_ref, span_ref, table_ref, own_ref, foreign_ref, out_ref):
     own_count = own_ref.shape[0]
-    for i in range(out_ref.shape[0]):
-        at = source_ref[i]
-        mine = own_ref[jnp.minimum(at, own_count - 1)]
-        theirs = foreign_ref[jnp.maximum(at - own_count, 0)]
-        out_ref[i] = jnp.where(at < own_count, mine, theirs)
+    slots = out_ref.shape[0] // own_count
+    for block in range(own_count):
+        position = span_ref[2 * me_ref[0] + block // per_span] * per_span + block % per_span
+        for j in range(slots):
+            at = table_ref[2 + j, position]
+            mine = own_ref[jnp.minimum(at, own_count - 1)]
+            theirs = foreign_ref[jnp.maximum(at - own_count, 0)]
+            out_ref[block * slots + j] = jnp.where(at < own_count, mine, theirs)
 
 
 def bundle(rank_ref, query_ref, sibling_ref, *out_refs):
@@ -187,28 +170,20 @@
     kv = jnp.stack([keys, values])
     kv = kv.reshape(2, halves, piece_rows, kv_heads, width).transpose(3, 1, 0, 2, 4)
     kv = kv.reshape((block_count,) + piece)
+    kv, listed, queries = lax.optimization_barrier((kv, listed, queries))
     own = lax.all_to_all(kv, "head", 0, 0, tiled=True, axis_index_groups=spread_groups)
 
-    ranges = pl.pallas_call(
-        functools.partial(asked_range, per_span),
-        out_shape=jax.ShapeDtypeStruct((2, key_blocks.shape[0]), i32),
+    table = pl.pallas_call(
+        functools.partial(tables, per_span),
+        out_shape=jax.ShapeDtypeStruct((2 + slot_count, key_blocks.shape[0]), i32),
         in_specs=[SMEM, SMEM, VMEM],
         out_specs=VMEM,
         compiler_params=small(),
+        cost_estimate=pl.CostEstimate(flops=2 * 10**10, bytes_accessed=2**14, transcendentals=0),
     )(me[None], span_order, listed)
-
-    asked = pl.pallas_call(
-        functools.partial(pick_asked, per_span),
-        out_shape=jax.ShapeDtypeStruct((ctx_count * CAP,) + piece, bf16),
-        in_specs=[SMEM, SMEM, VMEM],
-        out_specs=VMEM,
-        compiler_params=small(),
-    )(span_order, ranges, own)
-    foreign = lax.all_to_all(asked, "ctx", 0, 0, tiled=True)
 
     core = lax.rem(rank, 2)
     query_parts = queries.reshape(chips, 2, rows_device // group, width)
-    query_parts, span_after, _ = lax.optimization_barrier((query_parts, span_order, asked))
     crossing = lax.dynamic_index_in_dim(query_parts, 1 - core, 1, keepdims=False)
     sibling = lax.ppermute(crossing, "head", [(i, i ^ 1) for i in range(head_count)])
     part = jax.ShapeDtypeStruct((2, rows_device // group, width), bf16)
@@ -219,33 +194,34 @@
         out_specs=(VMEM,) * chips,
         compiler_params=small(8),
     )(rank[None], query_parts.reshape(group, rows_device // group, width), sibling)
-    source = pl.pallas_call(
-        functools.partial(find_sources, per_span),
-        out_shape=jax.ShapeDtypeStruct((block_count * slot_count,), i32),
-        in_specs=[SMEM, SMEM, SMEM],
-        out_specs=SMEM,
-        scratch_shapes=[
-            pltpu.SMEM((2 * ctx_count,), i32),
-            pltpu.SMEM((ctx_count,), i32),
-            pltpu.SMEM((block_count * slot_count,), i32),
-            pltpu.SMEM((block_count * slot_count,), i32),
-        ],
+
+    own, table, bundles = lax.optimization_barrier((own, table, bundles))
+
+    asked = pl.pallas_call(
+        functools.partial(pick_asked, per_span),
+        out_shape=jax.ShapeDtypeStruct((ctx_count * CAP,) + piece, bf16),
+        in_specs=[SMEM, SMEM, VMEM],
+        out_specs=VMEM,
         compiler_params=small(),
-    )(me[None], span_after, listed)
-    query_here = [bundles[0]] + [
+    )(span_order, table, own)
+    foreign = lax.all_to_all(asked, "ctx", 0, 0, tiled=True)
+
+    *bundles, _ = lax.optimization_barrier((*bundles, asked))
+    near, *far = [
         lax.ppermute(bundles[k], "head", [(i, i ^ (2 * k)) for i in range(head_count)])
         for k in range(1, chips)
     ]
-    source, _ = lax.optimization_barrier((source, bundles))
 
     kv_groups = [[g * group + i for i in range(group)] for g in range(kv_heads)]
+    foreign, far = lax.optimization_barrier((foreign, far))
+    query_here = [bundles[0], near, *far]
     pairs = pl.pallas_call(
-        pick_pairs,
+        functools.partial(pick_pairs, per_span),
         out_shape=jax.ShapeDtypeStruct((block_count * slot_count,) + piece, bf16),
-        in_specs=[SMEM, VMEM, VMEM],
+        in_specs=[SMEM, SMEM, SMEM, VMEM, VMEM],
         out_specs=VMEM,
         compiler_params=small(),
-    )(source, own, foreign)
+    )(me[None], span_order, table, own, foreign)
     pairs = lax.all_to_all(pairs, "head", 0, 0, tiled=True, axis_index_groups=kv_groups)
     pairs = pairs.reshape((group, per_rank * slot_count) + piece)
 

time: 113 us -> 103 us (0.912)
  waiting for transfers between devices: 29 us -> 17.8 us
  starting transfers between devices: 52.4 us -> 56.8 us
  Pallas kernels: 8.51 us -> 6.41 us
  blocking collectives: 19.6 us -> 17.8 us
  local copies, waits for them, and re-layouts: 1.73 us -> 3.23 us
    all_to_all x1, waiting for transfers between devices: 9.05 us -> 0.01 us  [body(): lax.all_to_all(kv, 'head', 0, 0, tiled=True, axis_index_groups=spread_gro...]
    ppermute x1, starting transfers between devices: 3.94 us -> 9.36 us  [body(): lax.ppermute(crossing, 'head', [(i, i ^ 1) for i in range(head_count)])]
    all_to_all x1, waiting for transfers between devices: 6.29 us -> 1.41 us  [body(): foreign = lax.all_to_all(asked, 'ctx', 0, 0, tiled=True)]
    all_to_all x1, waiting for transfers between devices: 0.01 us -> 2.68 us  [body(): lax.all_to_all(pairs, 'head', 0, 0, tiled=True, axis_index_groups=kv_groups)]
    pallas_call x3 -> x2, Pallas kernels: 4.78 us -> 2.58 us  [the longest x1 1.78 us: body(): pl.pallas_call(functools.partial(pick_pairs, per_span), out_shape=jax.Sha...]
    all_to_all x1, blocking collectives: 19.6 us -> 17.8 us  [body(): lax.all_to_all(done, 'head', 0, 0, tiled=True, axis_index_groups=kv_groups)]
  transfers between devices with their start and end apart: 7 -> 7, of which waited for: 4 -> 4; matrix products, arithmetic and copies ran while one was open for 0% -> 0% of each run, Pallas kernels for 3% -> 1%
where the time goes in v4:
time: 103 us
  starting transfers between devices  56.8 us (55%)
  waiting for transfers between devices  17.8 us (17%)
  blocking collectives  17.8 us (17%)
  Pallas kernels  6.41 us (6%)
  local copies, waits for them, and re-layouts  3.23 us (3%)
    all_to_all x1, blocking collectives, body(): lax.all_to_all(done, 'head', 0, 0, tiled=True, axis_index_groups=kv_groups)  17.8 us
    all_to_all x1, starting transfers between devices, body(): foreign = lax.all_to_all(asked, 'ctx', 0, 0, tiled=True)  17.5 us
    ppermute x3, waiting for transfers between devices, body(): lax.ppermute(bundles[k], 'head', [(i, i ^ 2 * k) for i in range(head_coun...  13.7 us
    all_to_all x1, starting transfers between devices, body(): lax.all_to_all(pairs, 'head', 0, 0, tiled=True, axis_index_groups=kv_groups)  10.3 us
    all_to_all x1, starting transfers between devices, body(): lax.all_to_all(kv, 'head', 0, 0, tiled=True, axis_index_groups=spread_gro...  10.2 us
    ppermute x3, starting transfers between devices, body(): lax.ppermute(bundles[k], 'head', [(i, i ^ 2 * k) for i in range(head_coun...  9.47 us
    ppermute x1, starting transfers between devices, body(): lax.ppermute(crossing, 'head', [(i, i ^ 1) for i in range(head_count)])  9.36 us
    all_to_all x1, waiting for transfers between devices, body(): lax.all_to_all(pairs, 'head', 0, 0, tiled=True, axis_index_groups=kv_groups)  2.68 us
  transfers between devices with their start and end apart: 7, of which 4 were waited for; matrix products, arithmetic and copies ran while one was open for 0% of the time, Pallas kernels for 1%

profile of v4, /device:TPU:1, one launch (start us, length us, event | category | flops | bytes accessed | tf_op | source)
XLA Modules:
  0.0 102.8 jit_solution(13544262030619529534)
XLA Ops:
  0.0 0.0 copy-start
  0.0 0.9 copy.6
  0.9 0.9 copy.7
  1.8 0.7 pad_maximum_fusion
  2.4 10.2 %all-to-all-start = ((bf16[16,2,16,128]{3,2,1,0:T(8,128)(2,1)}), bf16[16,2,16,128]{3,2,1,0:T(8,128)(2,1)S(1)}, u32[]{:S(2)}, u32[]{:S(2)}) async-start(bf16[16,2,16,128]{3,2,1,0:T(8,128)(2,1)} %bitcast.5), calls=%async_computation | async-start | bytes 262144 | tf_op jit(solution)/shard_map/all_to_all | solution.py:174
  12.7 0.0 copy-done
  12.7 0.0 copy-start.2
  12.7 9.4 %collective-permute-start = (bf16[4,256,128]{2,1,0:T(8,128)(2,1)S(1)}, bf16[4,256,128]{2,1,0:T(8,128)(2,1)S(1)}, u32[]{:S(2)}, u32[]{:S(2)}) collective-permute-start(bf16[4,256,128]{2,1,0:T(8,128)(2,1)S(1)} %dynamic-slice_bitcast_fusion), channel_id=1, source_target_pairs={{0,1},{1,0},{2,3},{3,2},{4,5},{5,4},{6,7},{7,6},{8,9},{9,8},{10,11... | collective-permute-start | bytes 786440 | tf_op jit(solution)/shard_map/ppermute | solution.py:188
  22.1 0.0 copy-start.1
  22.1 0.0 copy-done.2
  22.1 0.6 copy-done.1
  22.8 0.8 shard_map.55.table_ref
  23.6 0.0 collective-permute-done.sibling_ref
  23.6 0.0 all-to-all-done.own_ref
  23.6 1.5 %shard_map.57 = bf16[32,2,16,128]{3,2,1,0:T(8,128)(2,1)} custom-call(s32[32]{0:T(128)S(1)} %copy-done.1, s32[6,256]{1,0:T(8,128)S(1)} %shard_map.55.table_ref, bf16[16,2,16,128]{3,2,1,0:T(8,128)(2,1)S(1)} %all-to-all-done.own_ref), custom_call_target="tpu_custom_call" | custom-call | tf_op jit(solution)/shard_map/pallas_call | solution.py:200
  25.1 17.5 %all-to-all-start.1 = ((bf16[32,2,16,128]{3,2,1,0:T(8,128)(2,1)}), bf16[32,2,16,128]{3,2,1,0:T(8,128)(2,1)S(1)}, u32[]{:S(2)}, u32[]{:S(2)}) async-start(bf16[32,2,16,128]{3,2,1,0:T(8,128)(2,1)} %shard_map.57), calls=%async_computation.1 | async-start | bytes 524288 | tf_op jit(solution)/shard_map/all_to_all | solution.py:207
  42.6 1.9 %collective-permute-start.2 = (bf16[2,256,128]{2,1,0:T(8,128)(2,1)S(1)}, bf16[2,256,128]{2,1,0:T(8,128)(2,1)S(1)}, u32[]{:S(2)}, u32[]{:S(2)}) collective-permute-start(bf16[2,256,128]{2,1,0:T(8,128)(2,1)S(1)} %get-tuple-element.40), channel_id=1, source_target_pairs={{0,4},{1,5},{2,6},{3,7},{4,0},{5,1},{6,2},{7,3},{8,12},{9,13},{10,... | collective-permute-start | bytes 393224 | tf_op jit(solution)/shard_map/ppermute | solution.py:211
  44.5 4.3 %collective-permute-start.3 = (bf16[2,256,128]{2,1,0:T(8,128)(2,1)S(1)}, bf16[2,256,128]{2,1,0:T(8,128)(2,1)S(1)}, u32[]{:S(2)}, u32[]{:S(2)}) collective-permute-start(bf16[2,256,128]{2,1,0:T(8,128)(2,1)S(1)} %get-tuple-element.41), channel_id=1, source_target_pairs={{0,6},{1,7},{2,4},{3,5},{4,2},{5,3},{6,0},{7,1},{8,14},{9,15},{10,... | collective-permute-start | bytes 393224 | tf_op jit(solution)/shard_map/ppermute | solution.py:211
  48.8 5.2 %collective-permute-done.2.refs_2_ = bf16[2,256,128]{2,1,0:T(8,128)(2,1)S(1)} collective-permute-done((bf16[2,256,128]{2,1,0:T(8,128)(2,1)S(1)}, bf16[2,256,128]{2,1,0:T(8,128)(2,1)S(1)}, u32[]{:S(2)}, u32[]{:S(2)}) %collective-permute-start.2) | collective-permute-done | bytes 131104 | tf_op jit(solution)/shard_map/ppermute | solution.py:211
  54.0 0.0 collective-permute-done.3.refs_3_
  54.0 1.4 %all-to-all-done.1.foreign_ref = bf16[32,2,16,128]{3,2,1,0:T(8,128)(2,1)S(1)} async-done(((bf16[32,2,16,128]{3,2,1,0:T(8,128)(2,1)}), bf16[32,2,16,128]{3,2,1,0:T(8,128)(2,1)S(1)}, u32[]{:S(2)}, u32[]{:S(2)}) %all-to-all-start.1) | async-done | bytes 262176 | tf_op jit(solution)/shard_map/all_to_all | solution.py:207
  55.4 1.8 %shard_map.58 = bf16[64,2,16,128]{3,2,1,0:T(8,128)(2,1)} custom-call(s32[1]{0:T(128)} %bitcast.me_ref, s32[32]{0:T(128)S(1)} %copy-done.1, s32[6,256]{1,0:T(8,128)S(1)} %shard_map.55.table_ref, bf16[16,2,16,128]{3,2,1,0:T(8,128)(2,1)S(1)} %all-to-all-done.own_ref, bf16[32,2,16,128]{3,2,1,0:T(8,128)(2,1)S(1)} %all-to-all-done.1.foreign_ref), custom_call_target="tpu_custom_call" | custom-call | tf_op jit(solution)/shard_map/pallas_call | solution.py:218
  57.2 10.3 %all-to-all-start.2 = ((bf16[64,2,16,128]{3,2,1,0:T(8,128)(2,1)}), bf16[64,2,16,128]{3,2,1,0:T(8,128)(2,1)S(1)}, u32[]{:S(2)}, u32[]{:S(2)}) async-start(bf16[64,2,16,128]{3,2,1,0:T(8,128)(2,1)} %shard_map.58), calls=%async_computation.2 | async-start | bytes 1048576 | tf_op jit(solution)/shard_map/all_to_all | solution.py:225
  67.4 3.3 %collective-permute-start.1 = (bf16[2,256,128]{2,1,0:T(8,128)(2,1)S(1)}, bf16[2,256,128]{2,1,0:T(8,128)(2,1)S(1)}, u32[]{:S(2)}, u32[]{:S(2)}) collective-permute-start(bf16[2,256,128]{2,1,0:T(8,128)(2,1)S(1)} %get-tuple-element.39), channel_id=1, source_target_pairs={{0,2},{1,3},{2,0},{3,1},{4,6},{5,7},{6,4},{7,5},{8,10},{9,11},{10,... | collective-permute-start | bytes 393224 | tf_op jit(solution)/shard_map/ppermute | solution.py:211
  70.7 8.5 %collective-permute-done.1.refs_1_ = bf16[2,256,128]{2,1,0:T(8,128)(2,1)S(1)} collective-permute-done((bf16[2,256,128]{2,1,0:T(8,128)(2,1)S(1)}, bf16[2,256,128]{2,1,0:T(8,128)(2,1)S(1)}, u32[]{:S(2)}, u32[]{:S(2)}) %collective-permute-start.1) | collective-permute-done | bytes 131104 | tf_op jit(solution)/shard_map/ppermute | solution.py:211
  79.3 2.7 %all-to-all-done.2 = bf16[64,2,16,128]{3,2,1,0:T(8,128)(2,1)S(1)} async-done(((bf16[64,2,16,128]{3,2,1,0:T(8,128)(2,1)}), bf16[64,2,16,128]{3,2,1,0:T(8,128)(2,1)S(1)}, u32[]{:S(2)}, u32[]{:S(2)}) %all-to-all-start.2) | async-done | bytes 524320 | tf_op jit(solution)/shard_map/all_to_all | solution.py:225
  81.9 2.3 %shard_map.59 = bf16[8,256,128]{2,1,0:T(8,128)(2,1)S(1)} custom-call(s32[1]{0:T(128)} %bitcast.me_ref, s32[1]{0:T(128)} %bitcast.1.rank_ref, s32[32]{0:T(128)S(1)} %copy-done.1, bf16[2,256,128]{2,1,0:T(8,128)(2,1)S(1)} %get-tuple-element.38.refs_0_, bf16[2,256,128]{2,1,0:T(8,128)(2,1)S(1)} %collective-permute-done.1.refs_1_, ...), custom_call_target="tpu_custom_call" | custom-call | tf_op jit(solution)/shard_map/pallas_call | solution.py:228
  84.2 17.8 %all_to_all.20 = bf16[8,256,128]{2,1,0:T(8,128)(2,1)S(1)} all-to-all(bf16[8,256,128]{2,1,0:T(8,128)(2,1)S(1)} %shard_map.59), channel_id=1, replica_groups={{0,1,2,3,4,5,6,7},{8,9,10,11,12,13,14,15},{16,17,18,19,20,21,22,23},{24..., dimensions={0} | all-to-all | bytes 1048576 | tf_op jit(solution)/shard_map/all_to_all | solution.py:237
  102.1 0.8 copy.11
  (2 shorter events, 0.1 us)
Async XLA Ops:
  0.0 12.7 %copy-start = (bf16[2048,1,128]{2,0,1:T(8,128)(2,1)S(1)}, bf16[2048,1,128]{2,0,1:T(8,128)(2,1)}, u32[]{:S(2)}) copy-start(bf16[2048,1,128]{2,0,1:T(8,128)(2,1)} %param.5) | copy-start | bytes 1572868
  2.4 21.2 %all-to-all-start = ((bf16[16,2,16,128]{3,2,1,0:T(8,128)(2,1)}), bf16[16,2,16,128]{3,2,1,0:T(8,128)(2,1)S(1)}, u32[]{:S(2)}, u32[]{:S(2)}) async-start(bf16[16,2,16,128]{3,2,1,0:T(8,128)(2,1)} %bitcast.5), calls=%async_computation | async-start | bytes 262144 | tf_op jit(solution)/shard_map/all_to_all | solution.py:174
  12.7 9.4 %copy-start.2 = (s32[256,4]{0,1:T(4,128)S(1)}, s32[256,4]{0,1:T(4,128)}, u32[]{:S(2)}) copy-start(s32[256,4]{0,1:T(4,128)} %param.8) | copy-start | bytes 12292
  12.7 10.8 %collective-permute-start = (bf16[4,256,128]{2,1,0:T(8,128)(2,1)S(1)}, bf16[4,256,128]{2,1,0:T(8,128)(2,1)S(1)}, u32[]{:S(2)}, u32[]{:S(2)}) collective-permute-start(bf16[4,256,128]{2,1,0:T(8,128)(2,1)S(1)} %dynamic-slice_bitcast_fusion), channel_id=1, source_target_pairs={{0,1},{1,0},{2,3},{3,2},{4,5},{5,4},{6,7},{7,6},{8,9},{9,8},{10,11... | collective-permute-start | bytes 786440 | tf_op jit(solution)/shard_map/ppermute | solution.py:188
  22.1 0.7 copy-start.1
  25.1 30.3 %all-to-all-start.1 = ((bf16[32,2,16,128]{3,2,1,0:T(8,128)(2,1)}), bf16[32,2,16,128]{3,2,1,0:T(8,128)(2,1)S(1)}, u32[]{:S(2)}, u32[]{:S(2)}) async-start(bf16[32,2,16,128]{3,2,1,0:T(8,128)(2,1)} %shard_map.57), calls=%async_computation.1 | async-start | bytes 524288 | tf_op jit(solution)/shard_map/all_to_all | solution.py:207
  42.6 11.4 %collective-permute-start.2 = (bf16[2,256,128]{2,1,0:T(8,128)(2,1)S(1)}, bf16[2,256,128]{2,1,0:T(8,128)(2,1)S(1)}, u32[]{:S(2)}, u32[]{:S(2)}) collective-permute-start(bf16[2,256,128]{2,1,0:T(8,128)(2,1)S(1)} %get-tuple-element.40), channel_id=1, source_target_pairs={{0,4},{1,5},{2,6},{3,7},{4,0},{5,1},{6,2},{7,3},{8,12},{9,13},{10,... | collective-permute-start | bytes 393224 | tf_op jit(solution)/shard_map/ppermute | solution.py:211
  44.5 9.4 %collective-permute-start.3 = (bf16[2,256,128]{2,1,0:T(8,128)(2,1)S(1)}, bf16[2,256,128]{2,1,0:T(8,128)(2,1)S(1)}, u32[]{:S(2)}, u32[]{:S(2)}) collective-permute-start(bf16[2,256,128]{2,1,0:T(8,128)(2,1)S(1)} %get-tuple-element.41), channel_id=1, source_target_pairs={{0,6},{1,7},{2,4},{3,5},{4,2},{5,3},{6,0},{7,1},{8,14},{9,15},{10,... | collective-permute-start | bytes 393224 | tf_op jit(solution)/shard_map/ppermute | solution.py:211
  57.2 24.8 %all-to-all-start.2 = ((bf16[64,2,16,128]{3,2,1,0:T(8,128)(2,1)}), bf16[64,2,16,128]{3,2,1,0:T(8,128)(2,1)S(1)}, u32[]{:S(2)}, u32[]{:S(2)}) async-start(bf16[64,2,16,128]{3,2,1,0:T(8,128)(2,1)} %shard_map.58), calls=%async_computation.2 | async-start | bytes 1048576 | tf_op jit(solution)/shard_map/all_to_all | solution.py:225
  67.4 11.8 %collective-permute-start.1 = (bf16[2,256,128]{2,1,0:T(8,128)(2,1)S(1)}, bf16[2,256,128]{2,1,0:T(8,128)(2,1)S(1)}, u32[]{:S(2)}, u32[]{:S(2)}) collective-permute-start(bf16[2,256,128]{2,1,0:T(8,128)(2,1)S(1)} %get-tuple-element.39), channel_id=1, source_target_pairs={{0,2},{1,3},{2,0},{3,1},{4,6},{5,7},{6,4},{7,5},{8,10},{9,11},{10,... | collective-permute-start | bytes 393224 | tf_op jit(solution)/shard_map/ppermute | solution.py:211

commit v5 on v4

--- a/solution.py
+++ b/solution.py
@@ -17,6 +17,13 @@
 
 def small(mib=4):
     return pltpu.CompilerParams(vmem_limit_bytes=mib * 2**20)
+
+
+def pack(key_ref, value_ref, out_ref):
+    heads, halves, _, rows, width = out_ref.shape
+    for i, ref in enumerate((key_ref, value_ref)):
+        turned = jnp.swapaxes(ref[...].astype(jnp.float32), 0, 1).astype(jnp.bfloat16)
+        out_ref[:, :, i] = turned.reshape(heads, halves, rows, width)
 
 
 def tables(per_span, me_ref, span_ref, listed_ref, out_ref):
@@ -167,9 +174,13 @@
     spread_groups = [
         [shards_per_block * j + q for j in range(block_count)] for q in range(shards_per_block)
     ]
-    kv = jnp.stack([keys, values])
-    kv = kv.reshape(2, halves, piece_rows, kv_heads, width).transpose(3, 1, 0, 2, 4)
-    kv = kv.reshape((block_count,) + piece)
+    kv = pl.pallas_call(
+        pack,
+        out_shape=jax.ShapeDtypeStruct((kv_heads, halves) + piece, bf16),
+        in_specs=[VMEM, VMEM],
+        out_specs=VMEM,
+        compiler_params=small(60),
+    )(keys, values).reshape((block_count,) + piece)
     kv, listed, queries = lax.optimization_barrier((kv, listed, queries))
     own = lax.all_to_all(kv, "head", 0, 0, tiled=True, axis_index_groups=spread_groups)
 
@@ -207,14 +218,14 @@
     foreign = lax.all_to_all(asked, "ctx", 0, 0, tiled=True)
 
     *bundles, _ = lax.optimization_barrier((*bundles, asked))
-    near, *far = [
-        lax.ppermute(bundles[k], "head", [(i, i ^ (2 * k)) for i in range(head_count)])
-        for k in range(1, chips)
-    ]
+    arrived = {
+        k: lax.ppermute(bundles[k], "head", [(i, i ^ (2 * k)) for i in range(head_count)])
+        for k in (*range(2, chips), 1)
+    }
 
     kv_groups = [[g * group + i for i in range(group)] for g in range(kv_heads)]
-    foreign, far = lax.optimization_barrier((foreign, far))
-    query_here = [bundles[0], near, *far]
+    foreign, arrived = lax.optimization_barrier((foreign, arrived))
+    query_here = [bundles[0]] + [arrived[k] for k in range(1, chips)]
     pairs = pl.pallas_call(
         functools.partial(pick_pairs, per_span),
         out_shape=jax.ShapeDtypeStruct((block_count * slot_count,) + piece, bf16),

time: 103 us -> 101 us (0.981)
  blocking collectives: 17.8 us -> 40.8 us
  waiting for transfers between devices: 17.8 us -> 4.04 us
  starting transfers between devices: 56.8 us -> 46.3 us
  local copies, waits for them, and re-layouts: 3.23 us -> 1.47 us
    all_to_all x0 -> x1, blocking collectives: none -> 23 us  [body(): lax.all_to_all(pairs, 'head', 0, 0, tiled=True, axis_index_groups=kv_groups)]
    all_to_all x1 -> x0, starting transfers between devices: 10.3 us -> none  [body(): lax.all_to_all(pairs, 'head', 0, 0, tiled=True, axis_index_groups=kv_groups)]
    ppermute x3, waiting for transfers between devices: 13.7 us -> 4.03 us  [body(): lax.ppermute(bundles[k], 'head', [(i, i ^ 2 * k) for i in range(head_coun...]
    all_to_all x1 -> x0, waiting for transfers between devices: 2.68 us -> none  [body(): lax.all_to_all(pairs, 'head', 0, 0, tiled=True, axis_index_groups=kv_groups)]
    another operation x2 -> x0, local copies, waits for them, and re-layouts: 1.76 us -> none  [body(): kv = jnp.stack([keys, values])]
    pallas_call x0 -> x1, Pallas kernels: none -> 1.65 us  [body(): pl.pallas_call(pack, out_shape=jax.ShapeDtypeStruct((kv_heads, halves) +...]
    all_to_all x1, waiting for transfers between devices: 1.41 us -> 0.01 us  [body(): foreign = lax.all_to_all(asked, 'ctx', 0, 0, tiled=True)]
  transfers between devices with their start and end apart: 7 -> 6, of which waited for: 4 -> 2; matrix products, arithmetic and copies ran while one was open for 0% -> 0% of each run, Pallas kernels for 1% -> 1%
where the time goes in v5:
time: 101 us; the launch traced here: 100 us
  starting transfers between devices  46.3 us (46%)
  blocking collectives  40.8 us (40%)
  Pallas kernels  7.28 us (7%)
  waiting for transfers between devices  4.04 us (4%)
  local copies, waits for them, and re-layouts  1.47 us (1%)
    all_to_all x1, blocking collectives, body(): lax.all_to_all(pairs, 'head', 0, 0, tiled=True, axis_index_groups=kv_groups)  23 us
    all_to_all x1, blocking collectives, body(): lax.all_to_all(done, 'head', 0, 0, tiled=True, axis_index_groups=kv_groups)  17.8 us
    all_to_all x1, starting transfers between devices, body(): foreign = lax.all_to_all(asked, 'ctx', 0, 0, tiled=True)  17.5 us
    all_to_all x1, starting transfers between devices, body(): lax.all_to_all(kv, 'head', 0, 0, tiled=True, axis_index_groups=spread_gro...  10.2 us
    ppermute x1, starting transfers between devices, body(): lax.ppermute(crossing, 'head', [(i, i ^ 1) for i in range(head_count)])  9.36 us
    ppermute x3, starting transfers between devices, body(): lax.ppermute(bundles[k], 'head', [(i, i ^ 2 * k) for i in range(head_coun...  9.27 us
    ppermute x3, waiting for transfers between devices, body(): lax.ppermute(bundles[k], 'head', [(i, i ^ 2 * k) for i in range(head_coun...  4.03 us
    pallas_call x1, Pallas kernels, body(): pl.pallas_call(functools.partial(attend, per_span), out_shape=jax.ShapeDt...  2.3 us
  transfers between devices with their start and end apart: 6, of which 2 were waited for; matrix products, arithmetic and copies ran while one was open for 0% of the time, Pallas kernels for 1%

profile of v5, /device:TPU:1, one launch (start us, length us, event | category | flops | bytes accessed | tf_op | source)
XLA Modules:
  0.0 100.1 jit_solution(11874628644478234583)
XLA Ops:
  0.0 0.0 copy-start
  0.0 1.6 %shard_map.55 = bf16[8,2,2,16,128]{4,3,2,1,0:T(8,128)(2,1)} custom-call(bf16[32,8,128]{2,1,0:T(8,128)(2,1)} %key_ref.1, bf16[32,8,128]{2,1,0:T(8,128)(2,1)} %value_ref.1), custom_call_target="tpu_custom_call" | custom-call | tf_op jit(solution)/shard_map/pallas_call | solution.py:177
  1.6 10.2 %all-to-all-start = ((bf16[16,2,16,128]{3,2,1,0:T(8,128)(2,1)}), bf16[16,2,16,128]{3,2,1,0:T(8,128)(2,1)S(1)}, u32[]{:S(2)}, u32[]{:S(2)}) async-start(bf16[16,2,16,128]{3,2,1,0:T(8,128)(2,1)} %bitcast.17), calls=%async_computation | async-start | bytes 262144 | tf_op jit(solution)/shard_map/all_to_all | solution.py:185
  11.9 0.0 copy-done
  11.9 0.0 copy-start.2
  11.9 9.4 %collective-permute-start = (bf16[4,256,128]{2,1,0:T(8,128)(2,1)S(1)}, bf16[4,256,128]{2,1,0:T(8,128)(2,1)S(1)}, u32[]{:S(2)}, u32[]{:S(2)}) collective-permute-start(bf16[4,256,128]{2,1,0:T(8,128)(2,1)S(1)} %dynamic-slice_bitcast_fusion), channel_id=1, source_target_pairs={{0,1},{1,0},{2,3},{3,2},{4,5},{5,4},{6,7},{7,6},{8,9},{9,8},{10,11... | collective-permute-start | bytes 786440 | tf_op jit(solution)/shard_map/ppermute | solution.py:199
  21.3 0.0 copy-start.1
  21.3 0.0 copy-done.2
  21.3 0.6 copy-done.1
  22.0 0.8 shard_map.56.table_ref
  22.8 0.0 collective-permute-done.sibling_ref
  22.8 0.0 all-to-all-done.own_ref
  22.8 1.5 %shard_map.58 = bf16[32,2,16,128]{3,2,1,0:T(8,128)(2,1)} custom-call(s32[32]{0:T(128)S(1)} %copy-done.1, s32[6,256]{1,0:T(8,128)S(1)} %shard_map.56.table_ref, bf16[16,2,16,128]{3,2,1,0:T(8,128)(2,1)S(1)} %all-to-all-done.own_ref), custom_call_target="tpu_custom_call" | custom-call | tf_op jit(solution)/shard_map/pallas_call | solution.py:211
  24.3 17.5 %all-to-all-start.1 = ((bf16[32,2,16,128]{3,2,1,0:T(8,128)(2,1)}), bf16[32,2,16,128]{3,2,1,0:T(8,128)(2,1)S(1)}, u32[]{:S(2)}, u32[]{:S(2)}) async-start(bf16[32,2,16,128]{3,2,1,0:T(8,128)(2,1)} %shard_map.58), calls=%async_computation.1 | async-start | bytes 524288 | tf_op jit(solution)/shard_map/all_to_all | solution.py:218
  41.8 2.2 %collective-permute-start.1 = (bf16[2,256,128]{2,1,0:T(8,128)(2,1)S(1)}, bf16[2,256,128]{2,1,0:T(8,128)(2,1)S(1)}, u32[]{:S(2)}, u32[]{:S(2)}) collective-permute-start(bf16[2,256,128]{2,1,0:T(8,128)(2,1)S(1)} %get-tuple-element.40), channel_id=1, source_target_pairs={{0,2},{1,3},{2,0},{3,1},{4,6},{5,7},{6,4},{7,5},{8,10},{9,11},{10,... | collective-permute-start | bytes 393224 | tf_op jit(solution)/shard_map/ppermute | solution.py:222
  44.0 2.3 %collective-permute-start.2 = (bf16[2,256,128]{2,1,0:T(8,128)(2,1)S(1)}, bf16[2,256,128]{2,1,0:T(8,128)(2,1)S(1)}, u32[]{:S(2)}, u32[]{:S(2)}) collective-permute-start(bf16[2,256,128]{2,1,0:T(8,128)(2,1)S(1)} %get-tuple-element.41), channel_id=1, source_target_pairs={{0,4},{1,5},{2,6},{3,7},{4,0},{5,1},{6,2},{7,3},{8,12},{9,13},{10,... | collective-permute-start | bytes 393224 | tf_op jit(solution)/shard_map/ppermute | solution.py:222
  46.3 4.8 %collective-permute-start.3 = (bf16[2,256,128]{2,1,0:T(8,128)(2,1)S(1)}, bf16[2,256,128]{2,1,0:T(8,128)(2,1)S(1)}, u32[]{:S(2)}, u32[]{:S(2)}) collective-permute-start(bf16[2,256,128]{2,1,0:T(8,128)(2,1)S(1)} %get-tuple-element.42), channel_id=1, source_target_pairs={{0,6},{1,7},{2,4},{3,5},{4,2},{5,3},{6,0},{7,1},{8,14},{9,15},{10,... | collective-permute-start | bytes 393224 | tf_op jit(solution)/shard_map/ppermute | solution.py:222
  51.1 0.0 collective-permute-done.1.refs_1_
  51.1 1.2 %collective-permute-done.2.refs_2_ = bf16[2,256,128]{2,1,0:T(8,128)(2,1)S(1)} collective-permute-done((bf16[2,256,128]{2,1,0:T(8,128)(2,1)S(1)}, bf16[2,256,128]{2,1,0:T(8,128)(2,1)S(1)}, u32[]{:S(2)}, u32[]{:S(2)}) %collective-permute-start.2) | collective-permute-done | bytes 131104 | tf_op jit(solution)/shard_map/ppermute | solution.py:222
  52.3 2.8 %collective-permute-done.3.refs_3_ = bf16[2,256,128]{2,1,0:T(8,128)(2,1)S(1)} collective-permute-done((bf16[2,256,128]{2,1,0:T(8,128)(2,1)S(1)}, bf16[2,256,128]{2,1,0:T(8,128)(2,1)S(1)}, u32[]{:S(2)}, u32[]{:S(2)}) %collective-permute-start.3) | collective-permute-done | bytes 131104 | tf_op jit(solution)/shard_map/ppermute | solution.py:222
  55.2 0.0 all-to-all-done.1.foreign_ref
  55.2 1.0 shard_map.59
  56.2 23.0 %all_to_all.20 = bf16[64,2,16,128]{3,2,1,0:T(8,128)(2,1)S(1)} all-to-all(bf16[64,2,16,128]{3,2,1,0:T(8,128)(2,1)S(1)} %shard_map.59), channel_id=1, replica_groups={{0,1,2,3,4,5,6,7},{8,9,10,11,12,13,14,15},{16,17,18,19,20,21,22,23},{24..., dimensions={0} | all-to-all | bytes 1048576 | tf_op jit(solution)/shard_map/all_to_all | solution.py:236
  79.2 2.3 %shard_map.60 = bf16[8,256,128]{2,1,0:T(8,128)(2,1)S(1)} custom-call(s32[1]{0:T(128)} %bitcast.me_ref, s32[1]{0:T(128)} %bitcast.1.rank_ref, s32[32]{0:T(128)S(1)} %copy-done.1, bf16[2,256,128]{2,1,0:T(8,128)(2,1)S(1)} %get-tuple-element.39.refs_0_, bf16[2,256,128]{2,1,0:T(8,128)(2,1)S(1)} %collective-permute-done.1.refs_1_, ...), custom_call_target="tpu_custom_call" | custom-call | tf_op jit(solution)/shard_map/pallas_call | solution.py:239
  81.5 17.8 %all_to_all.21 = bf16[8,256,128]{2,1,0:T(8,128)(2,1)S(1)} all-to-all(bf16[8,256,128]{2,1,0:T(8,128)(2,1)S(1)} %shard_map.60), channel_id=1, replica_groups={{0,1,2,3,4,5,6,7},{8,9,10,11,12,13,14,15},{16,17,18,19,20,21,22,23},{24..., dimensions={0} | all-to-all | bytes 1048576 | tf_op jit(solution)/shard_map/all_to_all | solution.py:248
  99.3 0.8 copy.9
  (2 shorter events, 0.1 us)
Async XLA Ops:
  0.0 11.9 %copy-start = (bf16[2048,1,128]{2,0,1:T(8,128)(2,1)S(1)}, bf16[2048,1,128]{2,0,1:T(8,128)(2,1)}, u32[]{:S(2)}) copy-start(bf16[2048,1,128]{2,0,1:T(8,128)(2,1)} %param.5) | copy-start | bytes 1572868
  1.6 21.2 %all-to-all-start = ((bf16[16,2,16,128]{3,2,1,0:T(8,128)(2,1)}), bf16[16,2,16,128]{3,2,1,0:T(8,128)(2,1)S(1)}, u32[]{:S(2)}, u32[]{:S(2)}) async-start(bf16[16,2,16,128]{3,2,1,0:T(8,128)(2,1)} %bitcast.17), calls=%async_computation | async-start | bytes 262144 | tf_op jit(solution)/shard_map/all_to_all | solution.py:185
  11.9 9.4 %copy-start.2 = (s32[256,4]{0,1:T(4,128)S(1)}, s32[256,4]{0,1:T(4,128)}, u32[]{:S(2)}) copy-start(s32[256,4]{0,1:T(4,128)} %param.8) | copy-start | bytes 12292
  11.9 10.8 %collective-permute-start = (bf16[4,256,128]{2,1,0:T(8,128)(2,1)S(1)}, bf16[4,256,128]{2,1,0:T(8,128)(2,1)S(1)}, u32[]{:S(2)}, u32[]{:S(2)}) collective-permute-start(bf16[4,256,128]{2,1,0:T(8,128)(2,1)S(1)} %dynamic-slice_bitcast_fusion), channel_id=1, source_target_pairs={{0,1},{1,0},{2,3},{3,2},{4,5},{5,4},{6,7},{7,6},{8,9},{9,8},{10,11... | collective-permute-start | bytes 786440 | tf_op jit(solution)/shard_map/ppermute | solution.py:199
  21.3 0.7 copy-start.1
  24.3 30.8 %all-to-all-start.1 = ((bf16[32,2,16,128]{3,2,1,0:T(8,128)(2,1)}), bf16[32,2,16,128]{3,2,1,0:T(8,128)(2,1)S(1)}, u32[]{:S(2)}, u32[]{:S(2)}) async-start(bf16[32,2,16,128]{3,2,1,0:T(8,128)(2,1)} %shard_map.58), calls=%async_computation.1 | async-start | bytes 524288 | tf_op jit(solution)/shard_map/all_to_all | solution.py:218
  41.8 9.3 %collective-permute-start.1 = (bf16[2,256,128]{2,1,0:T(8,128)(2,1)S(1)}, bf16[2,256,128]{2,1,0:T(8,128)(2,1)S(1)}, u32[]{:S(2)}, u32[]{:S(2)}) collective-permute-start(bf16[2,256,128]{2,1,0:T(8,128)(2,1)S(1)} %get-tuple-element.40), channel_id=1, source_target_pairs={{0,2},{1,3},{2,0},{3,1},{4,6},{5,7},{6,4},{7,5},{8,10},{9,11},{10,... | collective-permute-start | bytes 393224 | tf_op jit(solution)/shard_map/ppermute | solution.py:222
  44.0 8.3 %collective-permute-start.2 = (bf16[2,256,128]{2,1,0:T(8,128)(2,1)S(1)}, bf16[2,256,128]{2,1,0:T(8,128)(2,1)S(1)}, u32[]{:S(2)}, u32[]{:S(2)}) collective-permute-start(bf16[2,256,128]{2,1,0:T(8,128)(2,1)S(1)} %get-tuple-element.41), channel_id=1, source_target_pairs={{0,4},{1,5},{2,6},{3,7},{4,0},{5,1},{6,2},{7,3},{8,12},{9,13},{10,... | collective-permute-start | bytes 393224 | tf_op jit(solution)/shard_map/ppermute | solution.py:222
  46.3 8.8 %collective-permute-start.3 = (bf16[2,256,128]{2,1,0:T(8,128)(2,1)S(1)}, bf16[2,256,128]{2,1,0:T(8,128)(2,1)S(1)}, u32[]{:S(2)}, u32[]{:S(2)}) collective-permute-start(bf16[2,256,128]{2,1,0:T(8,128)(2,1)S(1)} %get-tuple-element.42), channel_id=1, source_target_pairs={{0,6},{1,7},{2,4},{3,5},{4,2},{5,3},{6,0},{7,1},{8,14},{9,15},{10,... | collective-permute-start | bytes 393224 | tf_op jit(solution)/shard_map/ppermute | solution.py:222

commit v6 on v5

--- a/solution.py
+++ b/solution.py
@@ -19,14 +19,16 @@
     return pltpu.CompilerParams(vmem_limit_bytes=mib * 2**20)
 
 
-def pack(key_ref, value_ref, out_ref):
-    heads, halves, _, rows, width = out_ref.shape
+def pack(lead, key_ref, value_ref, out_ref):
+    count, _, rows, width = out_ref.shape
     for i, ref in enumerate((key_ref, value_ref)):
         turned = jnp.swapaxes(ref[...].astype(jnp.float32), 0, 1).astype(jnp.bfloat16)
-        out_ref[:, :, i] = turned.reshape(heads, halves, rows, width)
-
-
-def tables(per_span, me_ref, span_ref, listed_ref, out_ref):
+        turned = turned.reshape(count, rows, width)
+        for j in range(count):
+            out_ref[j ^ lead, i] = turned[j]
+
+
+def tables(per_span, spread_lead, ctx_lead, me_ref, span_ref, listed_ref, out_ref):
     listed = listed_ref[...]
     slots, positions = listed.shape
     span_count = span_ref.shape[0]
@@ -68,16 +70,18 @@
         least = jnp.where(here & asking, held_float, float(blocks))
         least = jnp.min(jnp.min(least, axis=0, keepdims=True), axis=1, keepdims=True)
         lowest = jnp.where(here, least, lowest)
-    foreign = blocks + CAP * owner + jnp.where(held_float > lowest, 1, 0)
-    out_ref[2:2 + slots, :] = jnp.where(owner == me, held, foreign)
-
-
-def pick_asked(per_span, span_ref, table_ref, own_ref, out_ref):
+    foreign = blocks + CAP * (owner ^ ctx_lead) + jnp.where(held_float > lowest, 1, 0)
+    out_ref[2:2 + slots, :] = jnp.where(owner == me, held ^ spread_lead, foreign)
+
+
+def pick_asked(per_span, spread_lead, ctx_lead, span_ref, table_ref, own_ref, out_ref):
     for d in range(out_ref.shape[0] // CAP):
         a = span_ref[2 * d] * per_span
         b = span_ref[2 * d + 1] * per_span
-        out_ref[2 * d] = own_ref[jnp.minimum(table_ref[0, a], table_ref[0, b])]
-        out_ref[2 * d + 1] = own_ref[jnp.maximum(table_ref[1, a], table_ref[1, b])]
+        low = jnp.minimum(table_ref[0, a], table_ref[0, b])
+        high = jnp.maximum(table_ref[1, a], table_ref[1, b])
+        out_ref[2 * (d ^ ctx_lead)] = own_ref[low ^ spread_lead]
+        out_ref[2 * (d ^ ctx_lead) + 1] = own_ref[high ^ spread_lead]
 
 
 def pick_pairs(per_span, me_ref, span_ref, table_ref, own_ref, foreign_ref, out_ref):
@@ -101,7 +105,7 @@
         out_ref[1] = sibling_ref[to]
 
 
-def attend(per_span, me_ref, rank_ref, span_ref, *refs):
+def attend(per_span, lead, me_ref, rank_ref, span_ref, *refs):
     *query_refs, pair_ref, out_ref, key_all, value_all = refs
     pieces, pair_count, _, rows, width = pair_ref.shape
     blocks = key_all.shape[0]
@@ -111,7 +115,7 @@
     core = rank_ref[0] % 2
     row = lax.broadcasted_iota(jnp.int32, (BLK, BLK), 0)
     col = lax.broadcasted_iota(jnp.int32, (BLK, BLK), 1)
-    piece = col // rows
+    piece = (col // rows) ^ lead
     half = pieces // 2
     causal = 2 * rows * (piece % half) + rows * (piece // half) + col % rows <= row
     causal = jnp.concatenate([causal, causal], axis=0)
@@ -167,25 +171,29 @@
     i32 = jnp.int32
     bf16 = jnp.bfloat16
     me = lax.axis_index("ctx").astype(i32)
-    rank = lax.rem(lax.axis_index("head").astype(i32), group)
+    spread_lead = block_count // 2 + block_count // 8
+    ctx_lead = ctx_count // 2 + ctx_count // 4
+    group_lead = 2
+    rank = lax.rem(lax.axis_index("head").astype(i32), group) ^ group_lead
     piece = (2, piece_rows, width)
     listed = key_blocks.T
 
     spread_groups = [
-        [shards_per_block * j + q for j in range(block_count)] for q in range(shards_per_block)
+        [shards_per_block * (j ^ spread_lead) + q for j in range(block_count)]
+        for q in range(shards_per_block)
     ]
     kv = pl.pallas_call(
-        pack,
-        out_shape=jax.ShapeDtypeStruct((kv_heads, halves) + piece, bf16),
+        functools.partial(pack, spread_lead),
+        out_shape=jax.ShapeDtypeStruct((block_count,) + piece, bf16),
         in_specs=[VMEM, VMEM],
         out_specs=VMEM,
         compiler_params=small(60),
-    )(keys, values).reshape((block_count,) + piece)
+    )(keys, values)
     kv, listed, queries = lax.optimization_barrier((kv, listed, queries))
     own = lax.all_to_all(kv, "head", 0, 0, tiled=True, axis_index_groups=spread_groups)
 
     table = pl.pallas_call(
-        functools.partial(tables, per_span),
+        functools.partial(tables, per_span, spread_lead, ctx_lead),
         out_shape=jax.ShapeDtypeStruct((2 + slot_count, key_blocks.shape[0]), i32),
         in_specs=[SMEM, SMEM, VMEM],
         out_specs=VMEM,
@@ -209,13 +217,14 @@
     own, table, bundles = lax.optimization_barrier((own, table, bundles))
 
     asked = pl.pallas_call(
-        functools.partial(pick_asked, per_span),
+        functools.partial(pick_asked, per_span, spread_lead, ctx_lead),
         out_shape=jax.ShapeDtypeStruct((ctx_count * CAP,) + piece, bf16),
         in_specs=[SMEM, SMEM, VMEM],
         out_specs=VMEM,
         compiler_params=small(),
     )(span_order, table, own)
-    foreign = lax.all_to_all(asked, "ctx", 0, 0, tiled=True)
+    ctx_groups = [[i ^ ctx_lead for i in range(ctx_count)]]
+    foreign = lax.all_to_all(asked, "ctx", 0, 0, tiled=True, axis_index_groups=ctx_groups)
 
     *bundles, _ = lax.optimization_barrier((*bundles, asked))
     arrived = {
@@ -223,7 +232,7 @@
         for k in (*range(2, chips), 1)
     }
 
-    kv_groups = [[g * group + i for i in range(group)] for g in range(kv_heads)]
+    kv_groups = [[g * group + (i ^ group_lead) for i in range(group)] for g in range(kv_heads)]
     foreign, arrived = lax.optimization_barrier((foreign, arrived))
     query_here = [bundles[0]] + [arrived[k] for k in range(1, chips)]
     pairs = pl.pallas_call(
@@ -237,7 +246,7 @@
     pairs = pairs.reshape((group, per_rank * slot_count) + piece)
 
     done = pl.pallas_call(
-        functools.partial(attend, per_span),
+        functools.partial(attend, per_span, group_lead),
         out_shape=jax.ShapeDtypeStruct((group, per_rank * BLK, width), bf16),
         in_specs=[SMEM, SMEM, SMEM] + [VMEM] * (chips + 1),
         out_specs=VMEM,

time: 101 us -> 97 us (0.960)
  blocking collectives: 40.8 us -> 37.1 us
  waiting for transfers between devices: 4.04 us -> 5.89 us
  starting transfers between devices: 46.3 us -> 44.6 us
    all_to_all x1, starting transfers between devices: 17.5 us -> 9.68 us  [body(): lax.all_to_all(asked, 'ctx', 0, 0, tiled=True, axis_index_groups=ctx_groups)]
    ppermute x1, starting transfers between devices: 9.36 us -> 13.5 us  [body(): lax.ppermute(crossing, 'head', [(i, i ^ 1) for i in range(head_count)])]
    all_to_all x1, blocking collectives: 23 us -> 20.1 us  [body(): lax.all_to_all(pairs, 'head', 0, 0, tiled=True, axis_index_groups=kv_groups)]
    all_to_all x1, starting transfers between devices: 10.2 us -> 12.2 us  [body(): lax.all_to_all(kv, 'head', 0, 0, tiled=True, axis_index_groups=spread_gro...]
    all_to_all x1, waiting for transfers between devices: 0.01 us -> 1.65 us  [body(): lax.all_to_all(asked, 'ctx', 0, 0, tiled=True, axis_index_groups=ctx_groups)]
where the time goes in v6:
time: 97 us; the launch traced here: 96.5 us
  starting transfers between devices  44.6 us (46%)
  blocking collectives  37.1 us (38%)
  Pallas kernels  7.29 us (8%)
  waiting for transfers between devices  5.89 us (6%)
  local copies, waits for them, and re-layouts  1.47 us (2%)
    all_to_all x1, blocking collectives, body(): lax.all_to_all(pairs, 'head', 0, 0, tiled=True, axis_index_groups=kv_groups)  20.1 us
    all_to_all x1, blocking collectives, body(): lax.all_to_all(done, 'head', 0, 0, tiled=True, axis_index_groups=kv_groups)  17 us
    ppermute x1, starting transfers between devices, body(): lax.ppermute(crossing, 'head', [(i, i ^ 1) for i in range(head_count)])  13.5 us
    all_to_all x1, starting transfers between devices, body(): lax.all_to_all(kv, 'head', 0, 0, tiled=True, axis_index_groups=spread_gro...  12.2 us
    all_to_all x1, starting transfers between devices, body(): lax.all_to_all(asked, 'ctx', 0, 0, tiled=True, axis_index_groups=ctx_groups)  9.68 us
    ppermute x3, starting transfers between devices, body(): lax.ppermute(bundles[k], 'head', [(i, i ^ 2 * k) for i in range(head_coun...  9.26 us
    ppermute x3, waiting for transfers between devices, body(): lax.ppermute(bundles[k], 'head', [(i, i ^ 2 * k) for i in range(head_coun...  4.24 us
    pallas_call x1, Pallas kernels, body(): pl.pallas_call(functools.partial(attend, per_span, group_lead), out_shape...  2.3 us
  transfers between devices with their start and end apart: 6, of which 2 were waited for; matrix products, arithmetic and copies ran while one was open for 0% of the time, Pallas kernels for 1%

profile of v6, /device:TPU:1, one launch (start us, length us, event | category | flops | bytes accessed | tf_op | source)
XLA Modules:
  0.0 96.5 jit_solution(11301956723317347386)
XLA Ops:
  0.0 0.0 copy-start
  0.0 1.6 %shard_map.55 = bf16[16,2,16,128]{3,2,1,0:T(8,128)(2,1)} custom-call(bf16[32,8,128]{2,1,0:T(8,128)(2,1)} %key_ref.1, bf16[32,8,128]{2,1,0:T(8,128)(2,1)} %value_ref.1), custom_call_target="tpu_custom_call" | custom-call | tf_op jit(solution)/shard_map/pallas_call | solution.py:185
  1.6 12.2 %all-to-all-start = ((bf16[16,2,16,128]{3,2,1,0:T(8,128)(2,1)}), bf16[16,2,16,128]{3,2,1,0:T(8,128)(2,1)S(1)}, u32[]{:S(2)}, u32[]{:S(2)}) async-start(bf16[16,2,16,128]{3,2,1,0:T(8,128)(2,1)} %shard_map.55), calls=%async_computation | async-start | bytes 262144 | tf_op jit(solution)/shard_map/all_to_all | solution.py:193
  13.8 0.0 copy-done
  13.9 0.0 copy-start.2
  13.9 13.5 %collective-permute-start = (bf16[4,256,128]{2,1,0:T(8,128)(2,1)S(1)}, bf16[4,256,128]{2,1,0:T(8,128)(2,1)S(1)}, u32[]{:S(2)}, u32[]{:S(2)}) collective-permute-start(bf16[4,256,128]{2,1,0:T(8,128)(2,1)S(1)} %dynamic-slice_bitcast_fusion), channel_id=1, source_target_pairs={{0,1},{1,0},{2,3},{3,2},{4,5},{5,4},{6,7},{7,6},{8,9},{9,8},{10,11... | collective-permute-start | bytes 786440 | tf_op jit(solution)/shard_map/ppermute | solution.py:207
  27.4 0.0 copy-start.1
  27.4 0.0 copy-done.2
  27.4 0.6 copy-done.1
  28.1 0.8 shard_map.56.table_ref
  28.9 0.0 collective-permute-done.sibling_ref
  28.9 0.0 all-to-all-done.own_ref
  28.9 1.5 %shard_map.58 = bf16[32,2,16,128]{3,2,1,0:T(8,128)(2,1)} custom-call(s32[32]{0:T(128)S(1)} %copy-done.1, s32[6,256]{1,0:T(8,128)S(1)} %shard_map.56.table_ref, bf16[16,2,16,128]{3,2,1,0:T(8,128)(2,1)S(1)} %all-to-all-done.own_ref), custom_call_target="tpu_custom_call" | custom-call | tf_op jit(solution)/shard_map/pallas_call | solution.py:219
  30.4 9.7 %all-to-all-start.1 = ((bf16[32,2,16,128]{3,2,1,0:T(8,128)(2,1)}), bf16[32,2,16,128]{3,2,1,0:T(8,128)(2,1)S(1)}, u32[]{:S(2)}, u32[]{:S(2)}) async-start(bf16[32,2,16,128]{3,2,1,0:T(8,128)(2,1)} %shard_map.58), calls=%async_computation.1 | async-start | bytes 524288 | tf_op jit(solution)/shard_map/all_to_all | solution.py:227
  40.1 2.3 %collective-permute-start.1 = (bf16[2,256,128]{2,1,0:T(8,128)(2,1)S(1)}, bf16[2,256,128]{2,1,0:T(8,128)(2,1)S(1)}, u32[]{:S(2)}, u32[]{:S(2)}) collective-permute-start(bf16[2,256,128]{2,1,0:T(8,128)(2,1)S(1)} %get-tuple-element.40), channel_id=1, source_target_pairs={{0,2},{1,3},{2,0},{3,1},{4,6},{5,7},{6,4},{7,5},{8,10},{9,11},{10,... | collective-permute-start | bytes 393224 | tf_op jit(solution)/shard_map/ppermute | solution.py:231
  42.4 2.6 %collective-permute-start.2 = (bf16[2,256,128]{2,1,0:T(8,128)(2,1)S(1)}, bf16[2,256,128]{2,1,0:T(8,128)(2,1)S(1)}, u32[]{:S(2)}, u32[]{:S(2)}) collective-permute-start(bf16[2,256,128]{2,1,0:T(8,128)(2,1)S(1)} %get-tuple-element.41), channel_id=1, source_target_pairs={{0,4},{1,5},{2,6},{3,7},{4,0},{5,1},{6,2},{7,3},{8,12},{9,13},{10,... | collective-permute-start | bytes 393224 | tf_op jit(solution)/shard_map/ppermute | solution.py:231
  45.0 4.4 %collective-permute-start.3 = (bf16[2,256,128]{2,1,0:T(8,128)(2,1)S(1)}, bf16[2,256,128]{2,1,0:T(8,128)(2,1)S(1)}, u32[]{:S(2)}, u32[]{:S(2)}) collective-permute-start(bf16[2,256,128]{2,1,0:T(8,128)(2,1)S(1)} %get-tuple-element.42), channel_id=1, source_target_pairs={{0,6},{1,7},{2,4},{3,5},{4,2},{5,3},{6,0},{7,1},{8,14},{9,15},{10,... | collective-permute-start | bytes 393224 | tf_op jit(solution)/shard_map/ppermute | solution.py:231
  49.4 0.0 collective-permute-done.1.refs_1_
  49.4 4.2 %collective-permute-done.2.refs_2_ = bf16[2,256,128]{2,1,0:T(8,128)(2,1)S(1)} collective-permute-done((bf16[2,256,128]{2,1,0:T(8,128)(2,1)S(1)}, bf16[2,256,128]{2,1,0:T(8,128)(2,1)S(1)}, u32[]{:S(2)}, u32[]{:S(2)}) %collective-permute-start.2) | collective-permute-done | bytes 131104 | tf_op jit(solution)/shard_map/ppermute | solution.py:231
  53.6 0.0 collective-permute-done.3.refs_3_
  53.6 1.6 %all-to-all-done.1.foreign_ref = bf16[32,2,16,128]{3,2,1,0:T(8,128)(2,1)S(1)} async-done(((bf16[32,2,16,128]{3,2,1,0:T(8,128)(2,1)}), bf16[32,2,16,128]{3,2,1,0:T(8,128)(2,1)S(1)}, u32[]{:S(2)}, u32[]{:S(2)}) %all-to-all-start.1) | async-done | bytes 262176 | tf_op jit(solution)/shard_map/all_to_all | solution.py:227
  55.3 1.0 %shard_map.59 = bf16[64,2,16,128]{3,2,1,0:T(8,128)(2,1)S(1)} custom-call(s32[1]{0:T(128)} %bitcast.me_ref, s32[32]{0:T(128)S(1)} %copy-done.1, s32[6,256]{1,0:T(8,128)S(1)} %shard_map.56.table_ref, bf16[16,2,16,128]{3,2,1,0:T(8,128)(2,1)S(1)} %all-to-all-done.own_ref, bf16[32,2,16,128]{3,2,1,0:T(8,128)(2,1)S(1)} %all-to-all-done.1.foreign_ref), custom_call_target="tpu_custom_call" | custom-call | tf_op jit(solution)/shard_map/pallas_call | solution.py:238
  56.3 20.1 %all_to_all.20 = bf16[64,2,16,128]{3,2,1,0:T(8,128)(2,1)S(1)} all-to-all(bf16[64,2,16,128]{3,2,1,0:T(8,128)(2,1)S(1)} %shard_map.59), channel_id=1, replica_groups={{2,3,0,1,6,7,4,5},{10,11,8,9,14,15,12,13},{18,19,16,17,22,23,20,21},{26..., dimensions={0} | all-to-all | bytes 1048576 | tf_op jit(solution)/shard_map/all_to_all | solution.py:245
  76.4 2.3 %shard_map.60 = bf16[8,256,128]{2,1,0:T(8,128)(2,1)S(1)} custom-call(s32[1]{0:T(128)} %bitcast.me_ref, s32[1]{0:T(128)} %bitcast.1.rank_ref, s32[32]{0:T(128)S(1)} %copy-done.1, bf16[2,256,128]{2,1,0:T(8,128)(2,1)S(1)} %get-tuple-element.39.refs_0_, bf16[2,256,128]{2,1,0:T(8,128)(2,1)S(1)} %collective-permute-done.1.refs_1_, ...), custom_call_target="tpu_custom_call" | custom-call | tf_op jit(solution)/shard_map/pallas_call | solution.py:248
  78.7 17.0 %all_to_all.21 = bf16[8,256,128]{2,1,0:T(8,128)(2,1)S(1)} all-to-all(bf16[8,256,128]{2,1,0:T(8,128)(2,1)S(1)} %shard_map.60), channel_id=1, replica_groups={{2,3,0,1,6,7,4,5},{10,11,8,9,14,15,12,13},{18,19,16,17,22,23,20,21},{26..., dimensions={0} | all-to-all | bytes 1048576 | tf_op jit(solution)/shard_map/all_to_all | solution.py:257
  95.7 0.8 copy.9
  (2 shorter events, 0.1 us)
Async XLA Ops:
  0.0 13.8 %copy-start = (bf16[2048,1,128]{2,0,1:T(8,128)(2,1)S(1)}, bf16[2048,1,128]{2,0,1:T(8,128)(2,1)}, u32[]{:S(2)}) copy-start(bf16[2048,1,128]{2,0,1:T(8,128)(2,1)} %param.5) | copy-start | bytes 1572868
  1.6 27.3 %all-to-all-start = ((bf16[16,2,16,128]{3,2,1,0:T(8,128)(2,1)}), bf16[16,2,16,128]{3,2,1,0:T(8,128)(2,1)S(1)}, u32[]{:S(2)}, u32[]{:S(2)}) async-start(bf16[16,2,16,128]{3,2,1,0:T(8,128)(2,1)} %shard_map.55), calls=%async_computation | async-start | bytes 262144 | tf_op jit(solution)/shard_map/all_to_all | solution.py:193
  13.9 13.5 %copy-start.2 = (s32[256,4]{0,1:T(4,128)S(1)}, s32[256,4]{0,1:T(4,128)}, u32[]{:S(2)}) copy-start(s32[256,4]{0,1:T(4,128)} %param.8) | copy-start | bytes 12292
  13.9 15.0 %collective-permute-start = (bf16[4,256,128]{2,1,0:T(8,128)(2,1)S(1)}, bf16[4,256,128]{2,1,0:T(8,128)(2,1)S(1)}, u32[]{:S(2)}, u32[]{:S(2)}) collective-permute-start(bf16[4,256,128]{2,1,0:T(8,128)(2,1)S(1)} %dynamic-slice_bitcast_fusion), channel_id=1, source_target_pairs={{0,1},{1,0},{2,3},{3,2},{4,5},{5,4},{6,7},{7,6},{8,9},{9,8},{10,11... | collective-permute-start | bytes 786440 | tf_op jit(solution)/shard_map/ppermute | solution.py:207
  27.4 0.7 copy-start.1
  30.4 24.9 %all-to-all-start.1 = ((bf16[32,2,16,128]{3,2,1,0:T(8,128)(2,1)}), bf16[32,2,16,128]{3,2,1,0:T(8,128)(2,1)S(1)}, u32[]{:S(2)}, u32[]{:S(2)}) async-start(bf16[32,2,16,128]{3,2,1,0:T(8,128)(2,1)} %shard_map.58), calls=%async_computation.1 | async-start | bytes 524288 | tf_op jit(solution)/shard_map/all_to_all | solution.py:227
  40.1 9.3 %collective-permute-start.1 = (bf16[2,256,128]{2,1,0:T(8,128)(2,1)S(1)}, bf16[2,256,128]{2,1,0:T(8,128)(2,1)S(1)}, u32[]{:S(2)}, u32[]{:S(2)}) collective-permute-start(bf16[2,256,128]{2,1,0:T(8,128)(2,1)S(1)} %get-tuple-element.40), channel_id=1, source_target_pairs={{0,2},{1,3},{2,0},{3,1},{4,6},{5,7},{6,4},{7,5},{8,10},{9,11},{10,... | collective-permute-start | bytes 393224 | tf_op jit(solution)/shard_map/ppermute | solution.py:231
  42.4 11.2 %collective-permute-start.2 = (bf16[2,256,128]{2,1,0:T(8,128)(2,1)S(1)}, bf16[2,256,128]{2,1,0:T(8,128)(2,1)S(1)}, u32[]{:S(2)}, u32[]{:S(2)}) collective-permute-start(bf16[2,256,128]{2,1,0:T(8,128)(2,1)S(1)} %get-tuple-element.41), channel_id=1, source_target_pairs={{0,4},{1,5},{2,6},{3,7},{4,0},{5,1},{6,2},{7,3},{8,12},{9,13},{10,... | collective-permute-start | bytes 393224 | tf_op jit(solution)/shard_map/ppermute | solution.py:231
  45.0 8.6 %collective-permute-start.3 = (bf16[2,256,128]{2,1,0:T(8,128)(2,1)S(1)}, bf16[2,256,128]{2,1,0:T(8,128)(2,1)S(1)}, u32[]{:S(2)}, u32[]{:S(2)}) collective-permute-start(bf16[2,256,128]{2,1,0:T(8,128)(2,1)S(1)} %get-tuple-element.42), channel_id=1, source_target_pairs={{0,6},{1,7},{2,4},{3,5},{4,2},{5,3},{6,0},{7,1},{8,14},{9,15},{10,... | collective-permute-start | bytes 393224 | tf_op jit(solution)/shard_map/ppermute | solution.py:231

commit v7 on v6

--- a/solution.py
+++ b/solution.py
@@ -86,50 +86,78 @@
 
 def pick_pairs(per_span, me_ref, span_ref, table_ref, own_ref, foreign_ref, out_ref):
     own_count = own_ref.shape[0]
-    slots = out_ref.shape[0] // own_count
+    others = out_ref.shape[0] // own_count
     for block in range(own_count):
         position = span_ref[2 * me_ref[0] + block // per_span] * per_span + block % per_span
-        for j in range(slots):
-            at = table_ref[2 + j, position]
+        for j in range(others):
+            at = table_ref[3 + j, position]
             mine = own_ref[jnp.minimum(at, own_count - 1)]
             theirs = foreign_ref[jnp.maximum(at - own_count, 0)]
-            out_ref[block * slots + j] = jnp.where(at < own_count, mine, theirs)
-
-
-def bundle(rank_ref, query_ref, sibling_ref, *out_refs):
+            out_ref[block * others + j] = jnp.where(at < own_count, mine, theirs)
+
+
+def bundle(spread_lead, rank_ref, query_ref, sibling_ref, own_ref, *out_refs):
     chip = rank_ref[0] // 2
     core = rank_ref[0] % 2
+    rows = query_ref.shape[1]
+    _, _, piece_rows, _ = own_ref.shape
+    per_chip = 2 * rows // BLK
     for k, out_ref in enumerate(out_refs):
         to = chip ^ k
-        out_ref[0] = query_ref[2 * to + core]
-        out_ref[1] = sibling_ref[to]
+        out_ref[0:rows] = query_ref[2 * to + core]
+        out_ref[rows:2 * rows] = sibling_ref[to]
+        for block in range(per_chip):
+            for i in range(2):
+                first = 2 * rows + (2 * block + i) * piece_rows
+                out_ref[first:first + piece_rows] = own_ref[(per_chip * to + block) ^ spread_lead, i]
+
+
+def cross(rank_ref, *refs):
+    *bundle_refs, out_ref = refs
+    each = out_ref.shape[0] // len(bundle_refs)
+    first = bundle_refs[0].shape[0] - 2 * each
+    theirs = pl.multiple_of(first + (1 - rank_ref[0] % 2) * each, 16)
+    for k, ref in enumerate(bundle_refs):
+        out_ref[k * each:(k + 1) * each] = ref[pl.ds(theirs, each)]
 
 
 def attend(per_span, lead, me_ref, rank_ref, span_ref, *refs):
-    *query_refs, pair_ref, out_ref, key_all, value_all = refs
+    *bundle_refs, crossed_ref, pair_ref, out_ref, key_all, value_all = refs
     pieces, pair_count, _, rows, width = pair_ref.shape
     blocks = key_all.shape[0]
-    slots = pair_count // blocks
+    others = pair_count // blocks
+    slots = others + 1
+    half = pieces // 2
     factor = (width ** -0.5) * LOG2E
     chip = rank_ref[0] // 2
     core = rank_ref[0] % 2
-    row = lax.broadcasted_iota(jnp.int32, (BLK, BLK), 0)
-    col = lax.broadcasted_iota(jnp.int32, (BLK, BLK), 1)
-    piece = (col // rows) ^ lead
-    half = pieces // 2
-    causal = 2 * rows * (piece % half) + rows * (piece // half) + col % rows <= row
-    causal = jnp.concatenate([causal, causal], axis=0)
+    row = lax.broadcasted_iota(jnp.int32, (2 * BLK, BLK), 0)
+    col = lax.broadcasted_iota(jnp.int32, (2 * BLK, BLK), 1)
+    causal = col <= row % BLK
+    each = 2 * rows * blocks
+    query_rows = bundle_refs[0].shape[0] - 2 * each
+    mine = query_rows + core * each
     for b in range(blocks):
-        for j in range(slots):
-            i = b * slots + j
+        for k, ref in enumerate(bundle_refs):
+            for from_core in range(2):
+                g = (2 * (chip ^ k) + (core if from_core == 0 else 1 - core)) ^ lead
+                to = pl.ds(pl.multiple_of(2 * rows * (g % half) + rows * (g // half), 16), rows)
+                for i, store in enumerate((key_all, value_all)):
+                    at = (2 * b + i) * rows
+                    if from_core == 0:
+                        store[b, to, :] = ref[pl.ds(pl.multiple_of(mine + at, 16), rows)]
+                    else:
+                        store[b, to, :] = crossed_ref[k * each + at:k * each + at + rows]
+        for j in range(1, slots):
+            i = b * others + j - 1
             key_all[b, j * BLK:(j + 1) * BLK, :] = pair_ref[:, i, 0].reshape(BLK, width)
             value_all[b, j * BLK:(j + 1) * BLK, :] = pair_ref[:, i, 1].reshape(BLK, width)
     for b in range(blocks):
         block = rank_ref[0] * blocks + b
         position = span_ref[2 * me_ref[0] + block // per_span] * per_span + block % per_span
         here = slice(b * BLK, (b + 1) * BLK)
-        for k, query_ref in enumerate(query_refs):
-            q = query_ref[:, here, :].reshape(2 * BLK, width)
+        for k, ref in enumerate(bundle_refs):
+            q = ref[0:query_rows].reshape(2, query_rows // 2, width)[:, here].reshape(2 * BLK, width)
             s = lax.dot_general(
                 q, key_all[b], (((1,), (1,)), ((), ())), preferred_element_type=jnp.float32
             )
@@ -205,16 +233,7 @@
     query_parts = queries.reshape(chips, 2, rows_device // group, width)
     crossing = lax.dynamic_index_in_dim(query_parts, 1 - core, 1, keepdims=False)
     sibling = lax.ppermute(crossing, "head", [(i, i ^ 1) for i in range(head_count)])
-    part = jax.ShapeDtypeStruct((2, rows_device // group, width), bf16)
-    bundles = pl.pallas_call(
-        bundle,
-        out_shape=(part,) * chips,
-        in_specs=[SMEM, VMEM, VMEM],
-        out_specs=(VMEM,) * chips,
-        compiler_params=small(8),
-    )(rank[None], query_parts.reshape(group, rows_device // group, width), sibling)
-
-    own, table, bundles = lax.optimization_barrier((own, table, bundles))
+    own, table, sibling = lax.optimization_barrier((own, table, sibling))
 
     asked = pl.pallas_call(
         functools.partial(pick_asked, per_span, spread_lead, ctx_lead),
@@ -226,33 +245,51 @@
     ctx_groups = [[i ^ ctx_lead for i in range(ctx_count)]]
     foreign = lax.all_to_all(asked, "ctx", 0, 0, tiled=True, axis_index_groups=ctx_groups)
 
-    *bundles, _ = lax.optimization_barrier((*bundles, asked))
-    arrived = {
-        k: lax.ppermute(bundles[k], "head", [(i, i ^ (2 * k)) for i in range(head_count)])
-        for k in (*range(2, chips), 1)
-    }
+    *parts, _ = lax.optimization_barrier((query_parts, sibling, own, asked))
+    own_rows = 2 * per_rank * 2 * piece_rows
+    part = jax.ShapeDtypeStruct((2 * (rows_device // group) + own_rows, width), bf16)
+    bundles = pl.pallas_call(
+        functools.partial(bundle, spread_lead),
+        out_shape=(part,) * chips,
+        in_specs=[SMEM, VMEM, VMEM, VMEM],
+        out_specs=(VMEM,) * chips,
+        compiler_params=small(8),
+    )(rank[None], parts[0].reshape(group, rows_device // group, width), *parts[1:])
+    arrived = [bundles[0]] + [
+        lax.ppermute(bundles[k], "head", [(i, i ^ (2 * k)) for i in range(head_count)])
+        for k in range(1, chips)
+    ]
 
     kv_groups = [[g * group + (i ^ group_lead) for i in range(group)] for g in range(kv_heads)]
     foreign, arrived = lax.optimization_barrier((foreign, arrived))
-    query_here = [bundles[0]] + [arrived[k] for k in range(1, chips)]
     pairs = pl.pallas_call(
         functools.partial(pick_pairs, per_span),
-        out_shape=jax.ShapeDtypeStruct((block_count * slot_count,) + piece, bf16),
+        out_shape=jax.ShapeDtypeStruct((block_count * (slot_count - 1),) + piece, bf16),
         in_specs=[SMEM, SMEM, SMEM, VMEM, VMEM],
         out_specs=VMEM,
         compiler_params=small(),
     )(me[None], span_order, table, own, foreign)
+    pairs, arrived = lax.optimization_barrier((pairs, arrived))
     pairs = lax.all_to_all(pairs, "head", 0, 0, tiled=True, axis_index_groups=kv_groups)
-    pairs = pairs.reshape((group, per_rank * slot_count) + piece)
+    pairs = pairs.reshape((group, per_rank * (slot_count - 1)) + piece)
+
+    crossed = pl.pallas_call(
+        cross,
+        out_shape=jax.ShapeDtypeStruct((chips * own_rows // 2, width), bf16),
+        in_specs=[SMEM] + [VMEM] * chips,
+        out_specs=VMEM,
+        compiler_params=small(8),
+    )(rank[None], *arrived)
+    crossed = lax.ppermute(crossed, "head", [(i, i ^ 1) for i in range(head_count)])
 
     done = pl.pallas_call(
         functools.partial(attend, per_span, group_lead),
         out_shape=jax.ShapeDtypeStruct((group, per_rank * BLK, width), bf16),
-        in_specs=[SMEM, SMEM, SMEM] + [VMEM] * (chips + 1),
+        in_specs=[SMEM, SMEM, SMEM] + [VMEM] * (chips + 2),
         out_specs=VMEM,
         scratch_shapes=[pltpu.VMEM((per_rank, slot_count * BLK, width), bf16)] * 2,
         compiler_params=small(24),
-    )(me[None], rank[None], span_order, *query_here, pairs)
+    )(me[None], rank[None], span_order, *arrived, crossed, pairs)
 
     out = lax.all_to_all(done, "head", 0, 0, tiled=True, axis_index_groups=kv_groups)
     return out.reshape(rows_device, 1, width)

time: 97 us -> 98.8 us (1.019)
  blocking collectives: 37.1 us -> 16.8 us
  starting transfers between devices: 44.6 us -> 55.6 us
  waiting for transfers between devices: 5.89 us -> 16.1 us
    all_to_all x1 -> x0, blocking collectives: 20.1 us -> none  [body(): lax.all_to_all(pairs, 'head', 0, 0, tiled=True, axis_index_groups=kv_groups)]
    all_to_all x0 -> x1, starting transfers between devices: none -> 8.74 us  [body(): lax.all_to_all(pairs, 'head', 0, 0, tiled=True, axis_index_groups=kv_groups)]
    all_to_all x0 -> x1, waiting for transfers between devices: none -> 7.44 us  [body(): lax.all_to_all(pairs, 'head', 0, 0, tiled=True, axis_index_groups=kv_groups)]
    ppermute x3, waiting for transfers between devices: 4.24 us -> 7.77 us  [body(): lax.ppermute(bundles[k], 'head', [(i, i ^ 2 * k) for i in range(head_coun...]
    ppermute x0 -> x1, starting transfers between devices: none -> 2.27 us  [body(): lax.ppermute(crossed, 'head', [(i, i ^ 1) for i in range(head_count)])]
    all_to_all x1, waiting for transfers between devices: 1.65 us -> 0.01 us  [body(): lax.all_to_all(asked, 'ctx', 0, 0, tiled=True, axis_index_groups=ctx_groups)]
  transfers between devices with their start and end apart: 6 -> 8, of which waited for: 2 -> 3; matrix products, arithmetic and copies ran while one was open for 0% -> 0% of each run, Pallas kernels for 1% -> 1%
where the time goes in v7:
time: 98.8 us; the launch traced here: 98.2 us
  starting transfers between devices  55.6 us (56%)
  blocking collectives  16.8 us (17%)
  waiting for transfers between devices  16.1 us (16%)
  Pallas kernels  8.03 us (8%)
  local copies, waits for them, and re-layouts  1.47 us (1%)
    all_to_all x1, blocking collectives, body(): lax.all_to_all(done, 'head', 0, 0, tiled=True, axis_index_groups=kv_groups)  16.8 us
    ppermute x1, starting transfers between devices, body(): lax.ppermute(crossing, 'head', [(i, i ^ 1) for i in range(head_count)])  13.5 us
    all_to_all x1, starting transfers between devices, body(): lax.all_to_all(kv, 'head', 0, 0, tiled=True, axis_index_groups=spread_gro...  12.2 us
    all_to_all x1, starting transfers between devices, body(): lax.all_to_all(asked, 'ctx', 0, 0, tiled=True, axis_index_groups=ctx_groups)  9.68 us
    ppermute x3, starting transfers between devices, body(): lax.ppermute(bundles[k], 'head', [(i, i ^ 2 * k) for i in range(head_coun...  9.27 us
    all_to_all x1, starting transfers between devices, body(): lax.all_to_all(pairs, 'head', 0, 0, tiled=True, axis_index_groups=kv_groups)  8.74 us
    ppermute x3, waiting for transfers between devices, body(): lax.ppermute(bundles[k], 'head', [(i, i ^ 2 * k) for i in range(head_coun...  7.77 us
    all_to_all x1, waiting for transfers between devices, body(): lax.all_to_all(pairs, 'head', 0, 0, tiled=True, axis_index_groups=kv_groups)  7.44 us
  transfers between devices with their start and end apart: 8, of which 3 were waited for; matrix products, arithmetic and copies ran while one was open for 0% of the time, Pallas kernels for 1%

profile of v7, /device:TPU:1, one launch (start us, length us, event | category | flops | bytes accessed | tf_op | source)
XLA Modules:
  0.0 98.2 jit_solution(10992677838231281197)
XLA Ops:
  0.0 0.0 copy-start
  0.0 1.6 %shard_map.55 = bf16[16,2,16,128]{3,2,1,0:T(8,128)(2,1)} custom-call(bf16[32,8,128]{2,1,0:T(8,128)(2,1)} %key_ref.1, bf16[32,8,128]{2,1,0:T(8,128)(2,1)} %value_ref.1), custom_call_target="tpu_custom_call" | custom-call | tf_op jit(solution)/shard_map/pallas_call | solution.py:213
  1.6 12.2 %all-to-all-start = ((bf16[16,2,16,128]{3,2,1,0:T(8,128)(2,1)}), bf16[16,2,16,128]{3,2,1,0:T(8,128)(2,1)S(1)}, u32[]{:S(2)}, u32[]{:S(2)}) async-start(bf16[16,2,16,128]{3,2,1,0:T(8,128)(2,1)} %shard_map.55), calls=%async_computation | async-start | bytes 262144 | tf_op jit(solution)/shard_map/all_to_all | solution.py:221
  13.8 0.0 copy-done
  13.9 0.0 copy-start.2
  13.9 13.5 %collective-permute-start = (bf16[4,256,128]{2,1,0:T(8,128)(2,1)S(1)}, bf16[4,256,128]{2,1,0:T(8,128)(2,1)S(1)}, u32[]{:S(2)}, u32[]{:S(2)}) collective-permute-start(bf16[4,256,128]{2,1,0:T(8,128)(2,1)S(1)} %dynamic-slice_bitcast_fusion), channel_id=1, source_target_pairs={{0,1},{1,0},{2,3},{3,2},{4,5},{5,4},{6,7},{7,6},{8,9},{9,8},{10,11... | collective-permute-start | bytes 786440 | tf_op jit(solution)/shard_map/ppermute | solution.py:235
  27.4 0.0 copy-start.1
  27.4 0.0 copy-done.2
  27.4 0.6 copy-done.1
  28.1 0.8 shard_map.56.table_ref
  28.9 0.0 all-to-all-done.own_ref
  28.9 0.0 collective-permute-done.sibling_ref
  28.9 1.5 %shard_map.57 = bf16[32,2,16,128]{3,2,1,0:T(8,128)(2,1)} custom-call(s32[32]{0:T(128)S(1)} %copy-done.1, s32[6,256]{1,0:T(8,128)S(1)} %shard_map.56.table_ref, bf16[16,2,16,128]{3,2,1,0:T(8,128)(2,1)S(1)} %all-to-all-done.own_ref), custom_call_target="tpu_custom_call" | custom-call | tf_op jit(solution)/shard_map/pallas_call | solution.py:238
  30.4 9.7 %all-to-all-start.1 = ((bf16[32,2,16,128]{3,2,1,0:T(8,128)(2,1)}), bf16[32,2,16,128]{3,2,1,0:T(8,128)(2,1)S(1)}, u32[]{:S(2)}, u32[]{:S(2)}) async-start(bf16[32,2,16,128]{3,2,1,0:T(8,128)(2,1)} %shard_map.57), calls=%async_computation.1 | async-start | bytes 524288 | tf_op jit(solution)/shard_map/all_to_all | solution.py:246
  40.1 2.3 %collective-permute-start.1 = (bf16[640,128]{1,0:T(8,128)(2,1)S(1)}, bf16[640,128]{1,0:T(8,128)(2,1)S(1)}, u32[]{:S(2)}, u32[]{:S(2)}) collective-permute-start(bf16[640,128]{1,0:T(8,128)(2,1)S(1)} %get-tuple-element.38), channel_id=1, source_target_pairs={{0,2},{1,3},{2,0},{3,1},{4,6},{5,7},{6,4},{7,5},{8,10},{9,11},{10,... | collective-permute-start | bytes 491528 | tf_op jit(solution)/shard_map/ppermute | solution.py:259
  42.4 2.6 %collective-permute-start.2 = (bf16[640,128]{1,0:T(8,128)(2,1)S(1)}, bf16[640,128]{1,0:T(8,128)(2,1)S(1)}, u32[]{:S(2)}, u32[]{:S(2)}) collective-permute-start(bf16[640,128]{1,0:T(8,128)(2,1)S(1)} %get-tuple-element.39), channel_id=1, source_target_pairs={{0,4},{1,5},{2,6},{3,7},{4,0},{5,1},{6,2},{7,3},{8,12},{9,13},{10,... | collective-permute-start | bytes 491528 | tf_op jit(solution)/shard_map/ppermute | solution.py:259
  45.1 4.3 %collective-permute-start.3 = (bf16[640,128]{1,0:T(8,128)(2,1)S(1)}, bf16[640,128]{1,0:T(8,128)(2,1)S(1)}, u32[]{:S(2)}, u32[]{:S(2)}) collective-permute-start(bf16[640,128]{1,0:T(8,128)(2,1)S(1)} %get-tuple-element.40), channel_id=1, source_target_pairs={{0,6},{1,7},{2,4},{3,5},{4,2},{5,3},{6,0},{7,1},{8,14},{9,15},{10,... | collective-permute-start | bytes 491528 | tf_op jit(solution)/shard_map/ppermute | solution.py:259
  49.4 0.0 collective-permute-done.1.refs_1_
  49.4 7.8 %collective-permute-done.2.refs_2_ = bf16[640,128]{1,0:T(8,128)(2,1)S(1)} collective-permute-done((bf16[640,128]{1,0:T(8,128)(2,1)S(1)}, bf16[640,128]{1,0:T(8,128)(2,1)S(1)}, u32[]{:S(2)}, u32[]{:S(2)}) %collective-permute-start.2) | collective-permute-done | bytes 163872 | tf_op jit(solution)/shard_map/ppermute | solution.py:259
  57.2 0.0 collective-permute-done.3.refs_3_
  57.2 0.0 all-to-all-done.1.foreign_ref
  57.2 1.7 %shard_map.59 = bf16[48,2,16,128]{3,2,1,0:T(8,128)(2,1)} custom-call(s32[1]{0:T(128)} %bitcast.me_ref, s32[32]{0:T(128)S(1)} %copy-done.1, s32[6,256]{1,0:T(8,128)S(1)} %shard_map.56.table_ref, bf16[16,2,16,128]{3,2,1,0:T(8,128)(2,1)S(1)} %all-to-all-done.own_ref, bf16[32,2,16,128]{3,2,1,0:T(8,128)(2,1)S(1)} %all-to-all-done.1.foreign_ref), custom_call_target="tpu_custom_call" | custom-call | tf_op jit(solution)/shard_map/pallas_call | solution.py:265
  58.9 8.7 %all-to-all-start.2 = ((bf16[48,2,16,128]{3,2,1,0:T(8,128)(2,1)}), bf16[48,2,16,128]{3,2,1,0:T(8,128)(2,1)S(1)}, u32[]{:S(2)}, u32[]{:S(2)}) async-start(bf16[48,2,16,128]{3,2,1,0:T(8,128)(2,1)} %shard_map.59), calls=%async_computation.2 | async-start | bytes 786432 | tf_op jit(solution)/shard_map/all_to_all | solution.py:273
  67.6 2.3 %collective-permute-start.4 = (bf16[256,128]{1,0:T(8,128)(2,1)S(1)}, bf16[256,128]{1,0:T(8,128)(2,1)S(1)}, u32[]{:S(2)}, u32[]{:S(2)}) collective-permute-start(bf16[256,128]{1,0:T(8,128)(2,1)S(1)} %shard_map.60), channel_id=1, source_target_pairs={{0,1},{1,0},{2,3},{3,2},{4,5},{5,4},{6,7},{7,6},{8,9},{9,8},{10,11... | collective-permute-start | bytes 196616 | tf_op jit(solution)/shard_map/ppermute | solution.py:283
  69.9 0.9 collective-permute-done.4.refs_4_
  70.8 7.4 %all-to-all-done.2 = bf16[48,2,16,128]{3,2,1,0:T(8,128)(2,1)S(1)} async-done(((bf16[48,2,16,128]{3,2,1,0:T(8,128)(2,1)}), bf16[48,2,16,128]{3,2,1,0:T(8,128)(2,1)S(1)}, u32[]{:S(2)}, u32[]{:S(2)}) %all-to-all-start.2) | async-done | bytes 393248 | tf_op jit(solution)/shard_map/all_to_all | solution.py:273
  78.2 2.4 %shard_map.61 = bf16[8,256,128]{2,1,0:T(8,128)(2,1)S(1)} custom-call(s32[1]{0:T(128)} %bitcast.me_ref, s32[1]{0:T(128)} %bitcast.1.rank_ref, s32[32]{0:T(128)S(1)} %copy-done.1, bf16[640,128]{1,0:T(8,128)(2,1)S(1)} %get-tuple-element.46.refs_0_, bf16[640,128]{1,0:T(8,128)(2,1)S(1)} %collective-permute-done.1.refs_1_, ...), custom_call_target="tpu_custom_call" | custom-call | tf_op jit(solution)/shard_map/pallas_call | solution.py:285
  80.6 16.8 %all_to_all.20 = bf16[8,256,128]{2,1,0:T(8,128)(2,1)S(1)} all-to-all(bf16[8,256,128]{2,1,0:T(8,128)(2,1)S(1)} %shard_map.61), channel_id=1, replica_groups={{2,3,0,1,6,7,4,5},{10,11,8,9,14,15,12,13},{18,19,16,17,22,23,20,21},{26..., dimensions={0} | all-to-all | bytes 1048576 | tf_op jit(solution)/shard_map/all_to_all | solution.py:294
  97.4 0.8 copy.9
  (3 shorter events, 0.1 us)
Async XLA Ops:
  0.0 13.8 %copy-start = (bf16[2048,1,128]{2,0,1:T(8,128)(2,1)S(1)}, bf16[2048,1,128]{2,0,1:T(8,128)(2,1)}, u32[]{:S(2)}) copy-start(bf16[2048,1,128]{2,0,1:T(8,128)(2,1)} %param.5) | copy-start | bytes 1572868
  1.6 27.2 %all-to-all-start = ((bf16[16,2,16,128]{3,2,1,0:T(8,128)(2,1)}), bf16[16,2,16,128]{3,2,1,0:T(8,128)(2,1)S(1)}, u32[]{:S(2)}, u32[]{:S(2)}) async-start(bf16[16,2,16,128]{3,2,1,0:T(8,128)(2,1)} %shard_map.55), calls=%async_computation | async-start | bytes 262144 | tf_op jit(solution)/shard_map/all_to_all | solution.py:221
  13.9 13.5 %copy-start.2 = (s32[256,4]{0,1:T(4,128)S(1)}, s32[256,4]{0,1:T(4,128)}, u32[]{:S(2)}) copy-start(s32[256,4]{0,1:T(4,128)} %param.8) | copy-start | bytes 12292
  13.9 15.0 %collective-permute-start = (bf16[4,256,128]{2,1,0:T(8,128)(2,1)S(1)}, bf16[4,256,128]{2,1,0:T(8,128)(2,1)S(1)}, u32[]{:S(2)}, u32[]{:S(2)}) collective-permute-start(bf16[4,256,128]{2,1,0:T(8,128)(2,1)S(1)} %dynamic-slice_bitcast_fusion), channel_id=1, source_target_pairs={{0,1},{1,0},{2,3},{3,2},{4,5},{5,4},{6,7},{7,6},{8,9},{9,8},{10,11... | collective-permute-start | bytes 786440 | tf_op jit(solution)/shard_map/ppermute | solution.py:235
  27.4 0.7 copy-start.1
  30.4 26.8 %all-to-all-start.1 = ((bf16[32,2,16,128]{3,2,1,0:T(8,128)(2,1)}), bf16[32,2,16,128]{3,2,1,0:T(8,128)(2,1)S(1)}, u32[]{:S(2)}, u32[]{:S(2)}) async-start(bf16[32,2,16,128]{3,2,1,0:T(8,128)(2,1)} %shard_map.57), calls=%async_computation.1 | async-start | bytes 524288 | tf_op jit(solution)/shard_map/all_to_all | solution.py:246
  40.1 9.3 %collective-permute-start.1 = (bf16[640,128]{1,0:T(8,128)(2,1)S(1)}, bf16[640,128]{1,0:T(8,128)(2,1)S(1)}, u32[]{:S(2)}, u32[]{:S(2)}) collective-permute-start(bf16[640,128]{1,0:T(8,128)(2,1)S(1)} %get-tuple-element.38), channel_id=1, source_target_pairs={{0,2},{1,3},{2,0},{3,1},{4,6},{5,7},{6,4},{7,5},{8,10},{9,11},{10,... | collective-permute-start | bytes 491528 | tf_op jit(solution)/shard_map/ppermute | solution.py:259
  42.4 14.8 %collective-permute-start.2 = (bf16[640,128]{1,0:T(8,128)(2,1)S(1)}, bf16[640,128]{1,0:T(8,128)(2,1)S(1)}, u32[]{:S(2)}, u32[]{:S(2)}) collective-permute-start(bf16[640,128]{1,0:T(8,128)(2,1)S(1)} %get-tuple-element.39), channel_id=1, source_target_pairs={{0,4},{1,5},{2,6},{3,7},{4,0},{5,1},{6,2},{7,3},{8,12},{9,13},{10,... | collective-permute-start | bytes 491528 | tf_op jit(solution)/shard_map/ppermute | solution.py:259
  45.1 12.1 %collective-permute-start.3 = (bf16[640,128]{1,0:T(8,128)(2,1)S(1)}, bf16[640,128]{1,0:T(8,128)(2,1)S(1)}, u32[]{:S(2)}, u32[]{:S(2)}) collective-permute-start(bf16[640,128]{1,0:T(8,128)(2,1)S(1)} %get-tuple-element.40), channel_id=1, source_target_pairs={{0,6},{1,7},{2,4},{3,5},{4,2},{5,3},{6,0},{7,1},{8,14},{9,15},{10,... | collective-permute-start | bytes 491528 | tf_op jit(solution)/shard_map/ppermute | solution.py:259
  58.9 19.3 %all-to-all-start.2 = ((bf16[48,2,16,128]{3,2,1,0:T(8,128)(2,1)}), bf16[48,2,16,128]{3,2,1,0:T(8,128)(2,1)S(1)}, u32[]{:S(2)}, u32[]{:S(2)}) async-start(bf16[48,2,16,128]{3,2,1,0:T(8,128)(2,1)} %shard_map.59), calls=%async_computation.2 | async-start | bytes 786432 | tf_op jit(solution)/shard_map/all_to_all | solution.py:273
  67.6 3.2 %collective-permute-start.4 = (bf16[256,128]{1,0:T(8,128)(2,1)S(1)}, bf16[256,128]{1,0:T(8,128)(2,1)S(1)}, u32[]{:S(2)}, u32[]{:S(2)}) collective-permute-start(bf16[256,128]{1,0:T(8,128)(2,1)S(1)} %shard_map.60), channel_id=1, source_target_pairs={{0,1},{1,0},{2,3},{3,2},{4,5},{5,4},{6,7},{7,6},{8,9},{9,8},{10,11... | collective-permute-start | bytes 196616 | tf_op jit(solution)/shard_map/ppermute | solution.py:283

commit v8 on v6

--- a/solution.py
+++ b/solution.py
@@ -227,14 +227,14 @@
     foreign = lax.all_to_all(asked, "ctx", 0, 0, tiled=True, axis_index_groups=ctx_groups)
 
     *bundles, _ = lax.optimization_barrier((*bundles, asked))
-    arrived = {
-        k: lax.ppermute(bundles[k], "head", [(i, i ^ (2 * k)) for i in range(head_count)])
+    arrived = [
+        lax.ppermute(bundles[k], "head", [(i, i ^ (2 * k)) for i in range(head_count)])
         for k in (*range(2, chips), 1)
-    }
+    ]
 
     kv_groups = [[g * group + (i ^ group_lead) for i in range(group)] for g in range(kv_heads)]
     foreign, arrived = lax.optimization_barrier((foreign, arrived))
-    query_here = [bundles[0]] + [arrived[k] for k in range(1, chips)]
+    query_here = [bundles[0], arrived[-1], *arrived[:-1]]
     pairs = pl.pallas_call(
         functools.partial(pick_pairs, per_span),
         out_shape=jax.ShapeDtypeStruct((block_count * slot_count,) + piece, bf16),

time: 97 us -> 95.2 us (0.981)
  blocking collectives: 37.1 us -> 33.9 us
  waiting for transfers between devices: 5.89 us -> 8.25 us
    ppermute x3, waiting for transfers between devices: 4.24 us -> 8.24 us  [body(): lax.ppermute(bundles[k], 'head', [(i, i ^ 2 * k) for i in range(head_coun...]
    all_to_all x1, blocking collectives: 20.1 us -> 16.8 us  [body(): lax.all_to_all(pairs, 'head', 0, 0, tiled=True, axis_index_groups=kv_groups)]
    all_to_all x1, waiting for transfers between devices: 1.65 us -> 0.01 us  [body(): lax.all_to_all(asked, 'ctx', 0, 0, tiled=True, axis_index_groups=ctx_groups)]
where the time goes in v8:
time: 95.2 us; the launch traced here: 94.7 us
  starting transfers between devices  43.7 us (46%)
  blocking collectives  33.9 us (36%)
  waiting for transfers between devices  8.25 us (9%)
  Pallas kernels  7.29 us (8%)
  local copies, waits for them, and re-layouts  1.47 us (2%)
    all_to_all x1, blocking collectives, body(): lax.all_to_all(done, 'head', 0, 0, tiled=True, axis_index_groups=kv_groups)  17 us
    all_to_all x1, blocking collectives, body(): lax.all_to_all(pairs, 'head', 0, 0, tiled=True, axis_index_groups=kv_groups)  16.8 us
    ppermute x1, starting transfers between devices, body(): lax.ppermute(crossing, 'head', [(i, i ^ 1) for i in range(head_count)])  13.5 us
    all_to_all x1, starting transfers between devices, body(): lax.all_to_all(kv, 'head', 0, 0, tiled=True, axis_index_groups=spread_gro...  12.2 us
    all_to_all x1, starting transfers between devices, body(): lax.all_to_all(asked, 'ctx', 0, 0, tiled=True, axis_index_groups=ctx_groups)  9.68 us
    ppermute x3, starting transfers between devices, body(): lax.ppermute(bundles[k], 'head', [(i, i ^ 2 * k) for i in range(head_coun...  8.36 us
    ppermute x3, waiting for transfers between devices, body(): lax.ppermute(bundles[k], 'head', [(i, i ^ 2 * k) for i in range(head_coun...  8.24 us
    pallas_call x1, Pallas kernels, body(): pl.pallas_call(functools.partial(attend, per_span, group_lead), out_shape...  2.3 us
  transfers between devices with their start and end apart: 6, of which 2 were waited for; matrix products, arithmetic and copies ran while one was open for 0% of the time, Pallas kernels for 1%

profile of v8, /device:TPU:1, one launch (start us, length us, event | category | flops | bytes accessed | tf_op | source)
XLA Modules:
  0.0 94.7 jit_solution(10146546144055330918)
XLA Ops:
  0.0 0.0 copy-start
  0.0 1.6 %shard_map.55 = bf16[16,2,16,128]{3,2,1,0:T(8,128)(2,1)} custom-call(bf16[32,8,128]{2,1,0:T(8,128)(2,1)} %key_ref.1, bf16[32,8,128]{2,1,0:T(8,128)(2,1)} %value_ref.1), custom_call_target="tpu_custom_call" | custom-call | tf_op jit(solution)/shard_map/pallas_call | solution.py:185
  1.6 12.2 %all-to-all-start = ((bf16[16,2,16,128]{3,2,1,0:T(8,128)(2,1)}), bf16[16,2,16,128]{3,2,1,0:T(8,128)(2,1)S(1)}, u32[]{:S(2)}, u32[]{:S(2)}) async-start(bf16[16,2,16,128]{3,2,1,0:T(8,128)(2,1)} %shard_map.55), calls=%async_computation | async-start | bytes 262144 | tf_op jit(solution)/shard_map/all_to_all | solution.py:193
  13.8 0.0 copy-done
  13.9 0.0 copy-start.2
  13.9 13.5 %collective-permute-start = (bf16[4,256,128]{2,1,0:T(8,128)(2,1)S(1)}, bf16[4,256,128]{2,1,0:T(8,128)(2,1)S(1)}, u32[]{:S(2)}, u32[]{:S(2)}) collective-permute-start(bf16[4,256,128]{2,1,0:T(8,128)(2,1)S(1)} %dynamic-slice_bitcast_fusion), channel_id=1, source_target_pairs={{0,1},{1,0},{2,3},{3,2},{4,5},{5,4},{6,7},{7,6},{8,9},{9,8},{10,11... | collective-permute-start | bytes 786440 | tf_op jit(solution)/shard_map/ppermute | solution.py:207
  27.4 0.0 copy-start.1
  27.4 0.0 copy-done.2
  27.4 0.6 copy-done.1
  28.1 0.8 shard_map.56.table_ref
  28.9 0.0 collective-permute-done.sibling_ref
  28.9 0.0 all-to-all-done.own_ref
  28.9 1.5 %shard_map.58 = bf16[32,2,16,128]{3,2,1,0:T(8,128)(2,1)} custom-call(s32[32]{0:T(128)S(1)} %copy-done.1, s32[6,256]{1,0:T(8,128)S(1)} %shard_map.56.table_ref, bf16[16,2,16,128]{3,2,1,0:T(8,128)(2,1)S(1)} %all-to-all-done.own_ref), custom_call_target="tpu_custom_call" | custom-call | tf_op jit(solution)/shard_map/pallas_call | solution.py:219
  30.4 9.7 %all-to-all-start.1 = ((bf16[32,2,16,128]{3,2,1,0:T(8,128)(2,1)}), bf16[32,2,16,128]{3,2,1,0:T(8,128)(2,1)S(1)}, u32[]{:S(2)}, u32[]{:S(2)}) async-start(bf16[32,2,16,128]{3,2,1,0:T(8,128)(2,1)} %shard_map.58), calls=%async_computation.1 | async-start | bytes 524288 | tf_op jit(solution)/shard_map/all_to_all | solution.py:227
  40.1 3.0 %collective-permute-start.1 = (bf16[2,256,128]{2,1,0:T(8,128)(2,1)S(1)}, bf16[2,256,128]{2,1,0:T(8,128)(2,1)S(1)}, u32[]{:S(2)}, u32[]{:S(2)}) collective-permute-start(bf16[2,256,128]{2,1,0:T(8,128)(2,1)S(1)} %get-tuple-element.40), channel_id=1, source_target_pairs={{0,4},{1,5},{2,6},{3,7},{4,0},{5,1},{6,2},{7,3},{8,12},{9,13},{10,... | collective-permute-start | bytes 393224 | tf_op jit(solution)/shard_map/ppermute | solution.py:231
  43.1 3.3 %collective-permute-start.2 = (bf16[2,256,128]{2,1,0:T(8,128)(2,1)S(1)}, bf16[2,256,128]{2,1,0:T(8,128)(2,1)S(1)}, u32[]{:S(2)}, u32[]{:S(2)}) collective-permute-start(bf16[2,256,128]{2,1,0:T(8,128)(2,1)S(1)} %get-tuple-element.41), channel_id=1, source_target_pairs={{0,6},{1,7},{2,4},{3,5},{4,2},{5,3},{6,0},{7,1},{8,14},{9,15},{10,... | collective-permute-start | bytes 393224 | tf_op jit(solution)/shard_map/ppermute | solution.py:231
  46.4 2.1 %collective-permute-start.3 = (bf16[2,256,128]{2,1,0:T(8,128)(2,1)S(1)}, bf16[2,256,128]{2,1,0:T(8,128)(2,1)S(1)}, u32[]{:S(2)}, u32[]{:S(2)}) collective-permute-start(bf16[2,256,128]{2,1,0:T(8,128)(2,1)S(1)} %get-tuple-element.42), channel_id=1, source_target_pairs={{0,2},{1,3},{2,0},{3,1},{4,6},{5,7},{6,4},{7,5},{8,10},{9,11},{10,... | collective-permute-start | bytes 393224 | tf_op jit(solution)/shard_map/ppermute | solution.py:231
  48.5 4.6 %collective-permute-done.1.refs_2_ = bf16[2,256,128]{2,1,0:T(8,128)(2,1)S(1)} collective-permute-done((bf16[2,256,128]{2,1,0:T(8,128)(2,1)S(1)}, bf16[2,256,128]{2,1,0:T(8,128)(2,1)S(1)}, u32[]{:S(2)}, u32[]{:S(2)}) %collective-permute-start.1) | collective-permute-done | bytes 131104 | tf_op jit(solution)/shard_map/ppermute | solution.py:231
  53.1 0.0 collective-permute-done.2.refs_3_
  53.1 3.7 %collective-permute-done.3.refs_1_ = bf16[2,256,128]{2,1,0:T(8,128)(2,1)S(1)} collective-permute-done((bf16[2,256,128]{2,1,0:T(8,128)(2,1)S(1)}, bf16[2,256,128]{2,1,0:T(8,128)(2,1)S(1)}, u32[]{:S(2)}, u32[]{:S(2)}) %collective-permute-start.3) | collective-permute-done | bytes 131104 | tf_op jit(solution)/shard_map/ppermute | solution.py:231
  56.7 0.0 all-to-all-done.1.foreign_ref
  56.7 1.0 %shard_map.59 = bf16[64,2,16,128]{3,2,1,0:T(8,128)(2,1)S(1)} custom-call(s32[1]{0:T(128)} %bitcast.me_ref, s32[32]{0:T(128)S(1)} %copy-done.1, s32[6,256]{1,0:T(8,128)S(1)} %shard_map.56.table_ref, bf16[16,2,16,128]{3,2,1,0:T(8,128)(2,1)S(1)} %all-to-all-done.own_ref, bf16[32,2,16,128]{3,2,1,0:T(8,128)(2,1)S(1)} %all-to-all-done.1.foreign_ref), custom_call_target="tpu_custom_call" | custom-call | tf_op jit(solution)/shard_map/pallas_call | solution.py:238
  57.7 16.8 %all_to_all.20 = bf16[64,2,16,128]{3,2,1,0:T(8,128)(2,1)S(1)} all-to-all(bf16[64,2,16,128]{3,2,1,0:T(8,128)(2,1)S(1)} %shard_map.59), channel_id=1, replica_groups={{2,3,0,1,6,7,4,5},{10,11,8,9,14,15,12,13},{18,19,16,17,22,23,20,21},{26..., dimensions={0} | all-to-all | bytes 1048576 | tf_op jit(solution)/shard_map/all_to_all | solution.py:245
  74.6 2.3 %shard_map.60 = bf16[8,256,128]{2,1,0:T(8,128)(2,1)S(1)} custom-call(s32[1]{0:T(128)} %bitcast.me_ref, s32[1]{0:T(128)} %bitcast.1.rank_ref, s32[32]{0:T(128)S(1)} %copy-done.1, bf16[2,256,128]{2,1,0:T(8,128)(2,1)S(1)} %get-tuple-element.39.refs_0_, bf16[2,256,128]{2,1,0:T(8,128)(2,1)S(1)} %collective-permute-done.3.refs_1_, ...), custom_call_target="tpu_custom_call" | custom-call | tf_op jit(solution)/shard_map/pallas_call | solution.py:248
  76.9 17.0 %all_to_all.21 = bf16[8,256,128]{2,1,0:T(8,128)(2,1)S(1)} all-to-all(bf16[8,256,128]{2,1,0:T(8,128)(2,1)S(1)} %shard_map.60), channel_id=1, replica_groups={{2,3,0,1,6,7,4,5},{10,11,8,9,14,15,12,13},{18,19,16,17,22,23,20,21},{26..., dimensions={0} | all-to-all | bytes 1048576 | tf_op jit(solution)/shard_map/all_to_all | solution.py:257
  93.9 0.8 copy.9
  (2 shorter events, 0.1 us)
Async XLA Ops:
  0.0 13.8 %copy-start = (bf16[2048,1,128]{2,0,1:T(8,128)(2,1)S(1)}, bf16[2048,1,128]{2,0,1:T(8,128)(2,1)}, u32[]{:S(2)}) copy-start(bf16[2048,1,128]{2,0,1:T(8,128)(2,1)} %param.5) | copy-start | bytes 1572868
  1.6 27.3 %all-to-all-start = ((bf16[16,2,16,128]{3,2,1,0:T(8,128)(2,1)}), bf16[16,2,16,128]{3,2,1,0:T(8,128)(2,1)S(1)}, u32[]{:S(2)}, u32[]{:S(2)}) async-start(bf16[16,2,16,128]{3,2,1,0:T(8,128)(2,1)} %shard_map.55), calls=%async_computation | async-start | bytes 262144 | tf_op jit(solution)/shard_map/all_to_all | solution.py:193
  13.9 13.5 %copy-start.2 = (s32[256,4]{0,1:T(4,128)S(1)}, s32[256,4]{0,1:T(4,128)}, u32[]{:S(2)}) copy-start(s32[256,4]{0,1:T(4,128)} %param.8) | copy-start | bytes 12292
  13.9 15.0 %collective-permute-start = (bf16[4,256,128]{2,1,0:T(8,128)(2,1)S(1)}, bf16[4,256,128]{2,1,0:T(8,128)(2,1)S(1)}, u32[]{:S(2)}, u32[]{:S(2)}) collective-permute-start(bf16[4,256,128]{2,1,0:T(8,128)(2,1)S(1)} %dynamic-slice_bitcast_fusion), channel_id=1, source_target_pairs={{0,1},{1,0},{2,3},{3,2},{4,5},{5,4},{6,7},{7,6},{8,9},{9,8},{10,11... | collective-permute-start | bytes 786440 | tf_op jit(solution)/shard_map/ppermute | solution.py:207
  27.4 0.7 copy-start.1
  30.4 26.3 %all-to-all-start.1 = ((bf16[32,2,16,128]{3,2,1,0:T(8,128)(2,1)}), bf16[32,2,16,128]{3,2,1,0:T(8,128)(2,1)S(1)}, u32[]{:S(2)}, u32[]{:S(2)}) async-start(bf16[32,2,16,128]{3,2,1,0:T(8,128)(2,1)} %shard_map.58), calls=%async_computation.1 | async-start | bytes 524288 | tf_op jit(solution)/shard_map/all_to_all | solution.py:227
  40.1 12.9 %collective-permute-start.1 = (bf16[2,256,128]{2,1,0:T(8,128)(2,1)S(1)}, bf16[2,256,128]{2,1,0:T(8,128)(2,1)S(1)}, u32[]{:S(2)}, u32[]{:S(2)}) collective-permute-start(bf16[2,256,128]{2,1,0:T(8,128)(2,1)S(1)} %get-tuple-element.40), channel_id=1, source_target_pairs={{0,4},{1,5},{2,6},{3,7},{4,0},{5,1},{6,2},{7,3},{8,12},{9,13},{10,... | collective-permute-start | bytes 393224 | tf_op jit(solution)/shard_map/ppermute | solution.py:231
  43.1 10.0 %collective-permute-start.2 = (bf16[2,256,128]{2,1,0:T(8,128)(2,1)S(1)}, bf16[2,256,128]{2,1,0:T(8,128)(2,1)S(1)}, u32[]{:S(2)}, u32[]{:S(2)}) collective-permute-start(bf16[2,256,128]{2,1,0:T(8,128)(2,1)S(1)} %get-tuple-element.41), channel_id=1, source_target_pairs={{0,6},{1,7},{2,4},{3,5},{4,2},{5,3},{6,0},{7,1},{8,14},{9,15},{10,... | collective-permute-start | bytes 393224 | tf_op jit(solution)/shard_map/ppermute | solution.py:231
  46.4 10.3 %collective-permute-start.3 = (bf16[2,256,128]{2,1,0:T(8,128)(2,1)S(1)}, bf16[2,256,128]{2,1,0:T(8,128)(2,1)S(1)}, u32[]{:S(2)}, u32[]{:S(2)}) collective-permute-start(bf16[2,256,128]{2,1,0:T(8,128)(2,1)S(1)} %get-tuple-element.42), channel_id=1, source_target_pairs={{0,2},{1,3},{2,0},{3,1},{4,6},{5,7},{6,4},{7,5},{8,10},{9,11},{10,... | collective-permute-start | bytes 393224 | tf_op jit(solution)/shard_map/ppermute | solution.py:231

commit v9 on v8

--- a/solution.py
+++ b/solution.py
@@ -172,7 +172,7 @@
     bf16 = jnp.bfloat16
     me = lax.axis_index("ctx").astype(i32)
     spread_lead = block_count // 2 + block_count // 8
-    ctx_lead = ctx_count // 2 + ctx_count // 4
+    ctx_lead = ctx_count - 2
     group_lead = 2
     rank = lax.rem(lax.axis_index("head").astype(i32), group) ^ group_lead
     piece = (2, piece_rows, width)

time: 95.2 us -> 94.2 us (0.989)
  no operation moved by 1% of the time
where the time goes in v9:
time: 94.2 us; the launch traced here: 93.7 us
  starting transfers between devices  42.9 us (46%)
  blocking collectives  33.8 us (36%)
  waiting for transfers between devices  8.25 us (9%)
  Pallas kernels  7.29 us (8%)
  local copies, waits for them, and re-layouts  1.47 us (2%)
    all_to_all x1, blocking collectives, body(): lax.all_to_all(done, 'head', 0, 0, tiled=True, axis_index_groups=kv_groups)  17 us
    all_to_all x1, blocking collectives, body(): lax.all_to_all(pairs, 'head', 0, 0, tiled=True, axis_index_groups=kv_groups)  16.8 us
    ppermute x1, starting transfers between devices, body(): lax.ppermute(crossing, 'head', [(i, i ^ 1) for i in range(head_count)])  13.5 us
    all_to_all x1, starting transfers between devices, body(): lax.all_to_all(kv, 'head', 0, 0, tiled=True, axis_index_groups=spread_gro...  12.2 us
    all_to_all x1, starting transfers between devices, body(): lax.all_to_all(asked, 'ctx', 0, 0, tiled=True, axis_index_groups=ctx_groups)  8.8 us
    ppermute x3, starting transfers between devices, body(): lax.ppermute(bundles[k], 'head', [(i, i ^ 2 * k) for i in range(head_coun...  8.36 us
    ppermute x3, waiting for transfers between devices, body(): lax.ppermute(bundles[k], 'head', [(i, i ^ 2 * k) for i in range(head_coun...  8.24 us
    pallas_call x1, Pallas kernels, body(): pl.pallas_call(functools.partial(attend, per_span, group_lead), out_shape...  2.3 us
  transfers between devices with their start and end apart: 6, of which 2 were waited for; matrix products, arithmetic and copies ran while one was open for 0% of the time, Pallas kernels for 1%

profile of v9, /device:TPU:1, one launch (start us, length us, event | category | flops | bytes accessed | tf_op | source)
XLA Modules:
  0.0 93.7 jit_solution(11287378751116865617)
XLA Ops:
  0.0 0.0 copy-start
  0.0 1.6 %shard_map.55 = bf16[16,2,16,128]{3,2,1,0:T(8,128)(2,1)} custom-call(bf16[32,8,128]{2,1,0:T(8,128)(2,1)} %key_ref.1, bf16[32,8,128]{2,1,0:T(8,128)(2,1)} %value_ref.1), custom_call_target="tpu_custom_call" | custom-call | tf_op jit(solution)/shard_map/pallas_call | solution.py:185
  1.6 12.2 %all-to-all-start = ((bf16[16,2,16,128]{3,2,1,0:T(8,128)(2,1)}), bf16[16,2,16,128]{3,2,1,0:T(8,128)(2,1)S(1)}, u32[]{:S(2)}, u32[]{:S(2)}) async-start(bf16[16,2,16,128]{3,2,1,0:T(8,128)(2,1)} %shard_map.55), calls=%async_computation | async-start | bytes 262144 | tf_op jit(solution)/shard_map/all_to_all | solution.py:193
  13.8 0.0 copy-done
  13.9 0.0 copy-start.2
  13.9 13.5 %collective-permute-start = (bf16[4,256,128]{2,1,0:T(8,128)(2,1)S(1)}, bf16[4,256,128]{2,1,0:T(8,128)(2,1)S(1)}, u32[]{:S(2)}, u32[]{:S(2)}) collective-permute-start(bf16[4,256,128]{2,1,0:T(8,128)(2,1)S(1)} %dynamic-slice_bitcast_fusion), channel_id=1, source_target_pairs={{0,1},{1,0},{2,3},{3,2},{4,5},{5,4},{6,7},{7,6},{8,9},{9,8},{10,11... | collective-permute-start | bytes 786440 | tf_op jit(solution)/shard_map/ppermute | solution.py:207
  27.4 0.0 copy-start.1
  27.4 0.0 copy-done.2
  27.4 0.6 copy-done.1
  28.1 0.8 shard_map.56.table_ref
  28.9 0.0 collective-permute-done.sibling_ref
  28.9 0.0 all-to-all-done.own_ref
  28.9 1.5 %shard_map.58 = bf16[32,2,16,128]{3,2,1,0:T(8,128)(2,1)} custom-call(s32[32]{0:T(128)S(1)} %copy-done.1, s32[6,256]{1,0:T(8,128)S(1)} %shard_map.56.table_ref, bf16[16,2,16,128]{3,2,1,0:T(8,128)(2,1)S(1)} %all-to-all-done.own_ref), custom_call_target="tpu_custom_call" | custom-call | tf_op jit(solution)/shard_map/pallas_call | solution.py:219
  30.4 8.8 %all-to-all-start.1 = ((bf16[32,2,16,128]{3,2,1,0:T(8,128)(2,1)}), bf16[32,2,16,128]{3,2,1,0:T(8,128)(2,1)S(1)}, u32[]{:S(2)}, u32[]{:S(2)}) async-start(bf16[32,2,16,128]{3,2,1,0:T(8,128)(2,1)} %shard_map.58), calls=%async_computation.1 | async-start | bytes 524288 | tf_op jit(solution)/shard_map/all_to_all | solution.py:227
  39.2 3.0 %collective-permute-start.1 = (bf16[2,256,128]{2,1,0:T(8,128)(2,1)S(1)}, bf16[2,256,128]{2,1,0:T(8,128)(2,1)S(1)}, u32[]{:S(2)}, u32[]{:S(2)}) collective-permute-start(bf16[2,256,128]{2,1,0:T(8,128)(2,1)S(1)} %get-tuple-element.40), channel_id=1, source_target_pairs={{0,4},{1,5},{2,6},{3,7},{4,0},{5,1},{6,2},{7,3},{8,12},{9,13},{10,... | collective-permute-start | bytes 393224 | tf_op jit(solution)/shard_map/ppermute | solution.py:231
  42.2 3.3 %collective-permute-start.2 = (bf16[2,256,128]{2,1,0:T(8,128)(2,1)S(1)}, bf16[2,256,128]{2,1,0:T(8,128)(2,1)S(1)}, u32[]{:S(2)}, u32[]{:S(2)}) collective-permute-start(bf16[2,256,128]{2,1,0:T(8,128)(2,1)S(1)} %get-tuple-element.41), channel_id=1, source_target_pairs={{0,6},{1,7},{2,4},{3,5},{4,2},{5,3},{6,0},{7,1},{8,14},{9,15},{10,... | collective-permute-start | bytes 393224 | tf_op jit(solution)/shard_map/ppermute | solution.py:231
  45.5 2.1 %collective-permute-start.3 = (bf16[2,256,128]{2,1,0:T(8,128)(2,1)S(1)}, bf16[2,256,128]{2,1,0:T(8,128)(2,1)S(1)}, u32[]{:S(2)}, u32[]{:S(2)}) collective-permute-start(bf16[2,256,128]{2,1,0:T(8,128)(2,1)S(1)} %get-tuple-element.42), channel_id=1, source_target_pairs={{0,2},{1,3},{2,0},{3,1},{4,6},{5,7},{6,4},{7,5},{8,10},{9,11},{10,... | collective-permute-start | bytes 393224 | tf_op jit(solution)/shard_map/ppermute | solution.py:231
  47.6 4.8 %collective-permute-done.1.refs_2_ = bf16[2,256,128]{2,1,0:T(8,128)(2,1)S(1)} collective-permute-done((bf16[2,256,128]{2,1,0:T(8,128)(2,1)S(1)}, bf16[2,256,128]{2,1,0:T(8,128)(2,1)S(1)}, u32[]{:S(2)}, u32[]{:S(2)}) %collective-permute-start.1) | collective-permute-done | bytes 131104 | tf_op jit(solution)/shard_map/ppermute | solution.py:231
  52.4 0.0 collective-permute-done.2.refs_3_
  52.4 3.5 %collective-permute-done.3.refs_1_ = bf16[2,256,128]{2,1,0:T(8,128)(2,1)S(1)} collective-permute-done((bf16[2,256,128]{2,1,0:T(8,128)(2,1)S(1)}, bf16[2,256,128]{2,1,0:T(8,128)(2,1)S(1)}, u32[]{:S(2)}, u32[]{:S(2)}) %collective-permute-start.3) | collective-permute-done | bytes 131104 | tf_op jit(solution)/shard_map/ppermute | solution.py:231
  55.9 0.0 all-to-all-done.1.foreign_ref
  55.9 1.0 %shard_map.59 = bf16[64,2,16,128]{3,2,1,0:T(8,128)(2,1)S(1)} custom-call(s32[1]{0:T(128)} %bitcast.me_ref, s32[32]{0:T(128)S(1)} %copy-done.1, s32[6,256]{1,0:T(8,128)S(1)} %shard_map.56.table_ref, bf16[16,2,16,128]{3,2,1,0:T(8,128)(2,1)S(1)} %all-to-all-done.own_ref, bf16[32,2,16,128]{3,2,1,0:T(8,128)(2,1)S(1)} %all-to-all-done.1.foreign_ref), custom_call_target="tpu_custom_call" | custom-call | tf_op jit(solution)/shard_map/pallas_call | solution.py:238
  56.9 16.8 %all_to_all.20 = bf16[64,2,16,128]{3,2,1,0:T(8,128)(2,1)S(1)} all-to-all(bf16[64,2,16,128]{3,2,1,0:T(8,128)(2,1)S(1)} %shard_map.59), channel_id=1, replica_groups={{2,3,0,1,6,7,4,5},{10,11,8,9,14,15,12,13},{18,19,16,17,22,23,20,21},{26..., dimensions={0} | all-to-all | bytes 1048576 | tf_op jit(solution)/shard_map/all_to_all | solution.py:245
  73.6 2.3 %shard_map.60 = bf16[8,256,128]{2,1,0:T(8,128)(2,1)S(1)} custom-call(s32[1]{0:T(128)} %bitcast.me_ref, s32[1]{0:T(128)} %bitcast.1.rank_ref, s32[32]{0:T(128)S(1)} %copy-done.1, bf16[2,256,128]{2,1,0:T(8,128)(2,1)S(1)} %get-tuple-element.39.refs_0_, bf16[2,256,128]{2,1,0:T(8,128)(2,1)S(1)} %collective-permute-done.3.refs_1_, ...), custom_call_target="tpu_custom_call" | custom-call | tf_op jit(solution)/shard_map/pallas_call | solution.py:248
  75.9 17.0 %all_to_all.21 = bf16[8,256,128]{2,1,0:T(8,128)(2,1)S(1)} all-to-all(bf16[8,256,128]{2,1,0:T(8,128)(2,1)S(1)} %shard_map.60), channel_id=1, replica_groups={{2,3,0,1,6,7,4,5},{10,11,8,9,14,15,12,13},{18,19,16,17,22,23,20,21},{26..., dimensions={0} | all-to-all | bytes 1048576 | tf_op jit(solution)/shard_map/all_to_all | solution.py:257
  92.9 0.8 copy.9
  (2 shorter events, 0.1 us)
Async XLA Ops:
  0.0 13.8 %copy-start = (bf16[2048,1,128]{2,0,1:T(8,128)(2,1)S(1)}, bf16[2048,1,128]{2,0,1:T(8,128)(2,1)}, u32[]{:S(2)}) copy-start(bf16[2048,1,128]{2,0,1:T(8,128)(2,1)} %param.5) | copy-start | bytes 1572868
  1.6 27.3 %all-to-all-start = ((bf16[16,2,16,128]{3,2,1,0:T(8,128)(2,1)}), bf16[16,2,16,128]{3,2,1,0:T(8,128)(2,1)S(1)}, u32[]{:S(2)}, u32[]{:S(2)}) async-start(bf16[16,2,16,128]{3,2,1,0:T(8,128)(2,1)} %shard_map.55), calls=%async_computation | async-start | bytes 262144 | tf_op jit(solution)/shard_map/all_to_all | solution.py:193
  13.9 13.5 %copy-start.2 = (s32[256,4]{0,1:T(4,128)S(1)}, s32[256,4]{0,1:T(4,128)}, u32[]{:S(2)}) copy-start(s32[256,4]{0,1:T(4,128)} %param.8) | copy-start | bytes 12292
  13.9 15.0 %collective-permute-start = (bf16[4,256,128]{2,1,0:T(8,128)(2,1)S(1)}, bf16[4,256,128]{2,1,0:T(8,128)(2,1)S(1)}, u32[]{:S(2)}, u32[]{:S(2)}) collective-permute-start(bf16[4,256,128]{2,1,0:T(8,128)(2,1)S(1)} %dynamic-slice_bitcast_fusion), channel_id=1, source_target_pairs={{0,1},{1,0},{2,3},{3,2},{4,5},{5,4},{6,7},{7,6},{8,9},{9,8},{10,11... | collective-permute-start | bytes 786440 | tf_op jit(solution)/shard_map/ppermute | solution.py:207
  27.4 0.7 copy-start.1
  30.4 25.4 %all-to-all-start.1 = ((bf16[32,2,16,128]{3,2,1,0:T(8,128)(2,1)}), bf16[32,2,16,128]{3,2,1,0:T(8,128)(2,1)S(1)}, u32[]{:S(2)}, u32[]{:S(2)}) async-start(bf16[32,2,16,128]{3,2,1,0:T(8,128)(2,1)} %shard_map.58), calls=%async_computation.1 | async-start | bytes 524288 | tf_op jit(solution)/shard_map/all_to_all | solution.py:227
  39.2 13.2 %collective-permute-start.1 = (bf16[2,256,128]{2,1,0:T(8,128)(2,1)S(1)}, bf16[2,256,128]{2,1,0:T(8,128)(2,1)S(1)}, u32[]{:S(2)}, u32[]{:S(2)}) collective-permute-start(bf16[2,256,128]{2,1,0:T(8,128)(2,1)S(1)} %get-tuple-element.40), channel_id=1, source_target_pairs={{0,4},{1,5},{2,6},{3,7},{4,0},{5,1},{6,2},{7,3},{8,12},{9,13},{10,... | collective-permute-start | bytes 393224 | tf_op jit(solution)/shard_map/ppermute | solution.py:231
  42.2 10.2 %collective-permute-start.2 = (bf16[2,256,128]{2,1,0:T(8,128)(2,1)S(1)}, bf16[2,256,128]{2,1,0:T(8,128)(2,1)S(1)}, u32[]{:S(2)}, u32[]{:S(2)}) collective-permute-start(bf16[2,256,128]{2,1,0:T(8,128)(2,1)S(1)} %get-tuple-element.41), channel_id=1, source_target_pairs={{0,6},{1,7},{2,4},{3,5},{4,2},{5,3},{6,0},{7,1},{8,14},{9,15},{10,... | collective-permute-start | bytes 393224 | tf_op jit(solution)/shard_map/ppermute | solution.py:231
  45.5 10.3 %collective-permute-start.3 = (bf16[2,256,128]{2,1,0:T(8,128)(2,1)S(1)}, bf16[2,256,128]{2,1,0:T(8,128)(2,1)S(1)}, u32[]{:S(2)}, u32[]{:S(2)}) collective-permute-start(bf16[2,256,128]{2,1,0:T(8,128)(2,1)S(1)} %get-tuple-element.42), channel_id=1, source_target_pairs={{0,2},{1,3},{2,0},{3,1},{4,6},{5,7},{6,4},{7,5},{8,10},{9,11},{10,... | collective-permute-start | bytes 393224 | tf_op jit(solution)/shard_map/ppermute | solution.py:231

commit v10 on v9

--- a/solution.py
+++ b/solution.py
@@ -117,7 +117,8 @@
     col = lax.broadcasted_iota(jnp.int32, (BLK, BLK), 1)
     piece = (col // rows) ^ lead
     half = pieces // 2
-    causal = 2 * rows * (piece % half) + rows * (piece // half) + col % rows <= row
+    key_row = 2 * rows * (piece % half) + rows * (piece // half) + col % rows
+    causal = (key_row ^ rank_ref[1]) <= row
     causal = jnp.concatenate([causal, causal], axis=0)
     for b in range(blocks):
         for j in range(slots):
@@ -175,11 +176,17 @@
     ctx_lead = ctx_count - 2
     group_lead = 2
     rank = lax.rem(lax.axis_index("head").astype(i32), group) ^ group_lead
+    line = lax.div(lax.axis_index("head").astype(i32), group)
+    turn = (lax.rem(line, 2) ^ lax.rem(rank, 2)) * (BLK // 2)
+    ranks = jnp.stack([rank, turn])
     piece = (2, piece_rows, width)
     listed = key_blocks.T
 
     spread_groups = [
-        [shards_per_block * (j ^ spread_lead) + q for j in range(block_count)]
+        [
+            shards_per_block * j + (q ^ (j // halves % 2 * halves))
+            for j in (i ^ spread_lead for i in range(block_count))
+        ]
         for q in range(shards_per_block)
     ]
     kv = pl.pallas_call(
@@ -212,7 +219,7 @@
         in_specs=[SMEM, VMEM, VMEM],
         out_specs=(VMEM,) * chips,
         compiler_params=small(8),
-    )(rank[None], query_parts.reshape(group, rows_device // group, width), sibling)
+    )(ranks, query_parts.reshape(group, rows_device // group, width), sibling)
 
     own, table, bundles = lax.optimization_barrier((own, table, bundles))
 
@@ -252,7 +259,7 @@
         out_specs=VMEM,
         scratch_shapes=[pltpu.VMEM((per_rank, slot_count * BLK, width), bf16)] * 2,
         compiler_params=small(24),
-    )(me[None], rank[None], span_order, *query_here, pairs)
+    )(me[None], ranks, span_order, *query_here, pairs)
 
     out = lax.all_to_all(done, "head", 0, 0, tiled=True, axis_index_groups=kv_groups)
     return out.reshape(rows_device, 1, width)

time: 94.2 us -> 94.6 us (level)
  no operation moved by 1% of the time
where the time goes in v10:
time: 94.6 us; the launch traced here: 93.9 us
  starting transfers between devices  42.6 us (45%)
  blocking collectives  34.2 us (36%)
  Pallas kernels  7.82 us (8%)
  waiting for transfers between devices  7.63 us (8%)
  local copies, waits for them, and re-layouts  1.47 us (2%)
    all_to_all x1, blocking collectives, body(): lax.all_to_all(pairs, 'head', 0, 0, tiled=True, axis_index_groups=kv_groups)  17.2 us
    all_to_all x1, blocking collectives, body(): lax.all_to_all(done, 'head', 0, 0, tiled=True, axis_index_groups=kv_groups)  17 us
    ppermute x1, starting transfers between devices, body(): lax.ppermute(crossing, 'head', [(i, i ^ 1) for i in range(head_count)])  13.4 us
    all_to_all x1, starting transfers between devices, body(): lax.all_to_all(kv, 'head', 0, 0, tiled=True, axis_index_groups=spread_gro...  11.4 us
    all_to_all x1, starting transfers between devices, body(): lax.all_to_all(asked, 'ctx', 0, 0, tiled=True, axis_index_groups=ctx_groups)  8.92 us
    ppermute x3, starting transfers between devices, body(): lax.ppermute(bundles[k], 'head', [(i, i ^ 2 * k) for i in range(head_coun...  8.88 us
    ppermute x3, waiting for transfers between devices, body(): lax.ppermute(bundles[k], 'head', [(i, i ^ 2 * k) for i in range(head_coun...  7.63 us
    pallas_call x1, Pallas kernels, body(): pl.pallas_call(functools.partial(attend, per_span, group_lead), out_shape...  2.29 us
  transfers between devices with their start and end apart: 6, of which 2 were waited for; matrix products, arithmetic and copies ran while one was open for 0% of the time, Pallas kernels for 1%

profile of v10, /device:TPU:1, one launch (start us, length us, event | category | flops | bytes accessed | tf_op | source)
XLA Modules:
  0.0 93.9 jit_solution(15088455459038599884)
XLA Ops:
  0.0 0.0 copy-start
  0.0 1.6 %shard_map.55 = bf16[16,2,16,128]{3,2,1,0:T(8,128)(2,1)} custom-call(bf16[32,8,128]{2,1,0:T(8,128)(2,1)} %key_ref.1, bf16[32,8,128]{2,1,0:T(8,128)(2,1)} %value_ref.1), custom_call_target="tpu_custom_call" | custom-call | tf_op jit(solution)/shard_map/pallas_call | solution.py:192
  1.6 11.4 %all-to-all-start = ((bf16[16,2,16,128]{3,2,1,0:T(8,128)(2,1)}), bf16[16,2,16,128]{3,2,1,0:T(8,128)(2,1)S(1)}, u32[]{:S(2)}, u32[]{:S(2)}) async-start(bf16[16,2,16,128]{3,2,1,0:T(8,128)(2,1)} %shard_map.55), calls=%async_computation | async-start | bytes 262144 | tf_op jit(solution)/shard_map/all_to_all | solution.py:200
  13.1 0.0 copy-done
  13.1 0.0 copy-start.2
  13.1 13.4 %collective-permute-start = (bf16[4,256,128]{2,1,0:T(8,128)(2,1)S(1)}, bf16[4,256,128]{2,1,0:T(8,128)(2,1)S(1)}, u32[]{:S(2)}, u32[]{:S(2)}) collective-permute-start(bf16[4,256,128]{2,1,0:T(8,128)(2,1)S(1)} %dynamic-slice_bitcast_fusion), channel_id=1, source_target_pairs={{0,1},{1,0},{2,3},{3,2},{4,5},{5,4},{6,7},{7,6},{8,9},{9,8},{10,11... | collective-permute-start | bytes 786440 | tf_op jit(solution)/shard_map/ppermute | solution.py:214
  26.5 0.0 copy-start.1
  26.5 0.0 copy-done.2
  26.5 0.6 copy-done.1
  27.2 0.8 shard_map.56.table_ref
  28.0 0.1 pad_add_fusion.rank_ref
  28.0 0.0 collective-permute-done.sibling_ref
  28.0 0.6 shard_map.57
  28.6 0.0 all-to-all-done.own_ref
  28.7 1.5 %shard_map.58 = bf16[32,2,16,128]{3,2,1,0:T(8,128)(2,1)} custom-call(s32[32]{0:T(128)S(1)} %copy-done.1, s32[6,256]{1,0:T(8,128)S(1)} %shard_map.56.table_ref, bf16[16,2,16,128]{3,2,1,0:T(8,128)(2,1)S(1)} %all-to-all-done.own_ref), custom_call_target="tpu_custom_call" | custom-call | tf_op jit(solution)/shard_map/pallas_call | solution.py:226
  30.2 8.9 %all-to-all-start.1 = ((bf16[32,2,16,128]{3,2,1,0:T(8,128)(2,1)}), bf16[32,2,16,128]{3,2,1,0:T(8,128)(2,1)S(1)}, u32[]{:S(2)}, u32[]{:S(2)}) async-start(bf16[32,2,16,128]{3,2,1,0:T(8,128)(2,1)} %shard_map.58), calls=%async_computation.1 | async-start | bytes 524288 | tf_op jit(solution)/shard_map/all_to_all | solution.py:234
  39.1 3.1 %collective-permute-start.1 = (bf16[2,256,128]{2,1,0:T(8,128)(2,1)S(1)}, bf16[2,256,128]{2,1,0:T(8,128)(2,1)S(1)}, u32[]{:S(2)}, u32[]{:S(2)}) collective-permute-start(bf16[2,256,128]{2,1,0:T(8,128)(2,1)S(1)} %get-tuple-element.40), channel_id=1, source_target_pairs={{0,4},{1,5},{2,6},{3,7},{4,0},{5,1},{6,2},{7,3},{8,12},{9,13},{10,... | collective-permute-start | bytes 393224 | tf_op jit(solution)/shard_map/ppermute | solution.py:238
  42.2 3.9 %collective-permute-start.2 = (bf16[2,256,128]{2,1,0:T(8,128)(2,1)S(1)}, bf16[2,256,128]{2,1,0:T(8,128)(2,1)S(1)}, u32[]{:S(2)}, u32[]{:S(2)}) collective-permute-start(bf16[2,256,128]{2,1,0:T(8,128)(2,1)S(1)} %get-tuple-element.41), channel_id=1, source_target_pairs={{0,6},{1,7},{2,4},{3,5},{4,2},{5,3},{6,0},{7,1},{8,14},{9,15},{10,... | collective-permute-start | bytes 393224 | tf_op jit(solution)/shard_map/ppermute | solution.py:238
  46.1 1.9 %collective-permute-start.3 = (bf16[2,256,128]{2,1,0:T(8,128)(2,1)S(1)}, bf16[2,256,128]{2,1,0:T(8,128)(2,1)S(1)}, u32[]{:S(2)}, u32[]{:S(2)}) collective-permute-start(bf16[2,256,128]{2,1,0:T(8,128)(2,1)S(1)} %get-tuple-element.42), channel_id=1, source_target_pairs={{0,2},{1,3},{2,0},{3,1},{4,6},{5,7},{6,4},{7,5},{8,10},{9,11},{10,... | collective-permute-start | bytes 393224 | tf_op jit(solution)/shard_map/ppermute | solution.py:238
  48.0 3.2 %collective-permute-done.1.refs_2_ = bf16[2,256,128]{2,1,0:T(8,128)(2,1)S(1)} collective-permute-done((bf16[2,256,128]{2,1,0:T(8,128)(2,1)S(1)}, bf16[2,256,128]{2,1,0:T(8,128)(2,1)S(1)}, u32[]{:S(2)}, u32[]{:S(2)}) %collective-permute-start.1) | collective-permute-done | bytes 131104 | tf_op jit(solution)/shard_map/ppermute | solution.py:238
  51.2 0.0 collective-permute-done.2.refs_3_
  51.2 4.4 %collective-permute-done.3.refs_1_ = bf16[2,256,128]{2,1,0:T(8,128)(2,1)S(1)} collective-permute-done((bf16[2,256,128]{2,1,0:T(8,128)(2,1)S(1)}, bf16[2,256,128]{2,1,0:T(8,128)(2,1)S(1)}, u32[]{:S(2)}, u32[]{:S(2)}) %collective-permute-start.3) | collective-permute-done | bytes 131104 | tf_op jit(solution)/shard_map/ppermute | solution.py:238
  55.6 0.0 all-to-all-done.1.foreign_ref
  55.6 1.0 %shard_map.59 = bf16[64,2,16,128]{3,2,1,0:T(8,128)(2,1)S(1)} custom-call(s32[1]{0:T(128)} %bitcast.me_ref, s32[32]{0:T(128)S(1)} %copy-done.1, s32[6,256]{1,0:T(8,128)S(1)} %shard_map.56.table_ref, bf16[16,2,16,128]{3,2,1,0:T(8,128)(2,1)S(1)} %all-to-all-done.own_ref, bf16[32,2,16,128]{3,2,1,0:T(8,128)(2,1)S(1)} %all-to-all-done.1.foreign_ref), custom_call_target="tpu_custom_call" | custom-call | tf_op jit(solution)/shard_map/pallas_call | solution.py:245
  56.6 17.2 %all_to_all.20 = bf16[64,2,16,128]{3,2,1,0:T(8,128)(2,1)S(1)} all-to-all(bf16[64,2,16,128]{3,2,1,0:T(8,128)(2,1)S(1)} %shard_map.59), channel_id=1, replica_groups={{2,3,0,1,6,7,4,5},{10,11,8,9,14,15,12,13},{18,19,16,17,22,23,20,21},{26..., dimensions={0} | all-to-all | bytes 1048576 | tf_op jit(solution)/shard_map/all_to_all | solution.py:252
  73.8 2.3 %shard_map.60 = bf16[8,256,128]{2,1,0:T(8,128)(2,1)S(1)} custom-call(s32[1]{0:T(128)} %bitcast.me_ref, s32[2]{0:T(128)S(1)} %pad_add_fusion.rank_ref, s32[32]{0:T(128)S(1)} %copy-done.1, bf16[2,256,128]{2,1,0:T(8,128)(2,1)S(1)} %get-tuple-element.39.refs_0_, bf16[2,256,128]{2,1,0:T(8,128)(2,1)S(1)} %collective-permute-done.3.refs_1_, ...), custom_call_target="tpu_custom_call" | custom-call | tf_op jit(solution)/shard_map/pallas_call | solution.py:255
  76.1 17.0 %all_to_all.21 = bf16[8,256,128]{2,1,0:T(8,128)(2,1)S(1)} all-to-all(bf16[8,256,128]{2,1,0:T(8,128)(2,1)S(1)} %shard_map.60), channel_id=1, replica_groups={{2,3,0,1,6,7,4,5},{10,11,8,9,14,15,12,13},{18,19,16,17,22,23,20,21},{26..., dimensions={0} | all-to-all | bytes 1048576 | tf_op jit(solution)/shard_map/all_to_all | solution.py:264
  93.1 0.8 copy.9
  (1 shorter events, 0.0 us)
Async XLA Ops:
  0.0 13.1 %copy-start = (bf16[2048,1,128]{2,0,1:T(8,128)(2,1)S(1)}, bf16[2048,1,128]{2,0,1:T(8,128)(2,1)}, u32[]{:S(2)}) copy-start(bf16[2048,1,128]{2,0,1:T(8,128)(2,1)} %param.5) | copy-start | bytes 1572868
  1.6 27.0 %all-to-all-start = ((bf16[16,2,16,128]{3,2,1,0:T(8,128)(2,1)}), bf16[16,2,16,128]{3,2,1,0:T(8,128)(2,1)S(1)}, u32[]{:S(2)}, u32[]{:S(2)}) async-start(bf16[16,2,16,128]{3,2,1,0:T(8,128)(2,1)} %shard_map.55), calls=%async_computation | async-start | bytes 262144 | tf_op jit(solution)/shard_map/all_to_all | solution.py:200
  13.1 13.4 %copy-start.2 = (s32[256,4]{0,1:T(4,128)S(1)}, s32[256,4]{0,1:T(4,128)}, u32[]{:S(2)}) copy-start(s32[256,4]{0,1:T(4,128)} %param.8) | copy-start | bytes 12292
  13.1 14.9 %collective-permute-start = (bf16[4,256,128]{2,1,0:T(8,128)(2,1)S(1)}, bf16[4,256,128]{2,1,0:T(8,128)(2,1)S(1)}, u32[]{:S(2)}, u32[]{:S(2)}) collective-permute-start(bf16[4,256,128]{2,1,0:T(8,128)(2,1)S(1)} %dynamic-slice_bitcast_fusion), channel_id=1, source_target_pairs={{0,1},{1,0},{2,3},{3,2},{4,5},{5,4},{6,7},{7,6},{8,9},{9,8},{10,11... | collective-permute-start | bytes 786440 | tf_op jit(solution)/shard_map/ppermute | solution.py:214
  26.5 0.7 copy-start.1
  30.2 25.4 %all-to-all-start.1 = ((bf16[32,2,16,128]{3,2,1,0:T(8,128)(2,1)}), bf16[32,2,16,128]{3,2,1,0:T(8,128)(2,1)S(1)}, u32[]{:S(2)}, u32[]{:S(2)}) async-start(bf16[32,2,16,128]{3,2,1,0:T(8,128)(2,1)} %shard_map.58), calls=%async_computation.1 | async-start | bytes 524288 | tf_op jit(solution)/shard_map/all_to_all | solution.py:234
  39.1 12.1 %collective-permute-start.1 = (bf16[2,256,128]{2,1,0:T(8,128)(2,1)S(1)}, bf16[2,256,128]{2,1,0:T(8,128)(2,1)S(1)}, u32[]{:S(2)}, u32[]{:S(2)}) collective-permute-start(bf16[2,256,128]{2,1,0:T(8,128)(2,1)S(1)} %get-tuple-element.40), channel_id=1, source_target_pairs={{0,4},{1,5},{2,6},{3,7},{4,0},{5,1},{6,2},{7,3},{8,12},{9,13},{10,... | collective-permute-start | bytes 393224 | tf_op jit(solution)/shard_map/ppermute | solution.py:238
  42.2 9.0 %collective-permute-start.2 = (bf16[2,256,128]{2,1,0:T(8,128)(2,1)S(1)}, bf16[2,256,128]{2,1,0:T(8,128)(2,1)S(1)}, u32[]{:S(2)}, u32[]{:S(2)}) collective-permute-start(bf16[2,256,128]{2,1,0:T(8,128)(2,1)S(1)} %get-tuple-element.41), channel_id=1, source_target_pairs={{0,6},{1,7},{2,4},{3,5},{4,2},{5,3},{6,0},{7,1},{8,14},{9,15},{10,... | collective-permute-start | bytes 393224 | tf_op jit(solution)/shard_map/ppermute | solution.py:238
  46.1 9.6 %collective-permute-start.3 = (bf16[2,256,128]{2,1,0:T(8,128)(2,1)S(1)}, bf16[2,256,128]{2,1,0:T(8,128)(2,1)S(1)}, u32[]{:S(2)}, u32[]{:S(2)}) collective-permute-start(bf16[2,256,128]{2,1,0:T(8,128)(2,1)S(1)} %get-tuple-element.42), channel_id=1, source_target_pairs={{0,2},{1,3},{2,0},{3,1},{4,6},{5,7},{6,4},{7,5},{8,10},{9,11},{10,... | collective-permute-start | bytes 393224 | tf_op jit(solution)/shard_map/ppermute | solution.py:238

commit v11 on v10

--- a/solution.py
+++ b/solution.py
@@ -96,29 +96,32 @@
             out_ref[block * slots + j] = jnp.where(at < own_count, mine, theirs)
 
 
-def bundle(rank_ref, query_ref, sibling_ref, *out_refs):
-    chip = rank_ref[0] // 2
-    core = rank_ref[0] % 2
+def bundle(group, lead, head_ref, query_ref, sibling_ref, *out_refs):
+    rank = head_ref[0] % group ^ lead
+    chip = rank // 2
+    core = rank % 2
     for k, out_ref in enumerate(out_refs):
         to = chip ^ k
         out_ref[0] = query_ref[2 * to + core]
         out_ref[1] = sibling_ref[to]
 
 
-def attend(per_span, lead, me_ref, rank_ref, span_ref, *refs):
+def attend(per_span, group, lead, me_ref, head_ref, span_ref, *refs):
     *query_refs, pair_ref, out_ref, key_all, value_all = refs
     pieces, pair_count, _, rows, width = pair_ref.shape
     blocks = key_all.shape[0]
     slots = pair_count // blocks
     factor = (width ** -0.5) * LOG2E
-    chip = rank_ref[0] // 2
-    core = rank_ref[0] % 2
+    rank = head_ref[0] % group ^ lead
+    chip = rank // 2
+    core = rank % 2
+    turn = (head_ref[0] // group % 2 ^ core) * (BLK // 2)
     row = lax.broadcasted_iota(jnp.int32, (BLK, BLK), 0)
     col = lax.broadcasted_iota(jnp.int32, (BLK, BLK), 1)
     piece = (col // rows) ^ lead
     half = pieces // 2
     key_row = 2 * rows * (piece % half) + rows * (piece // half) + col % rows
-    causal = (key_row ^ rank_ref[1]) <= row
+    causal = (key_row ^ turn) <= row
     causal = jnp.concatenate([causal, causal], axis=0)
     for b in range(blocks):
         for j in range(slots):
@@ -126,7 +129,7 @@
             key_all[b, j * BLK:(j + 1) * BLK, :] = pair_ref[:, i, 0].reshape(BLK, width)
             value_all[b, j * BLK:(j + 1) * BLK, :] = pair_ref[:, i, 1].reshape(BLK, width)
     for b in range(blocks):
-        block = rank_ref[0] * blocks + b
+        block = rank * blocks + b
         position = span_ref[2 * me_ref[0] + block // per_span] * per_span + block % per_span
         here = slice(b * BLK, (b + 1) * BLK)
         for k, query_ref in enumerate(query_refs):
@@ -138,11 +141,11 @@
             for j in range(1, slots):
                 parts.append(jnp.where(position >= j, s[:, j * BLK:(j + 1) * BLK], MASKED))
             peak = functools.reduce(jnp.maximum, parts)
-            peak = jnp.max(peak, axis=1, keepdims=True) * factor
+            peak = jnp.max(peak, axis=1, keepdims=True)
             total = jnp.zeros((2 * BLK, BLK), jnp.float32)
             mixed = jnp.zeros((2 * BLK, width), jnp.float32)
             for j in range(slots):
-                raised = jnp.exp2(parts[j] * factor - peak)
+                raised = jnp.exp2((parts[j] - peak) * factor)
                 total += raised
                 mixed += jnp.dot(
                     raised.astype(jnp.bfloat16),
@@ -175,10 +178,7 @@
     spread_lead = block_count // 2 + block_count // 8
     ctx_lead = ctx_count - 2
     group_lead = 2
-    rank = lax.rem(lax.axis_index("head").astype(i32), group) ^ group_lead
-    line = lax.div(lax.axis_index("head").astype(i32), group)
-    turn = (lax.rem(line, 2) ^ lax.rem(rank, 2)) * (BLK // 2)
-    ranks = jnp.stack([rank, turn])
+    head = lax.axis_index("head").astype(i32)
     piece = (2, piece_rows, width)
     listed = key_blocks.T
 
@@ -208,18 +208,18 @@
         cost_estimate=pl.CostEstimate(flops=2 * 10**10, bytes_accessed=2**14, transcendentals=0),
     )(me[None], span_order, listed)
 
-    core = lax.rem(rank, 2)
+    core = lax.rem(head, 2)
     query_parts = queries.reshape(chips, 2, rows_device // group, width)
     crossing = lax.dynamic_index_in_dim(query_parts, 1 - core, 1, keepdims=False)
     sibling = lax.ppermute(crossing, "head", [(i, i ^ 1) for i in range(head_count)])
     part = jax.ShapeDtypeStruct((2, rows_device // group, width), bf16)
     bundles = pl.pallas_call(
-        bundle,
+        functools.partial(bundle, group, group_lead),
         out_shape=(part,) * chips,
         in_specs=[SMEM, VMEM, VMEM],
         out_specs=(VMEM,) * chips,
         compiler_params=small(8),
-    )(ranks, query_parts.reshape(group, rows_device // group, width), sibling)
+    )(head[None], query_parts.reshape(group, rows_device // group, width), sibling)
 
     own, table, bundles = lax.optimization_barrier((own, table, bundles))
 
@@ -253,13 +253,13 @@
     pairs = pairs.reshape((group, per_rank * slot_count) + piece)
 
     done = pl.pallas_call(
-        functools.partial(attend, per_span, group_lead),
+        functools.partial(attend, per_span, group, group_lead),
         out_shape=jax.ShapeDtypeStruct((group, per_rank * BLK, width), bf16),
         in_specs=[SMEM, SMEM, SMEM] + [VMEM] * (chips + 1),
         out_specs=VMEM,
         scratch_shapes=[pltpu.VMEM((per_rank, slot_count * BLK, width), bf16)] * 2,
         compiler_params=small(24),
-    )(me[None], ranks, span_order, *query_here, pairs)
+    )(me[None], head[None], span_order, *query_here, pairs)
 
     out = lax.all_to_all(done, "head", 0, 0, tiled=True, axis_index_groups=kv_groups)
     return out.reshape(rows_device, 1, width)

time: 94.6 us -> 93.9 us (level)
  no operation moved by 1% of the time
where the time goes in v11:
time: 93.9 us; the launch traced here: 93.3 us
  starting transfers between devices  42.6 us (45%)
  blocking collectives  34.5 us (37%)
  waiting for transfers between devices  7.37 us (8%)
  Pallas kernels  7.22 us (8%)
  local copies, waits for them, and re-layouts  1.47 us (2%)
    all_to_all x1, blocking collectives, body(): lax.all_to_all(pairs, 'head', 0, 0, tiled=True, axis_index_groups=kv_groups)  17.5 us
    all_to_all x1, blocking collectives, body(): lax.all_to_all(done, 'head', 0, 0, tiled=True, axis_index_groups=kv_groups)  17 us
    ppermute x1, starting transfers between devices, body(): lax.ppermute(crossing, 'head', [(i, i ^ 1) for i in range(head_count)])  13.4 us
    all_to_all x1, starting transfers between devices, body(): lax.all_to_all(kv, 'head', 0, 0, tiled=True, axis_index_groups=spread_gro...  11.4 us
    all_to_all x1, starting transfers between devices, body(): lax.all_to_all(asked, 'ctx', 0, 0, tiled=True, axis_index_groups=ctx_groups)  8.92 us
    ppermute x3, starting transfers between devices, body(): lax.ppermute(bundles[k], 'head', [(i, i ^ 2 * k) for i in range(head_coun...  8.9 us
    ppermute x3, waiting for transfers between devices, body(): lax.ppermute(bundles[k], 'head', [(i, i ^ 2 * k) for i in range(head_coun...  7.36 us
    pallas_call x1, Pallas kernels, body(): pl.pallas_call(functools.partial(attend, per_span, group, group_lead), ou...  2.23 us
  transfers between devices with their start and end apart: 6, of which 2 were waited for; matrix products, arithmetic and copies ran while one was open for 0% of the time, Pallas kernels for 1%

profile of v11, /device:TPU:1, one launch (start us, length us, event | category | flops | bytes accessed | tf_op | source)
XLA Modules:
  0.0 93.3 jit_solution(5324356893487539569)
XLA Ops:
  0.0 0.0 copy-start
  0.0 1.6 %shard_map.55 = bf16[16,2,16,128]{3,2,1,0:T(8,128)(2,1)} custom-call(bf16[32,8,128]{2,1,0:T(8,128)(2,1)} %key_ref.1, bf16[32,8,128]{2,1,0:T(8,128)(2,1)} %value_ref.1), custom_call_target="tpu_custom_call" | custom-call | tf_op jit(solution)/shard_map/pallas_call | solution.py:192
  1.6 11.4 %all-to-all-start = ((bf16[16,2,16,128]{3,2,1,0:T(8,128)(2,1)}), bf16[16,2,16,128]{3,2,1,0:T(8,128)(2,1)S(1)}, u32[]{:S(2)}, u32[]{:S(2)}) async-start(bf16[16,2,16,128]{3,2,1,0:T(8,128)(2,1)} %shard_map.55), calls=%async_computation | async-start | bytes 262144 | tf_op jit(solution)/shard_map/all_to_all | solution.py:200
  13.1 0.0 copy-done
  13.1 0.0 copy-start.2
  13.1 13.4 %collective-permute-start = (bf16[4,256,128]{2,1,0:T(8,128)(2,1)S(1)}, bf16[4,256,128]{2,1,0:T(8,128)(2,1)S(1)}, u32[]{:S(2)}, u32[]{:S(2)}) collective-permute-start(bf16[4,256,128]{2,1,0:T(8,128)(2,1)S(1)} %dynamic-slice_bitcast_fusion), channel_id=1, source_target_pairs={{0,1},{1,0},{2,3},{3,2},{4,5},{5,4},{6,7},{7,6},{8,9},{9,8},{10,11... | collective-permute-start | bytes 786440 | tf_op jit(solution)/shard_map/ppermute | solution.py:214
  26.5 0.0 copy-start.1
  26.5 0.0 copy-done.2
  26.5 0.6 copy-done.1
  27.2 0.8 shard_map.56.table_ref
  28.0 0.0 collective-permute-done.sibling_ref
  28.0 0.1 shard_map.57
  28.0 0.0 all-to-all-done.own_ref
  28.0 1.5 %shard_map.58 = bf16[32,2,16,128]{3,2,1,0:T(8,128)(2,1)} custom-call(s32[32]{0:T(128)S(1)} %copy-done.1, s32[6,256]{1,0:T(8,128)S(1)} %shard_map.56.table_ref, bf16[16,2,16,128]{3,2,1,0:T(8,128)(2,1)S(1)} %all-to-all-done.own_ref), custom_call_target="tpu_custom_call" | custom-call | tf_op jit(solution)/shard_map/pallas_call | solution.py:226
  29.5 8.9 %all-to-all-start.1 = ((bf16[32,2,16,128]{3,2,1,0:T(8,128)(2,1)}), bf16[32,2,16,128]{3,2,1,0:T(8,128)(2,1)S(1)}, u32[]{:S(2)}, u32[]{:S(2)}) async-start(bf16[32,2,16,128]{3,2,1,0:T(8,128)(2,1)} %shard_map.58), calls=%async_computation.1 | async-start | bytes 524288 | tf_op jit(solution)/shard_map/all_to_all | solution.py:234
  38.5 3.3 %collective-permute-start.1 = (bf16[2,256,128]{2,1,0:T(8,128)(2,1)S(1)}, bf16[2,256,128]{2,1,0:T(8,128)(2,1)S(1)}, u32[]{:S(2)}, u32[]{:S(2)}) collective-permute-start(bf16[2,256,128]{2,1,0:T(8,128)(2,1)S(1)} %get-tuple-element.40), channel_id=1, source_target_pairs={{0,4},{1,5},{2,6},{3,7},{4,0},{5,1},{6,2},{7,3},{8,12},{9,13},{10,... | collective-permute-start | bytes 393224 | tf_op jit(solution)/shard_map/ppermute | solution.py:238
  41.8 3.7 %collective-permute-start.2 = (bf16[2,256,128]{2,1,0:T(8,128)(2,1)S(1)}, bf16[2,256,128]{2,1,0:T(8,128)(2,1)S(1)}, u32[]{:S(2)}, u32[]{:S(2)}) collective-permute-start(bf16[2,256,128]{2,1,0:T(8,128)(2,1)S(1)} %get-tuple-element.41), channel_id=1, source_target_pairs={{0,6},{1,7},{2,4},{3,5},{4,2},{5,3},{6,0},{7,1},{8,14},{9,15},{10,... | collective-permute-start | bytes 393224 | tf_op jit(solution)/shard_map/ppermute | solution.py:238
  45.5 1.9 %collective-permute-start.3 = (bf16[2,256,128]{2,1,0:T(8,128)(2,1)S(1)}, bf16[2,256,128]{2,1,0:T(8,128)(2,1)S(1)}, u32[]{:S(2)}, u32[]{:S(2)}) collective-permute-start(bf16[2,256,128]{2,1,0:T(8,128)(2,1)S(1)} %get-tuple-element.42), channel_id=1, source_target_pairs={{0,2},{1,3},{2,0},{3,1},{4,6},{5,7},{6,4},{7,5},{8,10},{9,11},{10,... | collective-permute-start | bytes 393224 | tf_op jit(solution)/shard_map/ppermute | solution.py:238
  47.4 2.6 %collective-permute-done.1.refs_2_ = bf16[2,256,128]{2,1,0:T(8,128)(2,1)S(1)} collective-permute-done((bf16[2,256,128]{2,1,0:T(8,128)(2,1)S(1)}, bf16[2,256,128]{2,1,0:T(8,128)(2,1)S(1)}, u32[]{:S(2)}, u32[]{:S(2)}) %collective-permute-start.1) | collective-permute-done | bytes 131104 | tf_op jit(solution)/shard_map/ppermute | solution.py:238
  50.0 0.0 collective-permute-done.2.refs_3_
  50.0 4.8 %collective-permute-done.3.refs_1_ = bf16[2,256,128]{2,1,0:T(8,128)(2,1)S(1)} collective-permute-done((bf16[2,256,128]{2,1,0:T(8,128)(2,1)S(1)}, bf16[2,256,128]{2,1,0:T(8,128)(2,1)S(1)}, u32[]{:S(2)}, u32[]{:S(2)}) %collective-permute-start.3) | collective-permute-done | bytes 131104 | tf_op jit(solution)/shard_map/ppermute | solution.py:238
  54.8 0.0 all-to-all-done.1.foreign_ref
  54.8 1.0 %shard_map.59 = bf16[64,2,16,128]{3,2,1,0:T(8,128)(2,1)S(1)} custom-call(s32[1]{0:T(128)} %bitcast.me_ref, s32[32]{0:T(128)S(1)} %copy-done.1, s32[6,256]{1,0:T(8,128)S(1)} %shard_map.56.table_ref, bf16[16,2,16,128]{3,2,1,0:T(8,128)(2,1)S(1)} %all-to-all-done.own_ref, bf16[32,2,16,128]{3,2,1,0:T(8,128)(2,1)S(1)} %all-to-all-done.1.foreign_ref), custom_call_target="tpu_custom_call" | custom-call | tf_op jit(solution)/shard_map/pallas_call | solution.py:245
  55.8 17.5 %all_to_all.20 = bf16[64,2,16,128]{3,2,1,0:T(8,128)(2,1)S(1)} all-to-all(bf16[64,2,16,128]{3,2,1,0:T(8,128)(2,1)S(1)} %shard_map.59), channel_id=1, replica_groups={{2,3,0,1,6,7,4,5},{10,11,8,9,14,15,12,13},{18,19,16,17,22,23,20,21},{26..., dimensions={0} | all-to-all | bytes 1048576 | tf_op jit(solution)/shard_map/all_to_all | solution.py:252
  73.3 2.2 %shard_map.60 = bf16[8,256,128]{2,1,0:T(8,128)(2,1)S(1)} custom-call(s32[1]{0:T(128)} %bitcast.me_ref, s32[1]{0:T(128)} %bitcast.1.head_ref, s32[32]{0:T(128)S(1)} %copy-done.1, bf16[2,256,128]{2,1,0:T(8,128)(2,1)S(1)} %get-tuple-element.39.refs_0_, bf16[2,256,128]{2,1,0:T(8,128)(2,1)S(1)} %collective-permute-done.3.refs_1_, ...), custom_call_target="tpu_custom_call" | custom-call | tf_op jit(solution)/shard_map/pallas_call | solution.py:255
  75.5 17.0 %all_to_all.21 = bf16[8,256,128]{2,1,0:T(8,128)(2,1)S(1)} all-to-all(bf16[8,256,128]{2,1,0:T(8,128)(2,1)S(1)} %shard_map.60), channel_id=1, replica_groups={{2,3,0,1,6,7,4,5},{10,11,8,9,14,15,12,13},{18,19,16,17,22,23,20,21},{26..., dimensions={0} | all-to-all | bytes 1048576 | tf_op jit(solution)/shard_map/all_to_all | solution.py:264
  92.5 0.8 copy.9
  (1 shorter events, 0.0 us)
Async XLA Ops:
  0.0 13.1 %copy-start = (bf16[2048,1,128]{2,0,1:T(8,128)(2,1)S(1)}, bf16[2048,1,128]{2,0,1:T(8,128)(2,1)}, u32[]{:S(2)}) copy-start(bf16[2048,1,128]{2,0,1:T(8,128)(2,1)} %param.5) | copy-start | bytes 1572868
  1.6 26.4 %all-to-all-start = ((bf16[16,2,16,128]{3,2,1,0:T(8,128)(2,1)}), bf16[16,2,16,128]{3,2,1,0:T(8,128)(2,1)S(1)}, u32[]{:S(2)}, u32[]{:S(2)}) async-start(bf16[16,2,16,128]{3,2,1,0:T(8,128)(2,1)} %shard_map.55), calls=%async_computation | async-start | bytes 262144 | tf_op jit(solution)/shard_map/all_to_all | solution.py:200
  13.1 13.4 %copy-start.2 = (s32[256,4]{0,1:T(4,128)S(1)}, s32[256,4]{0,1:T(4,128)}, u32[]{:S(2)}) copy-start(s32[256,4]{0,1:T(4,128)} %param.8) | copy-start | bytes 12292
  13.1 14.9 %collective-permute-start = (bf16[4,256,128]{2,1,0:T(8,128)(2,1)S(1)}, bf16[4,256,128]{2,1,0:T(8,128)(2,1)S(1)}, u32[]{:S(2)}, u32[]{:S(2)}) collective-permute-start(bf16[4,256,128]{2,1,0:T(8,128)(2,1)S(1)} %dynamic-slice_bitcast_fusion), channel_id=1, source_target_pairs={{0,1},{1,0},{2,3},{3,2},{4,5},{5,4},{6,7},{7,6},{8,9},{9,8},{10,11... | collective-permute-start | bytes 786440 | tf_op jit(solution)/shard_map/ppermute | solution.py:214
  26.5 0.7 copy-start.1
  29.5 25.2 %all-to-all-start.1 = ((bf16[32,2,16,128]{3,2,1,0:T(8,128)(2,1)}), bf16[32,2,16,128]{3,2,1,0:T(8,128)(2,1)S(1)}, u32[]{:S(2)}, u32[]{:S(2)}) async-start(bf16[32,2,16,128]{3,2,1,0:T(8,128)(2,1)} %shard_map.58), calls=%async_computation.1 | async-start | bytes 524288 | tf_op jit(solution)/shard_map/all_to_all | solution.py:234
  38.5 11.5 %collective-permute-start.1 = (bf16[2,256,128]{2,1,0:T(8,128)(2,1)S(1)}, bf16[2,256,128]{2,1,0:T(8,128)(2,1)S(1)}, u32[]{:S(2)}, u32[]{:S(2)}) collective-permute-start(bf16[2,256,128]{2,1,0:T(8,128)(2,1)S(1)} %get-tuple-element.40), channel_id=1, source_target_pairs={{0,4},{1,5},{2,6},{3,7},{4,0},{5,1},{6,2},{7,3},{8,12},{9,13},{10,... | collective-permute-start | bytes 393224 | tf_op jit(solution)/shard_map/ppermute | solution.py:238
  41.8 8.2 %collective-permute-start.2 = (bf16[2,256,128]{2,1,0:T(8,128)(2,1)S(1)}, bf16[2,256,128]{2,1,0:T(8,128)(2,1)S(1)}, u32[]{:S(2)}, u32[]{:S(2)}) collective-permute-start(bf16[2,256,128]{2,1,0:T(8,128)(2,1)S(1)} %get-tuple-element.41), channel_id=1, source_target_pairs={{0,6},{1,7},{2,4},{3,5},{4,2},{5,3},{6,0},{7,1},{8,14},{9,15},{10,... | collective-permute-start | bytes 393224 | tf_op jit(solution)/shard_map/ppermute | solution.py:238
  45.5 9.3 %collective-permute-start.3 = (bf16[2,256,128]{2,1,0:T(8,128)(2,1)S(1)}, bf16[2,256,128]{2,1,0:T(8,128)(2,1)S(1)}, u32[]{:S(2)}, u32[]{:S(2)}) collective-permute-start(bf16[2,256,128]{2,1,0:T(8,128)(2,1)S(1)} %get-tuple-element.42), channel_id=1, source_target_pairs={{0,2},{1,3},{2,0},{3,1},{4,6},{5,7},{6,4},{7,5},{8,10},{9,11},{10,... | collective-permute-start | bytes 393224 | tf_op jit(solution)/shard_map/ppermute | solution.py:238

commit v12 on v11

--- a/solution.py
+++ b/solution.py
@@ -236,12 +236,12 @@
     *bundles, _ = lax.optimization_barrier((*bundles, asked))
     arrived = [
         lax.ppermute(bundles[k], "head", [(i, i ^ (2 * k)) for i in range(head_count)])
-        for k in (*range(2, chips), 1)
+        for k in range(chips - 1, 0, -1)
     ]
 
     kv_groups = [[g * group + (i ^ group_lead) for i in range(group)] for g in range(kv_heads)]
     foreign, arrived = lax.optimization_barrier((foreign, arrived))
-    query_here = [bundles[0], arrived[-1], *arrived[:-1]]
+    query_here = [bundles[0], *arrived[::-1]]
     pairs = pl.pallas_call(
         functools.partial(pick_pairs, per_span),
         out_shape=jax.ShapeDtypeStruct((block_count * slot_count,) + piece, bf16),

time: 93.9 us -> 93.9 us (level)
  transfers between devices with their start and end apart: 6 -> 6, of which waited for: 2 -> 1; matrix products, arithmetic and copies ran while one was open for 0% -> 0% of each run, Pallas kernels for 1% -> 1%
where the time goes in v12:
time: 93.9 us; the launch traced here: 93.4 us
  starting transfers between devices  43 us (46%)
  blocking collectives  35 us (37%)
  Pallas kernels  7.22 us (8%)
  waiting for transfers between devices  6.61 us (7%)
  local copies, waits for them, and re-layouts  1.47 us (2%)
    all_to_all x1, blocking collectives, body(): lax.all_to_all(pairs, 'head', 0, 0, tiled=True, axis_index_groups=kv_groups)  18 us
    all_to_all x1, blocking collectives, body(): lax.all_to_all(done, 'head', 0, 0, tiled=True, axis_index_groups=kv_groups)  17 us
    ppermute x1, starting transfers between devices, body(): lax.ppermute(crossing, 'head', [(i, i ^ 1) for i in range(head_count)])  13.4 us
    all_to_all x1, starting transfers between devices, body(): lax.all_to_all(kv, 'head', 0, 0, tiled=True, axis_index_groups=spread_gro...  11.4 us
    ppermute x3, starting transfers between devices, body(): lax.ppermute(bundles[k], 'head', [(i, i ^ 2 * k) for i in range(head_coun...  9.26 us
    all_to_all x1, starting transfers between devices, body(): lax.all_to_all(asked, 'ctx', 0, 0, tiled=True, axis_index_groups=ctx_groups)  8.92 us
    ppermute x3, waiting for transfers between devices, body(): lax.ppermute(bundles[k], 'head', [(i, i ^ 2 * k) for i in range(head_coun...  6.6 us
    pallas_call x1, Pallas kernels, body(): pl.pallas_call(functools.partial(attend, per_span, group, group_lead), ou...  2.23 us
  transfers between devices with their start and end apart: 6, of which 1 were waited for; matrix products, arithmetic and copies ran while one was open for 0% of the time, Pallas kernels for 1%

profile of v12, /device:TPU:1, one launch (start us, length us, event | category | flops | bytes accessed | tf_op | source)
XLA Modules:
  0.0 93.4 jit_solution(4701563689766634948)
XLA Ops:
  0.0 0.0 copy-start
  0.0 1.6 %shard_map.55 = bf16[16,2,16,128]{3,2,1,0:T(8,128)(2,1)} custom-call(bf16[32,8,128]{2,1,0:T(8,128)(2,1)} %key_ref.1, bf16[32,8,128]{2,1,0:T(8,128)(2,1)} %value_ref.1), custom_call_target="tpu_custom_call" | custom-call | tf_op jit(solution)/shard_map/pallas_call | solution.py:192
  1.6 11.4 %all-to-all-start = ((bf16[16,2,16,128]{3,2,1,0:T(8,128)(2,1)}), bf16[16,2,16,128]{3,2,1,0:T(8,128)(2,1)S(1)}, u32[]{:S(2)}, u32[]{:S(2)}) async-start(bf16[16,2,16,128]{3,2,1,0:T(8,128)(2,1)} %shard_map.55), calls=%async_computation | async-start | bytes 262144 | tf_op jit(solution)/shard_map/all_to_all | solution.py:200
  13.1 0.0 copy-done
  13.1 0.0 copy-start.2
  13.1 13.4 %collective-permute-start = (bf16[4,256,128]{2,1,0:T(8,128)(2,1)S(1)}, bf16[4,256,128]{2,1,0:T(8,128)(2,1)S(1)}, u32[]{:S(2)}, u32[]{:S(2)}) collective-permute-start(bf16[4,256,128]{2,1,0:T(8,128)(2,1)S(1)} %dynamic-slice_bitcast_fusion), channel_id=1, source_target_pairs={{0,1},{1,0},{2,3},{3,2},{4,5},{5,4},{6,7},{7,6},{8,9},{9,8},{10,11... | collective-permute-start | bytes 786440 | tf_op jit(solution)/shard_map/ppermute | solution.py:214
  26.5 0.0 copy-start.1
  26.5 0.0 copy-done.2
  26.5 0.6 copy-done.1
  27.2 0.8 shard_map.56.table_ref
  28.0 0.0 collective-permute-done.sibling_ref
  28.0 0.1 shard_map.57
  28.0 0.0 all-to-all-done.own_ref
  28.0 1.5 %shard_map.58 = bf16[32,2,16,128]{3,2,1,0:T(8,128)(2,1)} custom-call(s32[32]{0:T(128)S(1)} %copy-done.1, s32[6,256]{1,0:T(8,128)S(1)} %shard_map.56.table_ref, bf16[16,2,16,128]{3,2,1,0:T(8,128)(2,1)S(1)} %all-to-all-done.own_ref), custom_call_target="tpu_custom_call" | custom-call | tf_op jit(solution)/shard_map/pallas_call | solution.py:226
  29.5 8.9 %all-to-all-start.1 = ((bf16[32,2,16,128]{3,2,1,0:T(8,128)(2,1)}), bf16[32,2,16,128]{3,2,1,0:T(8,128)(2,1)S(1)}, u32[]{:S(2)}, u32[]{:S(2)}) async-start(bf16[32,2,16,128]{3,2,1,0:T(8,128)(2,1)} %shard_map.58), calls=%async_computation.1 | async-start | bytes 524288 | tf_op jit(solution)/shard_map/all_to_all | solution.py:234
  38.5 3.2 %collective-permute-start.1 = (bf16[2,256,128]{2,1,0:T(8,128)(2,1)S(1)}, bf16[2,256,128]{2,1,0:T(8,128)(2,1)S(1)}, u32[]{:S(2)}, u32[]{:S(2)}) collective-permute-start(bf16[2,256,128]{2,1,0:T(8,128)(2,1)S(1)} %get-tuple-element.40), channel_id=1, source_target_pairs={{0,6},{1,7},{2,4},{3,5},{4,2},{5,3},{6,0},{7,1},{8,14},{9,15},{10,... | collective-permute-start | bytes 393224 | tf_op jit(solution)/shard_map/ppermute | solution.py:238
  41.7 2.8 %collective-permute-start.2 = (bf16[2,256,128]{2,1,0:T(8,128)(2,1)S(1)}, bf16[2,256,128]{2,1,0:T(8,128)(2,1)S(1)}, u32[]{:S(2)}, u32[]{:S(2)}) collective-permute-start(bf16[2,256,128]{2,1,0:T(8,128)(2,1)S(1)} %get-tuple-element.41), channel_id=1, source_target_pairs={{0,4},{1,5},{2,6},{3,7},{4,0},{5,1},{6,2},{7,3},{8,12},{9,13},{10,... | collective-permute-start | bytes 393224 | tf_op jit(solution)/shard_map/ppermute | solution.py:238
  44.6 3.2 %collective-permute-start.3 = (bf16[2,256,128]{2,1,0:T(8,128)(2,1)S(1)}, bf16[2,256,128]{2,1,0:T(8,128)(2,1)S(1)}, u32[]{:S(2)}, u32[]{:S(2)}) collective-permute-start(bf16[2,256,128]{2,1,0:T(8,128)(2,1)S(1)} %get-tuple-element.42), channel_id=1, source_target_pairs={{0,2},{1,3},{2,0},{3,1},{4,6},{5,7},{6,4},{7,5},{8,10},{9,11},{10,... | collective-permute-start | bytes 393224 | tf_op jit(solution)/shard_map/ppermute | solution.py:238
  47.7 0.0 collective-permute-done.1.refs_3_
  47.8 6.6 %collective-permute-done.2.refs_2_ = bf16[2,256,128]{2,1,0:T(8,128)(2,1)S(1)} collective-permute-done((bf16[2,256,128]{2,1,0:T(8,128)(2,1)S(1)}, bf16[2,256,128]{2,1,0:T(8,128)(2,1)S(1)}, u32[]{:S(2)}, u32[]{:S(2)}) %collective-permute-start.2) | collective-permute-done | bytes 131104 | tf_op jit(solution)/shard_map/ppermute | solution.py:238
  54.4 0.0 collective-permute-done.3.refs_1_
  54.4 0.0 all-to-all-done.1.foreign_ref
  54.4 1.0 %shard_map.59 = bf16[64,2,16,128]{3,2,1,0:T(8,128)(2,1)S(1)} custom-call(s32[1]{0:T(128)} %bitcast.me_ref, s32[32]{0:T(128)S(1)} %copy-done.1, s32[6,256]{1,0:T(8,128)S(1)} %shard_map.56.table_ref, bf16[16,2,16,128]{3,2,1,0:T(8,128)(2,1)S(1)} %all-to-all-done.own_ref, bf16[32,2,16,128]{3,2,1,0:T(8,128)(2,1)S(1)} %all-to-all-done.1.foreign_ref), custom_call_target="tpu_custom_call" | custom-call | tf_op jit(solution)/shard_map/pallas_call | solution.py:245
  55.4 18.0 %all_to_all.20 = bf16[64,2,16,128]{3,2,1,0:T(8,128)(2,1)S(1)} all-to-all(bf16[64,2,16,128]{3,2,1,0:T(8,128)(2,1)S(1)} %shard_map.59), channel_id=1, replica_groups={{2,3,0,1,6,7,4,5},{10,11,8,9,14,15,12,13},{18,19,16,17,22,23,20,21},{26..., dimensions={0} | all-to-all | bytes 1048576 | tf_op jit(solution)/shard_map/all_to_all | solution.py:252
  73.3 2.2 %shard_map.60 = bf16[8,256,128]{2,1,0:T(8,128)(2,1)S(1)} custom-call(s32[1]{0:T(128)} %bitcast.me_ref, s32[1]{0:T(128)} %bitcast.1.head_ref, s32[32]{0:T(128)S(1)} %copy-done.1, bf16[2,256,128]{2,1,0:T(8,128)(2,1)S(1)} %get-tuple-element.39.refs_0_, bf16[2,256,128]{2,1,0:T(8,128)(2,1)S(1)} %collective-permute-done.3.refs_1_, ...), custom_call_target="tpu_custom_call" | custom-call | tf_op jit(solution)/shard_map/pallas_call | solution.py:255
  75.6 17.0 %all_to_all.21 = bf16[8,256,128]{2,1,0:T(8,128)(2,1)S(1)} all-to-all(bf16[8,256,128]{2,1,0:T(8,128)(2,1)S(1)} %shard_map.60), channel_id=1, replica_groups={{2,3,0,1,6,7,4,5},{10,11,8,9,14,15,12,13},{18,19,16,17,22,23,20,21},{26..., dimensions={0} | all-to-all | bytes 1048576 | tf_op jit(solution)/shard_map/all_to_all | solution.py:264
  92.6 0.8 copy.9
  (1 shorter events, 0.0 us)
Async XLA Ops:
  0.0 13.1 %copy-start = (bf16[2048,1,128]{2,0,1:T(8,128)(2,1)S(1)}, bf16[2048,1,128]{2,0,1:T(8,128)(2,1)}, u32[]{:S(2)}) copy-start(bf16[2048,1,128]{2,0,1:T(8,128)(2,1)} %param.5) | copy-start | bytes 1572868
  1.6 26.4 %all-to-all-start = ((bf16[16,2,16,128]{3,2,1,0:T(8,128)(2,1)}), bf16[16,2,16,128]{3,2,1,0:T(8,128)(2,1)S(1)}, u32[]{:S(2)}, u32[]{:S(2)}) async-start(bf16[16,2,16,128]{3,2,1,0:T(8,128)(2,1)} %shard_map.55), calls=%async_computation | async-start | bytes 262144 | tf_op jit(solution)/shard_map/all_to_all | solution.py:200
  13.1 13.4 %copy-start.2 = (s32[256,4]{0,1:T(4,128)S(1)}, s32[256,4]{0,1:T(4,128)}, u32[]{:S(2)}) copy-start(s32[256,4]{0,1:T(4,128)} %param.8) | copy-start | bytes 12292
  13.1 14.9 %collective-permute-start = (bf16[4,256,128]{2,1,0:T(8,128)(2,1)S(1)}, bf16[4,256,128]{2,1,0:T(8,128)(2,1)S(1)}, u32[]{:S(2)}, u32[]{:S(2)}) collective-permute-start(bf16[4,256,128]{2,1,0:T(8,128)(2,1)S(1)} %dynamic-slice_bitcast_fusion), channel_id=1, source_target_pairs={{0,1},{1,0},{2,3},{3,2},{4,5},{5,4},{6,7},{7,6},{8,9},{9,8},{10,11... | collective-permute-start | bytes 786440 | tf_op jit(solution)/shard_map/ppermute | solution.py:214
  26.5 0.7 copy-start.1
  29.5 24.8 %all-to-all-start.1 = ((bf16[32,2,16,128]{3,2,1,0:T(8,128)(2,1)}), bf16[32,2,16,128]{3,2,1,0:T(8,128)(2,1)S(1)}, u32[]{:S(2)}, u32[]{:S(2)}) async-start(bf16[32,2,16,128]{3,2,1,0:T(8,128)(2,1)} %shard_map.58), calls=%async_computation.1 | async-start | bytes 524288 | tf_op jit(solution)/shard_map/all_to_all | solution.py:234
  38.5 9.3 %collective-permute-start.1 = (bf16[2,256,128]{2,1,0:T(8,128)(2,1)S(1)}, bf16[2,256,128]{2,1,0:T(8,128)(2,1)S(1)}, u32[]{:S(2)}, u32[]{:S(2)}) collective-permute-start(bf16[2,256,128]{2,1,0:T(8,128)(2,1)S(1)} %get-tuple-element.40), channel_id=1, source_target_pairs={{0,6},{1,7},{2,4},{3,5},{4,2},{5,3},{6,0},{7,1},{8,14},{9,15},{10,... | collective-permute-start | bytes 393224 | tf_op jit(solution)/shard_map/ppermute | solution.py:238
  41.7 12.6 %collective-permute-start.2 = (bf16[2,256,128]{2,1,0:T(8,128)(2,1)S(1)}, bf16[2,256,128]{2,1,0:T(8,128)(2,1)S(1)}, u32[]{:S(2)}, u32[]{:S(2)}) collective-permute-start(bf16[2,256,128]{2,1,0:T(8,128)(2,1)S(1)} %get-tuple-element.41), channel_id=1, source_target_pairs={{0,4},{1,5},{2,6},{3,7},{4,0},{5,1},{6,2},{7,3},{8,12},{9,13},{10,... | collective-permute-start | bytes 393224 | tf_op jit(solution)/shard_map/ppermute | solution.py:238
  44.6 9.8 %collective-permute-start.3 = (bf16[2,256,128]{2,1,0:T(8,128)(2,1)S(1)}, bf16[2,256,128]{2,1,0:T(8,128)(2,1)S(1)}, u32[]{:S(2)}, u32[]{:S(2)}) collective-permute-start(bf16[2,256,128]{2,1,0:T(8,128)(2,1)S(1)} %get-tuple-element.42), channel_id=1, source_target_pairs={{0,2},{1,3},{2,0},{3,1},{4,6},{5,7},{6,4},{7,5},{8,10},{9,11},{10,... | collective-permute-start | bytes 393224 | tf_op jit(solution)/shard_map/ppermute | solution.py:238

commit v13 on v12

--- a/solution.py
+++ b/solution.py
@@ -176,7 +176,7 @@
     bf16 = jnp.bfloat16
     me = lax.axis_index("ctx").astype(i32)
     spread_lead = block_count // 2 + block_count // 8
-    ctx_lead = ctx_count - 2
+    ctx_lead = ctx_count - 3
     group_lead = 2
     head = lax.axis_index("head").astype(i32)
     piece = (2, piece_rows, width)

time: 93.9 us -> 95.5 us (1.017)
  blocking collectives: 35 us -> 36.7 us
    all_to_all x1, blocking collectives: 18 us -> 19.7 us  [body(): lax.all_to_all(pairs, 'head', 0, 0, tiled=True, axis_index_groups=kv_groups)]
where the time goes in v13:
time: 95.5 us; the launch traced here: 95 us
  starting transfers between devices  43 us (45%)
  blocking collectives  36.7 us (38%)
  Pallas kernels  7.23 us (8%)
  waiting for transfers between devices  6.52 us (7%)
  local copies, waits for them, and re-layouts  1.47 us (2%)
    all_to_all x1, blocking collectives, body(): lax.all_to_all(pairs, 'head', 0, 0, tiled=True, axis_index_groups=kv_groups)  19.7 us
    all_to_all x1, blocking collectives, body(): lax.all_to_all(done, 'head', 0, 0, tiled=True, axis_index_groups=kv_groups)  17 us
    ppermute x1, starting transfers between devices, body(): lax.ppermute(crossing, 'head', [(i, i ^ 1) for i in range(head_count)])  13.4 us
    all_to_all x1, starting transfers between devices, body(): lax.all_to_all(kv, 'head', 0, 0, tiled=True, axis_index_groups=spread_gro...  11.4 us
    ppermute x3, starting transfers between devices, body(): lax.ppermute(bundles[k], 'head', [(i, i ^ 2 * k) for i in range(head_coun...  9.26 us
    all_to_all x1, starting transfers between devices, body(): lax.all_to_all(asked, 'ctx', 0, 0, tiled=True, axis_index_groups=ctx_groups)  8.9 us
    ppermute x3, waiting for transfers between devices, body(): lax.ppermute(bundles[k], 'head', [(i, i ^ 2 * k) for i in range(head_coun...  6.51 us
    pallas_call x1, Pallas kernels, body(): pl.pallas_call(functools.partial(attend, per_span, group, group_lead), ou...  2.23 us
  transfers between devices with their start and end apart: 6, of which 1 were waited for; matrix products, arithmetic and copies ran while one was open for 0% of the time, Pallas kernels for 1%

profile of v13, /device:TPU:1, one launch (start us, length us, event | category | flops | bytes accessed | tf_op | source)
XLA Modules:
  0.0 95.0 jit_solution(10947745178930835221)
XLA Ops:
  0.0 0.0 copy-start
  0.0 1.6 %shard_map.55 = bf16[16,2,16,128]{3,2,1,0:T(8,128)(2,1)} custom-call(bf16[32,8,128]{2,1,0:T(8,128)(2,1)} %key_ref.1, bf16[32,8,128]{2,1,0:T(8,128)(2,1)} %value_ref.1), custom_call_target="tpu_custom_call" | custom-call | tf_op jit(solution)/shard_map/pallas_call | solution.py:192
  1.6 11.4 %all-to-all-start = ((bf16[16,2,16,128]{3,2,1,0:T(8,128)(2,1)}), bf16[16,2,16,128]{3,2,1,0:T(8,128)(2,1)S(1)}, u32[]{:S(2)}, u32[]{:S(2)}) async-start(bf16[16,2,16,128]{3,2,1,0:T(8,128)(2,1)} %shard_map.55), calls=%async_computation | async-start | bytes 262144 | tf_op jit(solution)/shard_map/all_to_all | solution.py:200
  13.1 0.0 copy-done
  13.1 0.0 copy-start.2
  13.1 13.4 %collective-permute-start = (bf16[4,256,128]{2,1,0:T(8,128)(2,1)S(1)}, bf16[4,256,128]{2,1,0:T(8,128)(2,1)S(1)}, u32[]{:S(2)}, u32[]{:S(2)}) collective-permute-start(bf16[4,256,128]{2,1,0:T(8,128)(2,1)S(1)} %dynamic-slice_bitcast_fusion), channel_id=1, source_target_pairs={{0,1},{1,0},{2,3},{3,2},{4,5},{5,4},{6,7},{7,6},{8,9},{9,8},{10,11... | collective-permute-start | bytes 786440 | tf_op jit(solution)/shard_map/ppermute | solution.py:214
  26.5 0.0 copy-start.1
  26.5 0.0 copy-done.2
  26.5 0.6 copy-done.1
  27.2 0.8 shard_map.56.table_ref
  28.0 0.0 collective-permute-done.sibling_ref
  28.0 0.1 shard_map.57
  28.0 0.0 all-to-all-done.own_ref
  28.0 1.5 %shard_map.58 = bf16[32,2,16,128]{3,2,1,0:T(8,128)(2,1)} custom-call(s32[32]{0:T(128)S(1)} %copy-done.1, s32[6,256]{1,0:T(8,128)S(1)} %shard_map.56.table_ref, bf16[16,2,16,128]{3,2,1,0:T(8,128)(2,1)S(1)} %all-to-all-done.own_ref), custom_call_target="tpu_custom_call" | custom-call | tf_op jit(solution)/shard_map/pallas_call | solution.py:226
  29.5 8.9 %all-to-all-start.1 = ((bf16[32,2,16,128]{3,2,1,0:T(8,128)(2,1)}), bf16[32,2,16,128]{3,2,1,0:T(8,128)(2,1)S(1)}, u32[]{:S(2)}, u32[]{:S(2)}) async-start(bf16[32,2,16,128]{3,2,1,0:T(8,128)(2,1)} %shard_map.58), calls=%async_computation.1 | async-start | bytes 524288 | tf_op jit(solution)/shard_map/all_to_all | solution.py:234
  38.4 3.2 %collective-permute-start.1 = (bf16[2,256,128]{2,1,0:T(8,128)(2,1)S(1)}, bf16[2,256,128]{2,1,0:T(8,128)(2,1)S(1)}, u32[]{:S(2)}, u32[]{:S(2)}) collective-permute-start(bf16[2,256,128]{2,1,0:T(8,128)(2,1)S(1)} %get-tuple-element.40), channel_id=1, source_target_pairs={{0,6},{1,7},{2,4},{3,5},{4,2},{5,3},{6,0},{7,1},{8,14},{9,15},{10,... | collective-permute-start | bytes 393224 | tf_op jit(solution)/shard_map/ppermute | solution.py:238
  41.7 2.8 %collective-permute-start.2 = (bf16[2,256,128]{2,1,0:T(8,128)(2,1)S(1)}, bf16[2,256,128]{2,1,0:T(8,128)(2,1)S(1)}, u32[]{:S(2)}, u32[]{:S(2)}) collective-permute-start(bf16[2,256,128]{2,1,0:T(8,128)(2,1)S(1)} %get-tuple-element.41), channel_id=1, source_target_pairs={{0,4},{1,5},{2,6},{3,7},{4,0},{5,1},{6,2},{7,3},{8,12},{9,13},{10,... | collective-permute-start | bytes 393224 | tf_op jit(solution)/shard_map/ppermute | solution.py:238
  44.5 3.2 %collective-permute-start.3 = (bf16[2,256,128]{2,1,0:T(8,128)(2,1)S(1)}, bf16[2,256,128]{2,1,0:T(8,128)(2,1)S(1)}, u32[]{:S(2)}, u32[]{:S(2)}) collective-permute-start(bf16[2,256,128]{2,1,0:T(8,128)(2,1)S(1)} %get-tuple-element.42), channel_id=1, source_target_pairs={{0,2},{1,3},{2,0},{3,1},{4,6},{5,7},{6,4},{7,5},{8,10},{9,11},{10,... | collective-permute-start | bytes 393224 | tf_op jit(solution)/shard_map/ppermute | solution.py:238
  47.7 0.0 collective-permute-done.1.refs_3_
  47.7 6.5 %collective-permute-done.2.refs_2_ = bf16[2,256,128]{2,1,0:T(8,128)(2,1)S(1)} collective-permute-done((bf16[2,256,128]{2,1,0:T(8,128)(2,1)S(1)}, bf16[2,256,128]{2,1,0:T(8,128)(2,1)S(1)}, u32[]{:S(2)}, u32[]{:S(2)}) %collective-permute-start.2) | collective-permute-done | bytes 131104 | tf_op jit(solution)/shard_map/ppermute | solution.py:238
  54.2 0.0 collective-permute-done.3.refs_1_
  54.2 0.0 all-to-all-done.1.foreign_ref
  54.3 1.0 %shard_map.59 = bf16[64,2,16,128]{3,2,1,0:T(8,128)(2,1)S(1)} custom-call(s32[1]{0:T(128)} %bitcast.me_ref, s32[32]{0:T(128)S(1)} %copy-done.1, s32[6,256]{1,0:T(8,128)S(1)} %shard_map.56.table_ref, bf16[16,2,16,128]{3,2,1,0:T(8,128)(2,1)S(1)} %all-to-all-done.own_ref, bf16[32,2,16,128]{3,2,1,0:T(8,128)(2,1)S(1)} %all-to-all-done.1.foreign_ref), custom_call_target="tpu_custom_call" | custom-call | tf_op jit(solution)/shard_map/pallas_call | solution.py:245
  55.3 19.7 %all_to_all.20 = bf16[64,2,16,128]{3,2,1,0:T(8,128)(2,1)S(1)} all-to-all(bf16[64,2,16,128]{3,2,1,0:T(8,128)(2,1)S(1)} %shard_map.59), channel_id=1, replica_groups={{2,3,0,1,6,7,4,5},{10,11,8,9,14,15,12,13},{18,19,16,17,22,23,20,21},{26..., dimensions={0} | all-to-all | bytes 1048576 | tf_op jit(solution)/shard_map/all_to_all | solution.py:252
  75.0 2.2 %shard_map.60 = bf16[8,256,128]{2,1,0:T(8,128)(2,1)S(1)} custom-call(s32[1]{0:T(128)} %bitcast.me_ref, s32[1]{0:T(128)} %bitcast.1.head_ref, s32[32]{0:T(128)S(1)} %copy-done.1, bf16[2,256,128]{2,1,0:T(8,128)(2,1)S(1)} %get-tuple-element.39.refs_0_, bf16[2,256,128]{2,1,0:T(8,128)(2,1)S(1)} %collective-permute-done.3.refs_1_, ...), custom_call_target="tpu_custom_call" | custom-call | tf_op jit(solution)/shard_map/pallas_call | solution.py:255
  77.2 17.0 %all_to_all.21 = bf16[8,256,128]{2,1,0:T(8,128)(2,1)S(1)} all-to-all(bf16[8,256,128]{2,1,0:T(8,128)(2,1)S(1)} %shard_map.60), channel_id=1, replica_groups={{2,3,0,1,6,7,4,5},{10,11,8,9,14,15,12,13},{18,19,16,17,22,23,20,21},{26..., dimensions={0} | all-to-all | bytes 1048576 | tf_op jit(solution)/shard_map/all_to_all | solution.py:264
  94.2 0.8 copy.9
  (1 shorter events, 0.0 us)
Async XLA Ops:
  0.0 13.1 %copy-start = (bf16[2048,1,128]{2,0,1:T(8,128)(2,1)S(1)}, bf16[2048,1,128]{2,0,1:T(8,128)(2,1)}, u32[]{:S(2)}) copy-start(bf16[2048,1,128]{2,0,1:T(8,128)(2,1)} %param.5) | copy-start | bytes 1572868
  1.6 26.4 %all-to-all-start = ((bf16[16,2,16,128]{3,2,1,0:T(8,128)(2,1)}), bf16[16,2,16,128]{3,2,1,0:T(8,128)(2,1)S(1)}, u32[]{:S(2)}, u32[]{:S(2)}) async-start(bf16[16,2,16,128]{3,2,1,0:T(8,128)(2,1)} %shard_map.55), calls=%async_computation | async-start | bytes 262144 | tf_op jit(solution)/shard_map/all_to_all | solution.py:200
  13.1 13.4 %copy-start.2 = (s32[256,4]{0,1:T(4,128)S(1)}, s32[256,4]{0,1:T(4,128)}, u32[]{:S(2)}) copy-start(s32[256,4]{0,1:T(4,128)} %param.8) | copy-start | bytes 12292
  13.1 14.9 %collective-permute-start = (bf16[4,256,128]{2,1,0:T(8,128)(2,1)S(1)}, bf16[4,256,128]{2,1,0:T(8,128)(2,1)S(1)}, u32[]{:S(2)}, u32[]{:S(2)}) collective-permute-start(bf16[4,256,128]{2,1,0:T(8,128)(2,1)S(1)} %dynamic-slice_bitcast_fusion), channel_id=1, source_target_pairs={{0,1},{1,0},{2,3},{3,2},{4,5},{5,4},{6,7},{7,6},{8,9},{9,8},{10,11... | collective-permute-start | bytes 786440 | tf_op jit(solution)/shard_map/ppermute | solution.py:214
  26.5 0.7 copy-start.1
  29.5 24.7 %all-to-all-start.1 = ((bf16[32,2,16,128]{3,2,1,0:T(8,128)(2,1)}), bf16[32,2,16,128]{3,2,1,0:T(8,128)(2,1)S(1)}, u32[]{:S(2)}, u32[]{:S(2)}) async-start(bf16[32,2,16,128]{3,2,1,0:T(8,128)(2,1)} %shard_map.58), calls=%async_computation.1 | async-start | bytes 524288 | tf_op jit(solution)/shard_map/all_to_all | solution.py:234
  38.4 9.3 %collective-permute-start.1 = (bf16[2,256,128]{2,1,0:T(8,128)(2,1)S(1)}, bf16[2,256,128]{2,1,0:T(8,128)(2,1)S(1)}, u32[]{:S(2)}, u32[]{:S(2)}) collective-permute-start(bf16[2,256,128]{2,1,0:T(8,128)(2,1)S(1)} %get-tuple-element.40), channel_id=1, source_target_pairs={{0,6},{1,7},{2,4},{3,5},{4,2},{5,3},{6,0},{7,1},{8,14},{9,15},{10,... | collective-permute-start | bytes 393224 | tf_op jit(solution)/shard_map/ppermute | solution.py:238
  41.7 12.6 %collective-permute-start.2 = (bf16[2,256,128]{2,1,0:T(8,128)(2,1)S(1)}, bf16[2,256,128]{2,1,0:T(8,128)(2,1)S(1)}, u32[]{:S(2)}, u32[]{:S(2)}) collective-permute-start(bf16[2,256,128]{2,1,0:T(8,128)(2,1)S(1)} %get-tuple-element.41), channel_id=1, source_target_pairs={{0,4},{1,5},{2,6},{3,7},{4,0},{5,1},{6,2},{7,3},{8,12},{9,13},{10,... | collective-permute-start | bytes 393224 | tf_op jit(solution)/shard_map/ppermute | solution.py:238
  44.5 9.7 %collective-permute-start.3 = (bf16[2,256,128]{2,1,0:T(8,128)(2,1)S(1)}, bf16[2,256,128]{2,1,0:T(8,128)(2,1)S(1)}, u32[]{:S(2)}, u32[]{:S(2)}) collective-permute-start(bf16[2,256,128]{2,1,0:T(8,128)(2,1)S(1)} %get-tuple-element.42), channel_id=1, source_target_pairs={{0,2},{1,3},{2,0},{3,1},{4,6},{5,7},{6,4},{7,5},{8,10},{9,11},{10,... | collective-permute-start | bytes 393224 | tf_op jit(solution)/shard_map/ppermute | solution.py:238
